TPU v7x, 32 devices: a whole 2x2x4 slice. The times are simulated.
32 devices in a mesh: seq: 4 (over y, core), batch: 8 (over z, x).
Axes of the slice: x: 2, y: 2, z: 4, core: 2. Of those that a mesh axis runs over, the one named last changes fastest.
Arguments:
- tokens: bfloat16 [8, 1024, 2048], P('batch', 'seq'), may hold values from -6 to 6
- cotangent: bfloat16 [8, 1024, 2048], P('batch', 'seq'), may hold values from -6 to 6
- selection: int32 [8, 1024], P('batch', 'seq'), may hold values from 0 to 1, as said below
- segments: int32 [8, 1024], P('batch', 'seq'), may hold values from 0 to 510, as said below
- positions: int32 [8, 1024], P('batch', 'seq'), may hold values from 0 to 1534, as said below
- gain_attn: bfloat16 [2048], P(('seq', 'batch')), may hold values from 0.099609375 to 1.8984375
- w_query: bfloat16 [2048, 2048], P(('seq', 'batch')), may hold values from -0.125 to 0.125
- w_key: bfloat16 [2048, 256], P(('seq', 'batch')), may hold values from -0.125 to 0.125
- w_value: bfloat16 [2048, 256], P(('seq', 'batch')), may hold values from -0.125 to 0.125
- w_out: bfloat16 [2048, 2048], P(('seq', 'batch')), may hold values from -1 to 1
- gain_mlp: bfloat16 [2048], P(('seq', 'batch')), may hold values from 0.099609375 to 1.8984375
- w_gate: bfloat16 [2048, 5632], P(('seq', 'batch')), may hold values from -0.125 to 0.125
- w_up: bfloat16 [2048, 5632], P(('seq', 'batch')), may hold values from -0.125 to 0.125
- w_down: bfloat16 [5632, 2048], P(('seq', 'batch')), may hold values from -0.078125 to 0.078125
Outputs:
- mixed: bfloat16 [8, 1024, 2048], P('batch', 'seq')
- tokens_grad: bfloat16 [8, 1024, 2048], P('batch', 'seq')
- grad_query: float32 [2048, 2048], P(('seq', 'batch'))
- grad_key: float32 [2048, 256], P(('seq', 'batch'))
- grad_value: float32 [2048, 256], P(('seq', 'batch'))
- grad_out: float32 [2048, 2048], P(('seq', 'batch'))
- grad_gate: float32 [2048, 5632], P(('seq', 'batch'))
- grad_up: float32 [2048, 5632], P(('seq', 'batch'))
- grad_down: float32 [5632, 2048], P(('seq', 'batch'))
- grad_gain_attn: float32 [2048], P(('seq', 'batch'))
- grad_gain_mlp: float32 [2048], P(('seq', 'batch'))
Inputs may be any that keep to these rules, and one draw needn't show every extreme that they name: `selection`: 1 where the token's loss gradient is kept; each row keeps its own share of its tokens. `segments`: document number of each position, never falling along a row and starting at 0 in each row; a row holds at most 511 documents. `positions`: each token's place in its document; the first document of a row may continue an earlier one and start below 512.
All inputs are finite; a program needn't handle non-finite values.
Results may differ from a plain program's by a relative error of at most 0.015.
Values may be sent and summed in bfloat16 or wider, within the bound.
A program may use at most 448 MiB of HBM per device.

v0:
```python
import jax
import jax.numpy as jnp
from jax import lax
from jax.sharding import PartitionSpec as P

HEADS = 32
KV_HEADS = 4
HEAD_DIM = 64


EPSILON = 1e-05
MASKED_SCORE = -1e30
CONTRACT_ROWS = (((0,), (0,)), ((), ()))
CONTRACT_COLS = (((1,), (1,)), ((), ()))


def tables(pos_row):
    half_dim = HEAD_DIM // 2
    frequency = 10000.0 ** (-(jnp.arange(half_dim, dtype=jnp.float32) * 2.0 / HEAD_DIM))
    angles = pos_row.astype(jnp.float32)[:, None] * frequency[None, :]
    doubled = jnp.concatenate([angles, angles], axis=-1)
    return (jnp.cos(doubled)[:, None, :], jnp.sin(doubled)[:, None, :])


def rotate(vectors, cosine, sine):
    half_dim = vectors.shape[-1] // 2
    turned = jnp.concatenate([-vectors[..., half_dim:], vectors[..., :half_dim]], axis=-1)
    return vectors * cosine + turned * sine


def unrotate(grads_in, cosine, sine):
    half_dim = grads_in.shape[-1] // 2
    scaled = grads_in * sine
    turned = jnp.concatenate([scaled[..., half_dim:], -scaled[..., :half_dim]], axis=-1)
    return grads_in * cosine + turned


def product(left, right):
    return jnp.dot(left, right, preferred_element_type=jnp.float32)


def product_rows(left, right):
    return lax.dot_general(left, right, CONTRACT_ROWS, preferred_element_type=jnp.float32)


def product_cols(left, right):
    return lax.dot_general(left, right, CONTRACT_COLS, preferred_element_type=jnp.float32)


def rms_scale(inputs):
    return lax.rsqrt(jnp.mean(inputs * inputs, axis=-1, keepdims=True) + EPSILON)


def norm_back(grad_normed, inputs, inverse, gain):
    scaled = gain * grad_normed
    grad_gain = jnp.sum(grad_normed * inputs * inverse, axis=0)
    cubed = inverse * inverse * inverse
    grad_input = inverse * scaled - inputs * cubed * jnp.mean(
        scaled * inputs, axis=-1, keepdims=True
    )
    return (grad_input, grad_gain)


def per_device(
    tokens,
    cotangent,
    selection,
    segments,
    positions,
    gain_attn,
    w_query,
    w_key,
    w_value,
    w_out,
    gain_mlp,
    w_gate,
    w_up,
    w_down,
):
    seq_size = lax.axis_size("seq")
    seq_rank = lax.axis_index("seq")
    length = tokens.shape[1]
    total_len = length * seq_size
    group = HEADS // KV_HEADS
    kv_width = KV_HEADS * HEAD_DIM
    scale = HEAD_DIM ** (-0.5)
    kblock = min(512, total_len)
    block_count = total_len // kblock
    starts = jnp.arange(block_count, dtype=jnp.int32) * kblock
    attn_set = (
        lax.all_gather(w_query, ("seq", "batch"), axis=0, tiled=True),
        lax.all_gather(w_key, ("seq", "batch"), axis=0, tiled=True),
        lax.all_gather(w_value, ("seq", "batch"), axis=0, tiled=True),
        lax.all_gather(w_out, ("seq", "batch"), axis=0, tiled=True),
        lax.all_gather(gain_attn, ("seq", "batch"), axis=0, tiled=True),
        lax.all_gather(gain_mlp, ("seq", "batch"), axis=0, tiled=True),
    )
    wq_all, wk_all, wv_all, wo_all, ga_all, gm_all = attn_set
    row_input = tokens[0].astype(jnp.float32)
    inv_attn = rms_scale(row_input)
    gain_one = ga_all.astype(jnp.float32)
    normed1 = (row_input * inv_attn * gain_one).astype(jnp.bfloat16)
    queries = product(normed1, wq_all)
    key_proj = product(normed1, wk_all)
    values = product(normed1, wv_all).astype(jnp.bfloat16)
    cosine, sine = tables(positions[0])
    query_rows = rotate(queries.reshape(length, HEADS, HEAD_DIM), cosine, sine).astype(jnp.bfloat16)
    query_rows = query_rows.reshape(length, KV_HEADS, group, HEAD_DIM)
    key_rot = (
        rotate(key_proj.reshape(length, KV_HEADS, HEAD_DIM), cosine, sine)
        .astype(jnp.bfloat16)
        .reshape(length, kv_width)
    )
    seg_row = segments[0]
    seg_pair = jnp.stack([seg_row // 256, seg_row % 256]).astype(jnp.bfloat16)
    key_all, value_all, seg_all = (
        lax.all_gather(key_rot, "seq", axis=0, tiled=True),
        lax.all_gather(values, "seq", axis=0, tiled=True),
        lax.all_gather(seg_pair, "seq", axis=1, tiled=True),
    )
    key_heads = key_all.reshape(total_len, KV_HEADS, HEAD_DIM)
    value_heads = value_all.reshape(total_len, KV_HEADS, HEAD_DIM)
    key_seg = seg_all[0].astype(jnp.float32) * 256.0 + seg_all[1].astype(jnp.float32)
    query_seg = seg_row.astype(jnp.float32)
    query_pos = seq_rank * length + jnp.arange(length, dtype=jnp.int32)
    stat_shape = (KV_HEADS, group, length)

    def block_scores(key_start):
        key_part = lax.dynamic_slice_in_dim(key_heads, key_start, kblock, 0)
        value_part = lax.dynamic_slice_in_dim(value_heads, key_start, kblock, 0)
        seg_part = lax.dynamic_slice_in_dim(key_seg, key_start, kblock, 0)
        key_pos = key_start + jnp.arange(kblock, dtype=jnp.int32)
        scores = (
            jnp.einsum("qkgd,tkd->kgqt", query_rows, key_part, preferred_element_type=jnp.float32)
            * scale
        )
        allowed = (key_pos[None, :] <= query_pos[:, None]) & (
            seg_part[None, :] == query_seg[:, None]
        )
        return (scores, allowed, key_part, value_part)

    def first_pass(carried, key_start):
        row_max, row_sum = carried
        scores, allowed, key_part, value_part = block_scores(key_start)
        masked = jnp.where(allowed, scores, MASKED_SCORE)
        new_max = jnp.maximum(row_max, jnp.max(masked, axis=-1))
        kept_exp = jnp.where(allowed, jnp.exp(masked - new_max[..., None]), 0.0)
        row_sum = row_sum * jnp.exp(row_max - new_max) + jnp.sum(kept_exp, axis=-1)
        return ((new_max, row_sum), None)

    init_stats = (
        jnp.full(stat_shape, MASKED_SCORE, jnp.float32),
        jnp.zeros(stat_shape, jnp.float32),
    )
    (row_max, row_sum), unused = lax.scan(first_pass, init_stats, starts)
    log_sum = row_max + jnp.log(row_sum)

    def probabilities(key_start):
        scores, allowed, key_part, value_part = block_scores(key_start)
        attn_probs = jnp.where(allowed, jnp.exp(scores - log_sum[..., None]), 0.0)
        return (attn_probs, key_part, value_part)

    def second_pass(accum, key_start):
        attn_probs, key_part, value_part = probabilities(key_start)
        accum = accum + jnp.einsum(
            "kgqt,tkd->qkgd",
            attn_probs.astype(jnp.bfloat16),
            value_part,
            preferred_element_type=jnp.float32,
        )
        return (accum, None)

    head_shape = (length, KV_HEADS, group, HEAD_DIM)
    attn_acc, unused = lax.scan(second_pass, jnp.zeros(head_shape, jnp.float32), starts)
    mixed_heads = attn_acc.reshape(length, HEADS * HEAD_DIM).astype(jnp.bfloat16)
    residual = row_input + product(mixed_heads, wo_all)
    inv_mlp = rms_scale(residual)
    gain_two = gm_all.astype(jnp.float32)
    normed2 = (residual * inv_mlp * gain_two).astype(jnp.bfloat16)
    gate_use, up_use, down_use = (
        lax.all_gather(w_gate, ("seq", "batch"), axis=0, tiled=True),
        lax.all_gather(w_up, ("seq", "batch"), axis=0, tiled=True),
        lax.all_gather(w_down, ("seq", "batch"), axis=0, tiled=True),
    )
    gate_proj = product(normed2, gate_use)
    up_proj = product(normed2, up_use)
    sigma = jax.nn.sigmoid(gate_proj)
    activated = gate_proj * sigma
    hidden = (activated * up_proj).astype(jnp.bfloat16)
    branch_out = product(hidden, down_use)
    layer_out = residual + branch_out
    mixed = layer_out.astype(jnp.bfloat16)[None]
    grad_out_row = cotangent[0].astype(jnp.float32) * selection[0].astype(jnp.float32)[:, None]
    grad_low = grad_out_row.astype(jnp.bfloat16)
    gate_back, up_back, down_back = (
        lax.all_gather(w_gate, ("seq", "batch"), axis=0, tiled=True),
        lax.all_gather(w_up, ("seq", "batch"), axis=0, tiled=True),
        lax.all_gather(w_down, ("seq", "batch"), axis=0, tiled=True),
    )
    grad_hidden = product_cols(grad_low, down_back)
    grad_down = product_rows(hidden, grad_low)
    grad_gate_act = (grad_hidden * up_proj * sigma * (1.0 + gate_proj * (1.0 - sigma))).astype(
        jnp.bfloat16
    )
    grad_up_act = (grad_hidden * activated).astype(jnp.bfloat16)
    grad_gate = product_rows(normed2, grad_gate_act)
    grad_up = product_rows(normed2, grad_up_act)
    normed_terms = product_cols(grad_gate_act, gate_back) + product_cols(grad_up_act, up_back)
    grad_resid_norm, grad_gain2 = norm_back(normed_terms, residual, inv_mlp, gain_two)
    grad_resid = grad_out_row + grad_resid_norm
    mlp_parts = (
        lax.psum_scatter(grad_gate, ("seq", "batch"), scatter_dimension=0, tiled=True),
        lax.psum_scatter(grad_up, ("seq", "batch"), scatter_dimension=0, tiled=True),
        lax.psum_scatter(grad_down, ("seq", "batch"), scatter_dimension=0, tiled=True),
    )
    attn_back = (
        lax.all_gather(w_query, ("seq", "batch"), axis=0, tiled=True),
        lax.all_gather(w_key, ("seq", "batch"), axis=0, tiled=True),
        lax.all_gather(w_value, ("seq", "batch"), axis=0, tiled=True),
        lax.all_gather(w_out, ("seq", "batch"), axis=0, tiled=True),
        lax.all_gather(gain_attn, ("seq", "batch"), axis=0, tiled=True),
    )
    wq_back, wk_back, wv_back, wo_back, ga_back = attn_back
    grad_branch = grad_resid.astype(jnp.bfloat16)
    grad_wout = product_rows(mixed_heads, grad_branch)
    grad_heads = product_cols(grad_branch, wo_back).astype(jnp.bfloat16).reshape(head_shape)

    def delta_pass(accum, key_start):
        attn_probs, key_part, value_part = probabilities(key_start)
        grad_probs = jnp.einsum(
            "qkgd,tkd->kgqt", grad_heads, value_part, preferred_element_type=jnp.float32
        )
        return (accum + jnp.sum(attn_probs * grad_probs, axis=-1), None)

    row_delta, unused = lax.scan(delta_pass, jnp.zeros(stat_shape, jnp.float32), starts)

    def grad_pass(accum, key_start):
        attn_probs, key_part, value_part = probabilities(key_start)
        grad_probs = jnp.einsum(
            "qkgd,tkd->kgqt", grad_heads, value_part, preferred_element_type=jnp.float32
        )
        grad_scores = (attn_probs * (grad_probs - row_delta[..., None]) * scale).astype(
            jnp.bfloat16
        )
        accum = accum + jnp.einsum(
            "kgqt,tkd->qkgd", grad_scores, key_part, preferred_element_type=jnp.float32
        )
        key_block = jnp.einsum(
            "kgqt,qkgd->tkd", grad_scores, query_rows, preferred_element_type=jnp.float32
        )
        value_block = jnp.einsum(
            "kgqt,qkgd->tkd",
            attn_probs.astype(jnp.bfloat16),
            grad_heads,
            preferred_element_type=jnp.float32,
        )
        return (accum, (key_block, value_block))

    query_grad, (key_blocks, value_blocks) = lax.scan(
        grad_pass, jnp.zeros(head_shape, jnp.float32), starts
    )
    key_terms = key_blocks.reshape(total_len, kv_width)
    value_terms = value_blocks.reshape(total_len, kv_width)
    key_local, value_local = (
        lax.psum_scatter(
            key_terms.astype(jnp.bfloat16), "seq", scatter_dimension=0, tiled=True
        ).astype(jnp.float32),
        lax.psum_scatter(
            value_terms.astype(jnp.bfloat16), "seq", scatter_dimension=0, tiled=True
        ).astype(jnp.float32),
    )
    grad_query_act = (
        unrotate(query_grad.reshape(length, HEADS, HEAD_DIM), cosine, sine)
        .reshape(length, HEADS * HEAD_DIM)
        .astype(jnp.bfloat16)
    )
    grad_key_act = (
        unrotate(key_local.reshape(length, KV_HEADS, HEAD_DIM), cosine, sine)
        .reshape(length, kv_width)
        .astype(jnp.bfloat16)
    )
    grad_value_act = value_local.astype(jnp.bfloat16)
    grad_wq = product_rows(normed1, grad_query_act)
    grad_wk = product_rows(normed1, grad_key_act)
    grad_wv = product_rows(normed1, grad_value_act)
    grad_normed1 = (
        product_cols(grad_query_act, wq_back)
        + product_cols(grad_key_act, wk_back)
        + product_cols(grad_value_act, wv_back)
    )
    grad_input_norm, grad_gain1 = norm_back(
        grad_normed1, row_input, inv_attn, ga_back.astype(jnp.float32)
    )
    tokens_grad = (grad_resid + grad_input_norm).astype(jnp.bfloat16)[None]
    attn_parts = (
        lax.psum_scatter(grad_wq, ("seq", "batch"), scatter_dimension=0, tiled=True),
        lax.psum_scatter(grad_wk, ("seq", "batch"), scatter_dimension=0, tiled=True),
        lax.psum_scatter(grad_wv, ("seq", "batch"), scatter_dimension=0, tiled=True),
        lax.psum_scatter(grad_wout, ("seq", "batch"), scatter_dimension=0, tiled=True),
        lax.psum_scatter(grad_gain1, ("seq", "batch"), scatter_dimension=0, tiled=True),
        lax.psum_scatter(grad_gain2, ("seq", "batch"), scatter_dimension=0, tiled=True),
    )
    return (
        mixed,
        tokens_grad,
        attn_parts[0],
        attn_parts[1],
        attn_parts[2],
        attn_parts[3],
        mlp_parts[0],
        mlp_parts[1],
        mlp_parts[2],
        attn_parts[4],
        attn_parts[5],
    )


def solution(mesh):
    in_specs = (
        P("batch", "seq", None),
        P("batch", "seq", None),
        P("batch", "seq"),
        P("batch", "seq"),
        P("batch", "seq"),
        P(("seq", "batch")),
        P(("seq", "batch"), None),
        P(("seq", "batch"), None),
        P(("seq", "batch"), None),
        P(("seq", "batch"), None),
        P(("seq", "batch")),
        P(("seq", "batch"), None),
        P(("seq", "batch"), None),
        P(("seq", "batch"), None),
    )
    out_specs = (
        P("batch", "seq", None),
        P("batch", "seq", None),
        P(("seq", "batch"), None),
        P(("seq", "batch"), None),
        P(("seq", "batch"), None),
        P(("seq", "batch"), None),
        P(("seq", "batch"), None),
        P(("seq", "batch"), None),
        P(("seq", "batch"), None),
        P(("seq", "batch")),
        P(("seq", "batch")),
    )
    return jax.shard_map(
        per_device, mesh=mesh, in_specs=in_specs, out_specs=out_specs, check_vma=False
    )
```

profile of v0, /device:TPU:0, one launch (start us, length us, event | category | flops | bytes accessed | tf_op | source)
XLA Modules:
  0.0 4842.4 jit_solution(5300988548846983405)
XLA Ops:
  12.6 42.2 all-reduce.5
  54.9 5.4 all_gather.47
  61.4 6.2 all-gather.10.cloned.1.call-done
  69.9 53.5 %all-gather.8.cloned.1.call-done = bf16[2048,256]{1,0:T(8,128)(2,1)} async-done(((bf16[64,256]{1,0:T(8,128)(2,1)}), bf16[2048,256]{1,0:T(8,128)(2,1)}) %all-gather.8.cloned.1.call-update) | async-done | bytes 1048592 | tf_op jit(solution)/shard_map/all_gather | solution.py:93
  125.1 7.2 all_gather.46
  134.5 7.8 all_gather.49
  142.3 62.0 %all-gather.12.cloned.1.call-done = bf16[2048,2048]{1,0:T(8,128)(2,1)} async-done(((bf16[64,2048]{1,0:T(8,128)(2,1)}), bf16[2048,2048]{1,0:T(8,128)(2,1)}) %all-gather.12.cloned.1.call-update) | async-done | bytes 8388624 | tf_op jit(solution)/shard_map/all_gather | solution.py:91
  204.3 12.2 copy.54
  216.5 5.9 fusion.95
  223.3 38.7 while.50
  226.8 7.5 fusion.202
  234.3 8.1 select_reduce_fusion.2
  246.0 7.3 fusion.202
  253.3 8.7 select_reduce_fusion.2
  262.7 21.8 while.51
  266.1 6.9 bitcast_add_fusion.6
  276.5 7.7 bitcast_add_fusion.6
  284.4 2.7 convert_element_type.170
  287.2 6.2 multiply_reduce_fusion.2
  294.9 134.2 %all-gather.16.cloned.1.call-done = bf16[2048,5632]{1,0:T(8,128)(2,1)} async-done(((bf16[64,5632]{1,0:T(8,128)(2,1)}), bf16[2048,5632]{1,0:T(8,128)(2,1)}) %all-gather.16.cloned.1.call-update) | async-done | bytes 23068688 | tf_op jit(solution)/shard_map/all_gather | solution.py:181
  429.1 13.2 fusion.127
  442.3 132.4 %all-gather.18.cloned.1.call-done = bf16[2048,5632]{1,0:T(8,128)(2,1)} async-done(((bf16[64,5632]{1,0:T(8,128)(2,1)}), bf16[2048,5632]{1,0:T(8,128)(2,1)}) %all-gather.18.cloned.1.call-update) | async-done | bytes 23068688 | tf_op jit(solution)/shard_map/all_gather | solution.py:182
  574.7 13.3 fusion.128
  588.0 132.5 %all-gather.20.cloned.1.call-done = bf16[5632,2048]{1,0:T(8,128)(2,1)} async-done(((bf16[176,2048]{1,0:T(8,128)(2,1)}), bf16[5632,2048]{1,0:T(8,128)(2,1)}) %all-gather.20.cloned.1.call-update) | async-done | bytes 23068688 | tf_op jit(solution)/shard_map/all_gather | solution.py:183
  720.4 18.5 multiply_convert_fusion
  738.9 12.5 fusion.129
  751.5 14.9 multiply_reduce_fusion
  766.4 2.9 fusion.89
  770.7 6.7 convolution_convert_fusion
  778.9 24.1 while.52
  782.4 2.5 fusion.211
  784.9 6.0 fusion.212
  794.5 2.5 fusion.211
  797.0 6.0 fusion.212
  803.0 80.0 %while.53 = (s32[]{:T(128)}, f32[256,4,8,64]{0,3,2,1:T(8,128)}, bf16[2,512,4,64]{1,3,2,0:T(8,128)(2,1)}, bf16[2,512,4,64]{1,3,2,0:T(8,128)(2,1)}, s32[2]{0:T(128...) while((s32[]{:T(128)}, f32[256,4,8,64]{0,3,2,1:T(8,128)}, ...), condition=%wide.region_13.14_spmd.clone, body=%wide.region_12.13_spmd.clone.sunk | while | flops 2731934464 | bytes 196065264 | solution.py:259
  807.4 2.5 fusion.223
  809.9 5.8 copy-done.1
  815.7 9.0 fusion.224
  824.7 6.5 bitcast_add_fusion.7
  831.2 2.6 fusion.225
  834.6 8.2 fusion.226
  849.6 5.8 copy-done.1
  855.3 9.0 fusion.224
  864.3 7.1 bitcast_add_fusion.7
  871.4 2.6 fusion.225
  874.8 8.2 fusion.226
  887.2 18.4 reduce-scatter.10.cloned.1.call-done
  909.5 20.9 reduce-scatter.12.cloned.1.call-done
  930.4 3.0 fusion.120
  933.7 9.4 fusion.101
  946.8 8.3 fusion.99
  955.2 19.9 fusion.131
  975.2 19.6 fusion.132
  995.5 20.0 fusion.104
  1017.3 6.0 fusion.130
  1023.4 12.2 fusion.74
  1039.1 39.9 all-reduce.4
  1080.2 3.2 fusion.94
  1083.4 124.6 %reduce-scatter.18.cloned.1.call-done = f32[64,256]{1,0:T(8,128)} async-done(((f32[2048,256]{1,0:T(8,128)}), f32[64,256]{1,0:T(8,128)}) %reduce-scatter.18.cloned.1.call-update) | async-done | bytes 65552 | tf_op jit(solution)/shard_map/reduce_scatter | solution.py:298
  1208.0 357.9 %reduce-scatter.20.cloned.1.call-done = f32[64,2048]{1,0:T(8,128)} async-done(((f32[2048,2048]{1,0:T(8,128)}), f32[64,2048]{1,0:T(8,128)}) %reduce-scatter.20.cloned.1.call-update) | async-done | bytes 524304 | tf_op jit(solution)/shard_map/reduce_scatter | solution.py:299
  1565.9 360.2 %reduce-scatter.14.cloned.1.call-done = f32[64,2048]{1,0:T(8,128)} async-done(((f32[2048,2048]{1,0:T(8,128)}), f32[64,2048]{1,0:T(8,128)}) %reduce-scatter.14.cloned.1.call-update) | async-done | bytes 524304 | tf_op jit(solution)/shard_map/reduce_scatter | solution.py:296
  1926.1 969.4 %reduce-scatter.22.cloned.1.call-done = f32[64,5632]{1,0:T(8,128)} async-done(((f32[2048,5632]{1,0:T(8,128)}), f32[64,5632]{1,0:T(8,128)}) %reduce-scatter.22.cloned.1.call-update) | async-done | bytes 1441808 | tf_op jit(solution)/shard_map/reduce_scatter | solution.py:212
  2895.5 970.1 %reduce-scatter.24.cloned.1.call-done = f32[64,5632]{1,0:T(8,128)} async-done(((f32[2048,5632]{1,0:T(8,128)}), f32[64,5632]{1,0:T(8,128)}) %reduce-scatter.24.cloned.1.call-update) | async-done | bytes 1441808 | tf_op jit(solution)/shard_map/reduce_scatter | solution.py:213
  3865.6 970.1 %reduce-scatter.26.cloned.1.call-done = f32[176,2048]{1,0:T(8,128)} async-done(((f32[5632,2048]{1,0:T(8,128)}), f32[176,2048]{1,0:T(8,128)}) %reduce-scatter.26.cloned.1.call-update) | async-done | bytes 1441808 | tf_op jit(solution)/shard_map/reduce_scatter | solution.py:214
  (241 shorter events, 55.5 us)
Async XLA Ops:
  7.2 4.9 copy-start.41
  7.2 5.2 copy-start.42
  7.2 47.6 copy-start.38
  7.2 47.6 copy-start.39
  7.2 47.6 copy-start.40
  7.2 53.2 %copy-start.3 = (bf16[1,256,2048]{2,1,0:T(8,128)(2,1)S(1)}, bf16[1,256,2048]{2,1,0:T(8,128)(2,1)}, u32[]{:S(2)}) copy-start(bf16[1,256,2048]{2,1,0:T(8,128)(2,1)} %param.22) | copy-start | bytes 3145732
  7.2 60.4 %all-gather.10.cloned.1.call-start = ((), (), s32[]{:S(2)}) async-start(), calls=%async_computation.10 | async-start | bytes 1081344 | tf_op jit(solution)/shard_map/all_gather | solution.py:92
  8.0 115.4 %all-gather.8.cloned.1.call-start = ((), (), s32[]{:S(2)}) async-start(), calls=%async_computation.9 | async-start | bytes 1081344 | tf_op jit(solution)/shard_map/all_gather | solution.py:93
  8.7 195.5 %all-gather.12.cloned.1.call-start = ((), (), s32[]{:S(2)}) async-start(), calls=%async_computation.11 | async-start | bytes 8650752 | tf_op jit(solution)/shard_map/all_gather | solution.py:91
  9.5 277.7 %all-gather.14.cloned.1.call-start = ((), (), s32[]{:S(2)}) async-start(), calls=%async_computation.12 | async-start | bytes 8650752 | tf_op jit(solution)/shard_map/all_gather | solution.py:94
  10.0 419.1 %all-gather.16.cloned.1.call-start = ((), (), s32[]{:S(2)}) async-start(), calls=%async_computation.13 | async-start | bytes 23789568 | tf_op jit(solution)/shard_map/all_gather | solution.py:181
  10.6 564.1 %all-gather.18.cloned.1.call-start = ((), (), s32[]{:S(2)}) async-start(), calls=%async_computation.14 | async-start | bytes 23789568 | tf_op jit(solution)/shard_map/all_gather | solution.py:182
  11.2 709.2 %all-gather.20.cloned.1.call-start = ((), (), s32[]{:S(2)}) async-start(), calls=%async_computation.15 | async-start | bytes 23789568 | tf_op jit(solution)/shard_map/all_gather | solution.py:183
  11.9 893.6 %reduce-scatter.10.cloned.1.call-start = ((), (), s32[]{:S(2)}) async-start(), calls=%async_computation.16 | async-start | bytes 655360 | tf_op jit(solution)/shard_map/reduce_scatter | solution.py:265
  54.8 161.7 %copy-start.30 = (f32[2048]{0:T(1024)}, f32[2048]{0:T(1024)S(1)}, u32[]{:S(2)}) copy-start(f32[2048]{0:T(1024)S(1)} %convert_element_type.156) | copy-start | bytes 24580
  54.8 711.6 %copy-start.34 = (f32[1,256]{1,0:T(1,128)}, f32[1,256]{1,0:T(1,128)S(1)}, u32[]{:S(2)}) copy-start(f32[1,256]{1,0:T(1,128)S(1)} %convert_element_type.178) | copy-start | bytes 3076
  60.5 162.1 %copy-start.17 = (f32[256,64]{0,1:T(8,128)}, f32[256,64]{0,1:T(8,128)S(1)}, u32[]{:S(2)}) copy-start(f32[256,64]{0,1:T(8,128)S(1)} %get-tuple-element.563) | copy-start | bytes 196612
  60.5 162.1 %copy-start.19 = (f32[256,64]{0,1:T(8,128)}, f32[256,64]{0,1:T(8,128)S(1)}, u32[]{:S(2)}) copy-start(f32[256,64]{0,1:T(8,128)S(1)} %get-tuple-element.564) | copy-start | bytes 196612
  61.4 155.1 %copy-start.32 = (f32[256]{0:T(256)}, f32[256]{0:T(256)S(1)}, u32[]{:S(2)}) copy-start(f32[256]{0:T(256)S(1)} %get-tuple-element.566) | copy-start | bytes 3076
  293.3 1.3 copy-start.8
  294.9 279.8 %copy-start.10 = (bf16[256,2048]{1,0:T(8,128)(2,1)}, bf16[256,2048]{1,0:T(8,128)(2,1)S(1)}, u32[]{:S(2)}) copy-start(bf16[256,2048]{1,0:T(8,128)(2,1)S(1)} %multiply_convert_fusion.3) | copy-start | bytes 3145732
  751.5 14.9 copy-start.14
  769.3 1.4 copy-start.5
  777.4 1.5 copy-start.23
  803.2 4.2 copy-start.11
  803.2 4.2 copy-start.24
  809.9 5.8 copy-start.1
  824.7 6.5 copy-start
  824.7 6.5 copy-start.27
  831.2 3.4 copy-start.16
  834.6 8.2 copy-start.12
  834.6 8.2 copy-start.25
  842.8 4.2 copy-start.11
  842.8 4.2 copy-start.24
  849.6 5.8 copy-start.1
  864.3 7.1 copy-start
  864.3 7.1 copy-start.27
  871.4 3.4 copy-start.16
  874.8 8.2 copy-start.12
  874.8 8.2 copy-start.25
  883.0 2.6 copy-start.29
  884.7 20.9 copy-start.20
  885.6 21.0 copy-start.18
  885.6 44.8 reduce-scatter.12.cloned.1.call-start
  886.2 21.3 copy-start.4
  886.2 21.3 copy-start.31
  886.2 21.3 copy-start.33
  887.1 196.3 %reduce-scatter.16.cloned.1.call-start = ((), (), s32[]{:S(2)}) async-start(), calls=%async_computation.19 | async-start | bytes 2162688 | tf_op jit(solution)/shard_map/reduce_scatter | solution.py:297
  909.5 24.2 copy-start.6
  909.5 298.5 %reduce-scatter.18.cloned.1.call-start = ((), (), s32[]{:S(2)}) async-start(), calls=%async_computation.20 | async-start | bytes 2162688 | tf_op jit(solution)/shard_map/reduce_scatter | solution.py:298
  933.4 632.4 %reduce-scatter.20.cloned.1.call-start = ((), (), s32[]{:S(2)}) async-start(), calls=%async_computation.21 | async-start | bytes 17301504 | tf_op jit(solution)/shard_map/reduce_scatter | solution.py:299
  943.1 1.6 copy-start.2
  943.1 983.0 %reduce-scatter.14.cloned.1.call-start = ((), (), s32[]{:S(2)}) async-start(), calls=%async_computation.18 | async-start | bytes 17301504 | tf_op jit(solution)/shard_map/reduce_scatter | solution.py:296
  955.2 1940.3 %reduce-scatter.22.cloned.1.call-start = ((), (), s32[]{:S(2)}) async-start(), calls=%async_computation.22 | async-start | bytes 47579136 | tf_op jit(solution)/shard_map/reduce_scatter | solution.py:212
  975.2 2890.4 %reduce-scatter.24.cloned.1.call-start = ((), (), s32[]{:S(2)}) async-start(), calls=%async_computation.23 | async-start | bytes 47579136 | tf_op jit(solution)/shard_map/reduce_scatter | solution.py:213
  994.9 3840.9 %reduce-scatter.26.cloned.1.call-start = ((), (), s32[]{:S(2)}) async-start(), calls=%async_computation.24 | async-start | bytes 47579136 | tf_op jit(solution)/shard_map/reduce_scatter | solution.py:214
  1017.3 6.0 copy-start.9
  1017.3 6.0 copy-start.13
  1023.4 12.2 copy-start.15
  1035.6 1.2 copy-start.22
  1035.6 1.2 copy-start.26
  1036.8 2.3 copy-start.36
  1036.8 43.4 copy-start.7
  1036.8 43.4 copy-start.37
  (4 other events, 3.0 us)
Sparse Core Ops, SparseCore 0:
  11.1 56.5 all-gather.9
  70.6 52.7 all-gather.7
  126.4 77.8 all-gather.11
  207.1 75.9 all-gather.13
  285.9 143.1 all-gather.15
  431.9 142.7 all-gather.17
  577.6 142.7 all-gather.19
  885.7 19.8 reduce-scatter.9
  908.8 21.6 reduce-scatter.11
  933.1 137.5 reduce-scatter.15
  1073.7 134.3 reduce-scatter.17
  1210.7 355.1 reduce-scatter.19
  1568.7 357.3 reduce-scatter.13
  1928.8 966.6 reduce-scatter.21
  2898.2 967.3 reduce-scatter.23
  3868.3 967.3 reduce-scatter.25
where the time goes:
time: 4850 us; the launch traced here: 4840 us
  waiting for transfers between devices  4320 us (89%)
  matrix products  302 us (6%)
  blocking collectives  102 us (2%)
    reduce_scatter x1, waiting for transfers between devices, per_device(): lax.psum_scatter(grad_down, ('seq', 'batch'), scatter_dimension=0, tiled=...  970 us
    reduce_scatter x1, waiting for transfers between devices, per_device(): lax.psum_scatter(grad_up, ('seq', 'batch'), scatter_dimension=0, tiled=True)  970 us
    reduce_scatter x1, waiting for transfers between devices, per_device(): lax.psum_scatter(grad_gate, ('seq', 'batch'), scatter_dimension=0, tiled=...  969 us
    reduce_scatter x1, waiting for transfers between devices, per_device(): lax.psum_scatter(grad_wq, ('seq', 'batch'), scatter_dimension=0, tiled=True)  360 us
    reduce_scatter x1, waiting for transfers between devices, per_device(): lax.psum_scatter(grad_wout, ('seq', 'batch'), scatter_dimension=0, tiled=...  358 us
    all_gather x1, waiting for transfers between devices, per_device(): lax.all_gather(w_gate, ('seq', 'batch'), axis=0, tiled=True)  134 us
    all_gather x1, waiting for transfers between devices, per_device(): lax.all_gather(w_down, ('seq', 'batch'), axis=0, tiled=True)  132 us
    all_gather x1, waiting for transfers between devices, per_device(): lax.all_gather(w_up, ('seq', 'batch'), axis=0, tiled=True)  132 us
  transfers between devices with their start and end apart: 16, of which 14 were waited for; matrix products, arithmetic and copies ran while one was open for 5% of the time, Pallas kernels for 0%

commit v1 on v0

v1 whole, which is shorter than its diff:
```python
import functools

import jax
import jax.numpy as jnp
from jax import lax
from jax.experimental import pallas as pl
from jax.experimental.pallas import tpu as pltpu
from jax.sharding import PartitionSpec as P

HEADS = 32
KV_HEADS = 4
HEAD_DIM = 64
HALF = HEAD_DIM // 2

EPSILON = 1e-05
MASKED_SCORE = -1e30
SCALE = HEAD_DIM ** (-0.5)
CONTRACT_ROWS = (((0,), (0,)), ((), ()))
CONTRACT_COLS = (((1,), (1,)), ((), ()))
BF16 = jnp.bfloat16
F32 = jnp.float32


def product(left, right):
    return jnp.dot(left, right, preferred_element_type=F32)


def product_rows(left, right):
    return lax.dot_general(left, right, CONTRACT_ROWS, preferred_element_type=F32)


def product_cols(left, right):
    return lax.dot_general(left, right, CONTRACT_COLS, preferred_element_type=F32)


def rms_scale(inputs):
    return lax.rsqrt(jnp.mean(inputs * inputs, axis=-1, keepdims=True) + EPSILON)


def norm_back(grad_normed, inputs, inverse, gain):
    scaled = gain * grad_normed
    cubed = inverse * inverse * inverse
    return inverse * scaled - inputs * cubed * jnp.mean(scaled * inputs, axis=-1, keepdims=True)


class Axis:
    def __init__(self, name, inner):
        self.name = name
        self.size = lax.axis_size(name)
        self.inner = inner
        self.outer = self.size // inner
        index = lax.axis_index(name)
        self.index = index
        self.o = index // inner
        self.i = index % inner

    def shift(self, value, outer_by, inner_by):
        pairs = []
        for o in range(self.outer):
            for i in range(self.inner):
                target = ((o + outer_by) % self.outer) * self.inner + (i + inner_by) % self.inner
                pairs.append((o * self.inner + i, target))
        return lax.ppermute(value, self.name, pairs)

    def before(self, outer_by, inner_by):
        o = lax.rem(self.o + self.outer - outer_by, self.outer)
        i = lax.rem(self.i + self.inner - inner_by, self.inner)
        return o * self.inner + i

    def after(self, outer_by, inner_by):
        o = lax.rem(self.o + outer_by, self.outer)
        i = lax.rem(self.i + inner_by, self.inner)
        return o * self.inner + i

    def gather(self, block, dim=0):
        shape = block.shape[:dim] + (self.size,) + block.shape[dim:]
        out = jnp.zeros(shape, block.dtype)
        for k in range(self.outer):
            got = block if k == 0 else self.shift(block, k, 0)
            for m in range(self.inner):
                piece = got if m == 0 else self.shift(got, 0, m)
                out = lax.dynamic_update_slice_in_dim(
                    out, jnp.expand_dims(piece, dim), self.before(k, m), dim
                )
        return out

    def scatter_sum(self, parts, dim=0):
        shape = parts.shape[:dim] + (self.outer, self.inner) + parts.shape[dim + 1 :]
        grid = parts.reshape(shape)

        def inner_part(i):
            return lax.squeeze(lax.dynamic_slice_in_dim(grid, i, 1, dim + 1), (dim + 1,))

        total = inner_part(self.i).astype(F32)
        for m in range(1, self.inner):
            mine = inner_part(lax.rem(self.i + m, self.inner))
            total = total + self.shift(mine, 0, m).astype(F32)
        low = total.astype(BF16)

        def outer_part(o):
            return lax.squeeze(lax.dynamic_slice_in_dim(low, o, 1, dim), (dim,))

        out = outer_part(self.o).astype(F32)
        for k in range(1, self.outer):
            out = out + self.shift(outer_part(lax.rem(self.o + k, self.outer)), k, 0).astype(F32)
        return out

    def exchange(self, parts):
        out = jnp.zeros(parts.shape, parts.dtype)
        for k in range(self.outer):
            for m in range(self.inner):
                part = lax.dynamic_slice_in_dim(parts, self.after(k, m), 1, 0)
                got = part if (k, m) == (0, 0) else self.shift(part, k, m)
                out = lax.dynamic_update_slice_in_dim(out, got, self.before(k, m), 0)
        return out


def rotate_lanes(value, sign):
    lane = lax.broadcasted_iota(jnp.int32, value.shape, 1) % HEAD_DIM
    first = lane < HALF
    width = value.shape[1]
    up = pltpu.roll(value, width - HALF, 1)
    down = pltpu.roll(value, HALF, 1)
    return jnp.where(first, -sign * up, sign * down)


def mask_bias(bias_ref, seg_row_ref, seg_col_ref, length):
    rows = 256
    for start in range(0, length, rows):
        keys = seg_col_ref[start : start + rows, :]
        queries = seg_row_ref[:, :]
        key_pos = start + lax.broadcasted_iota(jnp.int32, (rows, length), 0)
        query_pos = lax.broadcasted_iota(jnp.int32, (rows, length), 1)
        allowed = (keys == queries) & (key_pos <= query_pos)
        bias_ref[start : start + rows, :] = jnp.where(allowed, 0.0, MASKED_SCORE)


def attend_kernel(
    qblock,
    q_ref,
    kv_ref,
    cos_ref,
    sin_ref,
    seg_row_ref,
    seg_col_ref,
    o_ref,
    qr_ref,
    kvr_ref,
    lse_ref,
    bias_ref,
):
    length = q_ref.shape[0]
    cosine = cos_ref[...]
    sine = sin_ref[...]

    @pl.when(pl.program_id(0) == 0)
    def _():
        mask_bias(bias_ref, seg_row_ref, seg_col_ref, length)
        kv = kv_ref[...]
        rotated = kv * cosine + rotate_lanes(kv, 1.0) * sine
        lane = lax.broadcasted_iota(jnp.int32, kv.shape, 1)
        kvr_ref[...] = jnp.where(lane < HEAD_DIM, rotated, kv).astype(BF16)

    q = q_ref[...]
    qr_ref[...] = (q * cosine + rotate_lanes(q, 1.0) * sine).astype(BF16)
    for start in range(0, length, qblock):
        stop = start + qblock
        keys = kvr_ref[:stop, :HEAD_DIM]
        values = kvr_ref[:stop, HEAD_DIM:]
        for head in range(2):
            lanes = slice(head * HEAD_DIM, (head + 1) * HEAD_DIM)
            queries = qr_ref[start:stop, lanes] * SCALE
            scores = product_cols(keys, queries.astype(BF16)) + bias_ref[:stop, start:stop]
            top = jnp.max(scores, axis=0, keepdims=True)
            grown = jnp.exp(scores - top)
            total = jnp.sum(grown, axis=0, keepdims=True)
            probs = (grown * (1.0 / total)).astype(BF16)
            lse_ref[0, head : head + 1, start:stop] = top + jnp.log(total)
            o_ref[start:stop, lanes] = product_rows(probs, values).astype(BF16)


def attend_back_kernel(
    qblock,
    qr_ref,
    kvr_ref,
    do_ref,
    lse_ref,
    cos_ref,
    sin_ref,
    seg_row_ref,
    seg_col_ref,
    dqkv_ref,
    bias_ref,
    dq_ref,
    dk_ref,
    dv_ref,
):
    length = qr_ref.shape[0]
    cosine = cos_ref[...]
    sine = sin_ref[...]
    pair = pl.program_id(0)

    @pl.when(pair == 0)
    def _():
        mask_bias(bias_ref, seg_row_ref, seg_col_ref, length)
        dk_ref[...] = jnp.zeros_like(dk_ref)
        dv_ref[...] = jnp.zeros_like(dv_ref)

    for start in range(0, length, qblock):
        stop = start + qblock
        keys = kvr_ref[:stop, :HEAD_DIM]
        values = kvr_ref[:stop, HEAD_DIM:]
        for head in range(2):
            lanes = slice(head * HEAD_DIM, (head + 1) * HEAD_DIM)
            queries = (qr_ref[start:stop, lanes] * SCALE).astype(BF16)
            grads = do_ref[start:stop, lanes]
            scores = product_cols(keys, queries) + bias_ref[:stop, start:stop]
            probs = jnp.exp(scores - lse_ref[0, head : head + 1, start:stop])
            dprobs = product_cols(values, grads)
            delta = jnp.sum(probs * dprobs, axis=0, keepdims=True)
            dscores = (probs * (dprobs - delta)).astype(BF16)
            dv_ref[:stop, :] += product(probs.astype(BF16), grads)
            dk_ref[:stop, :] += product(dscores, queries)
            dq_ref[start:stop, lanes] = product_rows(dscores, keys) * SCALE

    dq = dq_ref[...]
    turned = rotate_lanes(dq * sine, -1.0)
    columns = pl.ds(pl.multiple_of(pair * 128, 128), 128)
    dqkv_ref[:, columns] = (dq * cosine + turned).astype(BF16)

    @pl.when(pair == pl.num_programs(0) - 1)
    def _():
        grads = jnp.concatenate([dk_ref[...], dv_ref[...]], axis=1)
        back = grads * cosine + rotate_lanes(grads * sine, -1.0)
        lane = lax.broadcasted_iota(jnp.int32, grads.shape, 1)
        width = dqkv_ref.shape[1]
        dqkv_ref[:, width - 128 :] = jnp.where(lane < HEAD_DIM, back, grads).astype(BF16)


def whole_spec(shape):
    return pl.BlockSpec(shape, lambda j: (0,) * len(shape))


def attend(qkv, cosine, sine, seg_row, seg_col):
    length, width = qkv.shape
    pairs = width // 128 - 1
    qblock = min(256, length)
    return pl.pallas_call(
        functools.partial(attend_kernel, qblock),
        grid=(pairs,),
        in_specs=[
            pl.BlockSpec((length, 128), lambda j: (0, j)),
            pl.BlockSpec((length, 128), lambda j: (0, pairs)),
            whole_spec((length, 128)),
            whole_spec((length, 128)),
            whole_spec((1, length)),
            whole_spec((length, 1)),
        ],
        out_specs=[
            pl.BlockSpec((length, 128), lambda j: (0, j)),
            pl.BlockSpec((length, 128), lambda j: (0, j)),
            whole_spec((length, 128)),
            pl.BlockSpec((1, 2, length), lambda j: (j, 0, 0)),
        ],
        out_shape=[
            jax.ShapeDtypeStruct((length, pairs * 128), BF16),
            jax.ShapeDtypeStruct((length, pairs * 128), BF16),
            jax.ShapeDtypeStruct((length, 128), BF16),
            jax.ShapeDtypeStruct((pairs, 2, length), F32),
        ],
        scratch_shapes=[pltpu.VMEM((length, length), F32)],
        compiler_params=pltpu.CompilerParams(vmem_limit_bytes=48 * 1024 * 1024),
        cost_estimate=pl.CostEstimate(
            flops=pairs * 2 * length * length * HEAD_DIM * 2,
            bytes_accessed=8 * length * width,
            transcendentals=pairs * length * length,
        ),
    )(qkv, qkv, cosine, sine, seg_row, seg_col)


def attend_back(qr, kvr, grads, lse, cosine, sine, seg_row, seg_col):
    length = qr.shape[0]
    pairs = qr.shape[1] // 128
    qblock = min(256, length)
    return pl.pallas_call(
        functools.partial(attend_back_kernel, qblock),
        grid=(pairs,),
        in_specs=[
            pl.BlockSpec((length, 128), lambda j: (0, j)),
            whole_spec((length, 128)),
            pl.BlockSpec((length, 128), lambda j: (0, j)),
            pl.BlockSpec((1, 2, length), lambda j: (j, 0, 0)),
            whole_spec((length, 128)),
            whole_spec((length, 128)),
            whole_spec((1, length)),
            whole_spec((length, 1)),
        ],
        out_specs=whole_spec((length, (pairs + 1) * 128)),
        out_shape=jax.ShapeDtypeStruct((length, (pairs + 1) * 128), BF16),
        scratch_shapes=[
            pltpu.VMEM((length, length), F32),
            pltpu.VMEM((length, 128), F32),
            pltpu.VMEM((length, HEAD_DIM), F32),
            pltpu.VMEM((length, HEAD_DIM), F32),
        ],
        compiler_params=pltpu.CompilerParams(vmem_limit_bytes=48 * 1024 * 1024),
        cost_estimate=pl.CostEstimate(
            flops=pairs * 5 * length * length * HEAD_DIM * 2,
            bytes_accessed=12 * length * qr.shape[1],
            transcendentals=pairs * length * length,
        ),
    )(qr, kvr, grads, lse, cosine, sine, seg_row, seg_col)


def per_device(
    tokens,
    cotangent,
    selection,
    segments,
    positions,
    gain_attn,
    w_query,
    w_key,
    w_value,
    w_out,
    gain_mlp,
    w_gate,
    w_up,
    w_down,
):
    seq = Axis("seq", 2)
    batch = Axis("batch", lax.axis_size("batch") // 4)
    n_seq, n_batch = seq.size, batch.size
    length, width = tokens.shape[1], tokens.shape[2]
    total_len = length * n_seq
    rows = w_query.shape[0]
    ff = w_gate.shape[1]
    q_cols = w_query.shape[1] // n_seq
    sharers = n_seq // KV_HEADS

    query_parts = w_query.reshape(rows, n_seq, q_cols)
    key_parts = jnp.repeat(w_key.reshape(rows, KV_HEADS, HEAD_DIM), sharers, axis=1)
    value_parts = jnp.repeat(w_value.reshape(rows, KV_HEADS, HEAD_DIM), sharers, axis=1)
    qkv_parts = jnp.concatenate([query_parts, key_parts, value_parts], axis=2).transpose(1, 0, 2)

    def spread(parts):
        mine = seq.exchange(parts)
        return batch.gather(mine, 1).reshape(n_seq * n_batch * rows, parts.shape[2])

    def collect(grad):
        parts = grad.astype(BF16).reshape(n_seq, n_batch, rows, grad.shape[1])
        return seq.exchange(batch.scatter_sum(parts, 1).astype(BF16)).astype(F32)

    def by_columns(weight):
        return weight.reshape(rows, n_seq, weight.shape[1] // n_seq).transpose(1, 0, 2)

    places = seq.gather(jnp.stack([segments[0], positions[0]]), 1)
    seg_all = places[0].reshape(total_len)
    pos_all = places[1].reshape(total_len)
    gains = batch.gather(seq.gather(jnp.stack([gain_attn, gain_mlp]), 1), 2)
    gain_one = gains[0].reshape(1, width).astype(F32)
    gain_two = gains[1].reshape(1, width).astype(F32)
    x_all = seq.gather(tokens[0], 0).reshape(total_len, width).astype(F32)
    w_qkv = spread(qkv_parts)
    wo = batch.gather(w_out, 0).reshape(n_batch * rows, width)
    wg = spread(by_columns(w_gate))
    wu = spread(by_columns(w_up))
    wd = batch.gather(w_down, 0).reshape(n_batch * w_down.shape[0], width)

    grad_out_row = cotangent[0].astype(F32) * selection[0].astype(F32)[:, None]
    grad_low = seq.gather(grad_out_row.astype(BF16), 0).reshape(total_len, width)

    row_input = tokens[0].astype(F32)
    inv_attn = rms_scale(row_input)
    normed1 = (x_all * rms_scale(x_all) * gain_one).astype(BF16)
    qkv = product(normed1, w_qkv)
    frequency = 10000.0 ** (-(jnp.arange(HALF, dtype=F32) * 2.0 / HEAD_DIM))
    angles = pos_all.astype(F32)[:, None] * jnp.tile(frequency, 4)[None, :]
    cosine, sine = jnp.cos(angles), jnp.sin(angles)
    seg_row, seg_col = seg_all[None, :], seg_all[:, None]
    heads_out, query_rot, kv_rot, lse = attend(qkv, cosine, sine, seg_row, seg_col)
    attn_part = product(heads_out, wo).astype(BF16).reshape(n_seq, length, width)
    residual = row_input + seq.scatter_sum(attn_part, 0)

    inv_mlp = rms_scale(residual)
    normed2_own = (residual * inv_mlp * gain_two).astype(BF16)
    normed2 = seq.gather(normed2_own, 0).reshape(total_len, width)
    gate_proj = product(normed2, wg)
    up_proj = product(normed2, wu)
    sigma = jax.nn.sigmoid(gate_proj)
    activated = gate_proj * sigma
    hidden = (activated * up_proj).astype(BF16)
    mixed_part = product(hidden, wd).astype(BF16).reshape(n_seq, length, width)
    mixed = (residual + seq.scatter_sum(mixed_part, 0)).astype(BF16)[None]

    grad_down = product_rows(hidden, grad_low)
    grad_hidden = product_cols(grad_low, wd)
    grad_gate_act = (
        grad_hidden * up_proj * sigma * (1.0 + gate_proj * (1.0 - sigma))
    ).astype(BF16)
    grad_up_act = (grad_hidden * activated).astype(BF16)
    grad_gate = product_rows(normed2, grad_gate_act)
    grad_up = product_rows(normed2, grad_up_act)
    normed_part = product_cols(grad_gate_act, wg) + product_cols(grad_up_act, wu)
    normed_terms = seq.scatter_sum(normed_part.astype(BF16).reshape(n_seq, length, width), 0)
    grad_resid = grad_out_row + norm_back(normed_terms, residual, inv_mlp, gain_two)

    down_own = batch.scatter_sum(
        grad_down.astype(BF16).reshape(n_batch, w_down.shape[0], width), 0
    )
    gate_own = collect(grad_gate).transpose(1, 0, 2).reshape(rows, ff)
    up_own = collect(grad_up).transpose(1, 0, 2).reshape(rows, ff)

    grad_branch = seq.gather(grad_resid.astype(BF16), 0).reshape(total_len, width)
    grad_wout = product_rows(heads_out, grad_branch)
    grad_heads = product_cols(grad_branch, wo).astype(BF16)
    grad_qkv_act = attend_back(
        query_rot, kv_rot, grad_heads, lse, cosine, sine, seg_row, seg_col
    )
    grad_wqkv = product_rows(normed1, grad_qkv_act)
    input_part = product_cols(grad_qkv_act, w_qkv).astype(BF16).reshape(n_seq, length, width)
    grad_normed1 = seq.scatter_sum(input_part, 0)
    tokens_grad = (
        grad_resid + norm_back(grad_normed1, row_input, inv_attn, gain_one)
    ).astype(BF16)[None]
    out_own = batch.scatter_sum(grad_wout.astype(BF16).reshape(n_batch, rows, width), 0)
    qkv_own = collect(grad_wqkv)
    query_own = qkv_own[:, :, :q_cols].transpose(1, 0, 2).reshape(rows, n_seq * q_cols)

    def shared(columns):
        heads = columns.reshape(KV_HEADS, sharers, rows, HEAD_DIM).sum(axis=1)
        return heads.transpose(1, 0, 2).reshape(rows, KV_HEADS * HEAD_DIM)

    key_own = shared(qkv_own[:, :, q_cols : q_cols + HEAD_DIM])
    value_own = shared(qkv_own[:, :, q_cols + HEAD_DIM :])

    def along(weight, grad):
        return jnp.sum(weight.astype(F32) * grad, axis=1)

    gain1_own = (
        along(w_query, query_own) + along(w_key, key_own) + along(w_value, value_own)
    ) / gain_attn.astype(F32)
    gain2_own = (along(w_gate, gate_own) + along(w_up, up_own)) / gain_mlp.astype(F32)
    return (
        mixed,
        tokens_grad,
        query_own,
        key_own,
        value_own,
        out_own,
        gate_own,
        up_own,
        down_own,
        gain1_own,
        gain2_own,
    )


def solution(mesh):
    both = ("seq", "batch")
    tokens = P("batch", "seq", None)
    flags = P("batch", "seq")
    matrix = P(both, None)
    vector = P(both)
    in_specs = (
        (tokens, tokens, flags, flags, flags)
        + (vector, matrix, matrix, matrix, matrix)
        + (vector, matrix, matrix, matrix)
    )
    out_specs = (tokens, tokens) + (matrix,) * 7 + (vector, vector)
    return jax.shard_map(
        per_device, mesh=mesh, in_specs=in_specs, out_specs=out_specs, check_vma=False
    )
```

time: 4850 us -> 1110 us (0.23)
  waiting for transfers between devices: 4320 us -> 599 us
  matrix products: 302 us -> 111 us
  starting transfers between devices: 1.25 us -> 183 us
  blocking collectives: 102 us -> 0 us
  local copies, waits for them, and re-layouts: 45.9 us -> 113 us
    reduce_scatter x9 -> x0, waiting for transfers between devices: 3790 us -> none  [the longest x1 970 us: per_device(): lax.psum_scatter(grad_down, ('seq', 'batch'), scatter_dimension=0, tiled=...]
    ppermute x0 -> x106, waiting for transfers between devices: none -> 599 us  [shift(): return lax.ppermute(value, self.name, pairs)]
    all_gather x7 -> x0, waiting for transfers between devices: 521 us -> none  [the longest x1 134 us: per_device(): lax.all_gather(w_gate, ('seq', 'batch'), axis=0, tiled=True)]
    dot_general x39 -> x15, matrix products: 302 us -> 111 us  [the longest x5 40.3 us: product(): return jnp.dot(left, right, preferred_element_type=F32)]
    ppermute x0 -> x106, starting transfers between devices: none -> 183 us  [shift(): return lax.ppermute(value, self.name, pairs)]
    unnamed x2 -> x0, blocking collectives: 82.1 us -> none
  transfers between devices with their start and end apart: 16 -> 106, of which waited for: 14 -> 45; matrix products, arithmetic and copies ran while one was open for 5% -> 17% of each run, Pallas kernels for 0% -> 1%
where the time goes in v1:
time: 1110 us; the launch traced here: 1100 us
  waiting for transfers between devices  599 us (54%)
  starting transfers between devices  183 us (16%)
  local copies, waits for them, and re-layouts  113 us (10%)
  matrix products  111 us (10%)
  other arithmetic  50.5 us (5%)
  Pallas kernels  38.4 us (3%)
    ppermute x106, waiting for transfers between devices, shift(): return lax.ppermute(value, self.name, pairs)  599 us
    ppermute x106, starting transfers between devices, shift(): return lax.ppermute(value, self.name, pairs)  183 us
    dynamic_update_slice x69, local copies, waits for them, and re-layouts, gather(): lax.dynamic_update_slice_in_dim(out, jnp.expand_dims(piece, dim), self.be...  41.1 us
    dot_general x5, matrix products, product(): return jnp.dot(left, right, preferred_element_type=F32)  40.3 us
    dot_general x5, matrix products, product_cols(): lax.dot_general(left, right, CONTRACT_COLS, preferred_element_type=F32)  38.3 us
    dot_general x5, matrix products, product_rows(): lax.dot_general(left, right, CONTRACT_ROWS, preferred_element_type=F32)  32.1 us
    pallas_call x1, Pallas kernels, attend_back(): pl.pallas_call(functools.partial(attend_back_kernel, qblock), grid=(pairs...  22.8 us
  transfers between devices with their start and end apart: 106, of which 45 were waited for; matrix products, arithmetic and copies ran while one was open for 17% of the time, Pallas kernels for 1%

profile of v1, /device:TPU:0, one launch (start us, length us, event | category | flops | bytes accessed | tf_op | source)
XLA Modules:
  0.0 1097.9 jit_solution(17224495226722061045)
XLA Ops:
  26.6 3.3 broadcast_in_dim.302
  58.2 17.5 %collective-permute-done.14 = bf16[1,64,640]{2,1,0:T(8,128)(2,1)S(1)} collective-permute-done((bf16[1,64,640]{2,1,0:T(8,128)(2,1)}, bf16[1,64,640]{2,1,0:T(8,128)(2,1)S(1)}, u32[]{:S(2)}, u32[]{:S(2)}) %collective-permute-start.14) | collective-permute-done | bytes 81952 | tf_op jit(solution)/shard_map/ppermute | solution.py:63
  77.3 3.3 collective-permute-done.15
  84.3 5.4 collective-permute-done.49
  90.6 5.8 collective-permute-done.50
  100.1 4.3 collective-permute-done.39
  105.6 5.4 collective-permute-done.40
  122.4 3.2 collective-permute-done.16
  126.2 3.3 collective-permute-done.17
  129.5 5.6 collective-permute-start.31
  142.2 15.4 %collective-permute-done.30 = bf16[64,2048]{1,0:T(8,128)(2,1)S(1)} collective-permute-done((bf16[64,2048]{1,0:T(8,128)(2,1)S(1)}, bf16[64,2048]{1,0:T(8,128)(2,1)S(1)}, u32[]{:S(2)}, u32[]{:S(2)}) %collective-permute-start.30) | collective-permute-done | bytes 262176 | tf_op jit(solution)/shard_map/ppermute | solution.py:63
  160.1 4.0 collective-permute-done.32
  169.7 13.1 %collective-permute-done.19 = bf16[4,64,640]{2,1,0:T(8,128)(2,1)S(1)} collective-permute-done((bf16[4,64,640]{2,1,0:T(8,128)(2,1)S(1)}, bf16[4,64,640]{2,1,0:T(8,128)(2,1)S(1)}, u32[]{:S(2)}, u32[]{:S(2)}) %collective-permute-start.19) | collective-permute-done | bytes 327712 | tf_op jit(solution)/shard_map/ppermute | solution.py:63
  182.8 3.2 collective-permute-start.21
  186.7 6.4 collective-permute-done.21
  196.5 21.3 %collective-permute-done.22 = bf16[4,64,640]{2,1,0:T(8,128)(2,1)S(1)} collective-permute-done((bf16[4,64,640]{2,1,0:T(8,128)(2,1)S(1)}, bf16[4,64,640]{2,1,0:T(8,128)(2,1)S(1)}, u32[]{:S(2)}, u32[]{:S(2)}) %collective-permute-start.22) | collective-permute-done | bytes 327712 | tf_op jit(solution)/shard_map/ppermute | solution.py:63
  218.6 17.8 %collective-permute-done.52 = bf16[4,64,1408]{2,1,0:T(8,128)(2,1)} collective-permute-done((bf16[4,64,1408]{2,1,0:T(8,128)(2,1)S(1)}, bf16[4,64,1408]{2,1,0:T(8,128)(2,1)}, u32[]{:S(2)}, u32[]{:S(2)}) %collective-permute-start.52) | collective-permute-done | bytes 720928 | tf_op jit(solution)/shard_map/ppermute | solution.py:63
  238.7 17.1 %collective-permute-done.42 = bf16[4,64,1408]{2,1,0:T(8,128)(2,1)S(1)} collective-permute-done((bf16[4,64,1408]{2,1,0:T(8,128)(2,1)}, bf16[4,64,1408]{2,1,0:T(8,128)(2,1)S(1)}, u32[]{:S(2)}, u32[]{:S(2)}) %collective-permute-start.42) | collective-permute-done | bytes 720928 | tf_op jit(solution)/shard_map/ppermute | solution.py:63
  267.8 20.1 %collective-permute-done.61 = bf16[176,2048]{1,0:T(8,128)(2,1)S(1)} collective-permute-done((bf16[176,2048]{1,0:T(8,128)(2,1)S(1)}, bf16[176,2048]{1,0:T(8,128)(2,1)S(1)}, u32[]{:S(2)}, u32[]{:S(2)}) %collective-permute-start.61) | collective-permute-done | bytes 720928 | tf_op jit(solution)/shard_map/ppermute | solution.py:63
  294.3 15.1 %collective-permute-done.62 = bf16[176,2048]{1,0:T(8,128)(2,1)S(1)} collective-permute-done((bf16[176,2048]{1,0:T(8,128)(2,1)S(1)}, bf16[176,2048]{1,0:T(8,128)(2,1)S(1)}, u32[]{:S(2)}, u32[]{:S(2)}) %collective-permute-start.62) | collective-permute-done | bytes 720928 | tf_op jit(solution)/shard_map/ppermute | solution.py:63
  311.3 9.9 collective-permute-done.64
  321.2 57.9 %collective-permute-start.46 = (bf16[4,64,1408]{2,1,0:T(8,128)(2,1)}, bf16[4,64,1408]{2,1,0:T(8,128)(2,1)}, u32[]{:S(2)}, u32[]{:S(2)}) collective-permute-start(bf16[4,64,1408]{2,1,0:T(8,128)(2,1)} %constant_dynamic-update-slice_fusion.12), channel_id=1, source_target_pairs={{0,6},{1,7},{2,0},{3,1},{4,2},{5,3},{6,4},{7,5},{8,14},{9,15},{10,... | collective-permute-start | bytes 2162696 | tf_op jit(solution)/shard_map/ppermute | solution.py:63
  383.2 3.1 multiply_reduce_fusion
  386.3 3.2 multiply_convert_fusion
  389.5 5.0 fusion.48.q_ref.kv_ref
  394.5 15.6 %shard_map.221 = (bf16[1024,512]{1,0:T(8,128)(2,1)S(1)}, bf16[1024,512]{1,0:T(8,128)(2,1)S(1)}, bf16[1024,128]{1,0:T(8,128)(2,1)S(1)}, f32[4,2,1024]{2,1,0:T(2,128)S(1)}) custom-call(f32[1024,640]{1,0:T(8,128)} %fusion.48.q_ref.kv_ref, f32[1024,640]{1,0:T(8,128)} %fusion.48.q_ref.kv_ref, f32[1024,128]{1,0:T(8,128)S(1)} %get-tuple-element.84.cos_ref, ...), custom_call_target="tpu_custom_call" | custom-call | flops 1073741824 | bytes 5242880 | tf_op jit(solution)/shard_map/pallas_call | solution.py:248
  410.1 4.3 convolution_convert_fusion.5
  427.1 10.8 collective-permute-done.43
  441.1 27.7 %collective-permute-done.45 = bf16[4,64,1408]{2,1,0:T(8,128)(2,1)S(1)} collective-permute-done((bf16[4,64,1408]{2,1,0:T(8,128)(2,1)}, bf16[4,64,1408]{2,1,0:T(8,128)(2,1)S(1)}, u32[]{:S(2)}, u32[]{:S(2)}) %collective-permute-start.45) | collective-permute-done | bytes 720928 | tf_op jit(solution)/shard_map/ppermute | solution.py:63
  473.7 10.1 collective-permute-done.47
  484.1 12.1 %collective-permute-done.36 = bf16[256,2048]{1,0:T(8,128)(2,1)S(1)} collective-permute-done((bf16[256,2048]{1,0:T(8,128)(2,1)S(1)}, bf16[256,2048]{1,0:T(8,128)(2,1)S(1)}, u32[]{:S(2)}, u32[]{:S(2)}) %collective-permute-start.36) | collective-permute-done | bytes 1048608 | tf_op jit(solution)/shard_map/ppermute | solution.py:63
  496.2 11.0 fusion.50
  507.6 8.4 fusion.49
  516.0 13.9 %multiply_convert_fusion.2 = (bf16[1024,1408]{1,0:T(8,128)(2,1)}, bf16[1024,1408]{1,0:T(8,128)(2,1)}, bf16[1024,1408]{1,0:T(8,128)(2,1)}) fusion(f32[1024,1408]{1,0:T(8,128)} %fusion.50, f32[1024,1408]{1,0:T(8,128)} %fusion.49, bf16[1024,2048]{1,0:T(8,128)(2,1)S(1)} %bitcast.483, bf16[2048,1408]{1,0:T(8,128)(2,1)S(1)} %bitcast.460), kind=kOutput, calls=%fused_computation.16 | convolution fusion | flops 5927206912 | bytes 30146560 | tf_op jit(solution)/shard_map/dot_general | solution.py:25
  529.9 10.5 fusion.51
  540.4 8.8 convolution_convert_fusion.1
  549.2 8.7 convolution_convert_fusion.2
  557.9 9.0 add_convert_fusion
  570.9 8.7 convolution_convert_fusion.4
  583.7 8.8 constant_dynamic-slice_fusion.4
  592.6 3.9 copy.698
  597.0 8.5 convolution_convert_fusion
  608.8 3.3 fusion.1
  622.8 39.4 %collective-permute-done.88 = bf16[4,4,64,1408]{3,2,0,1:T(8,128)(2,1)} collective-permute-done((bf16[4,4,64,1408]{3,2,0,1:T(8,128)(2,1)}, bf16[4,4,64,1408]{3,2,0,1:T(8,128)(2,1)}, u32[]{:S(2)}, u32[]{:S(2)}) %collective-permute-start.88) | collective-permute-done | bytes 2883616 | tf_op jit(solution)/shard_map/ppermute | solution.py:63
  666.1 57.9 %collective-permute-done.102 = bf16[4,176,2048]{2,1,0:T(8,128)(2,1)} collective-permute-done((bf16[4,176,2048]{2,1,0:T(8,128)(2,1)}, bf16[4,176,2048]{2,1,0:T(8,128)(2,1)}, u32[]{:S(2)}, u32[]{:S(2)}) %collective-permute-start.102) | collective-permute-done | bytes 2883616 | tf_op jit(solution)/shard_map/ppermute | solution.py:63
  729.2 55.5 %collective-permute-done.95 = bf16[4,4,64,1408]{3,2,0,1:T(8,128)(2,1)S(1)} collective-permute-done((bf16[4,4,64,1408]{3,2,0,1:T(8,128)(2,1)}, bf16[4,4,64,1408]{3,2,0,1:T(8,128)(2,1)S(1)}, u32[]{:S(2)}, u32[]{:S(2)}) %collective-permute-start.95) | collective-permute-done | bytes 2883616 | tf_op jit(solution)/shard_map/ppermute | solution.py:63
  787.1 3.6 collective-permute-start.98
  796.9 3.4 collective-permute-start.105
  800.3 5.4 collective-permute-done.89
  805.7 31.1 %collective-permute-start.104 = (bf16[176,2048]{1,0:T(8,128)(2,1)S(1)}, bf16[176,2048]{1,0:T(8,128)(2,1)S(1)}, u32[]{:S(2)}, u32[]{:S(2)}) collective-permute-start(bf16[176,2048]{1,0:T(8,128)(2,1)S(1)} %get-tuple-element.37), channel_id=1, source_target_pairs={{0,4},{1,5},{2,6},{3,7},{4,0},{5,1},{6,2},{7,3},{8,12},{9,13},{10,... | collective-permute-start | bytes 2162696 | tf_op jit(solution)/shard_map/ppermute | solution.py:63
  839.7 27.8 %collective-permute-done.97 = bf16[4,64,1408]{2,1,0:T(8,128)(2,1)S(1)} collective-permute-done((bf16[4,64,1408]{2,1,0:T(8,128)(2,1)S(1)}, bf16[4,64,1408]{2,1,0:T(8,128)(2,1)S(1)}, u32[]{:S(2)}, u32[]{:S(2)}) %collective-permute-start.97) | collective-permute-done | bytes 720928 | tf_op jit(solution)/shard_map/ppermute | solution.py:63
  870.1 57.2 %collective-permute-done.104 = bf16[176,2048]{1,0:T(8,128)(2,1)S(1)} collective-permute-done((bf16[176,2048]{1,0:T(8,128)(2,1)S(1)}, bf16[176,2048]{1,0:T(8,128)(2,1)S(1)}, u32[]{:S(2)}, u32[]{:S(2)}) %collective-permute-start.104) | collective-permute-done | bytes 720928 | tf_op jit(solution)/shard_map/ppermute | solution.py:63
  931.2 3.4 collective-permute-done.93
  939.1 3.3 collective-permute-done.100
  949.2 4.0 convolution_convert_fusion.8.do_ref
  953.2 22.8 %shard_map.222 = bf16[1024,640]{1,0:T(8,128)(2,1)S(1)} custom-call(bf16[1024,512]{1,0:T(8,128)(2,1)S(1)} %get-tuple-element.16.qr_ref, bf16[1024,128]{1,0:T(8,128)(2,1)S(1)} %get-tuple-element.17.kvr_ref, bf16[1024,512]{1,0:T(8,128)(2,1)S(1)} %convolution_convert_fusion.8.do_ref, f32[4,2,1024]{2,1,0:T(2,128)S(1)} %get-tuple-element.18.lse_ref, ...), custom_call_target="tpu_custom_call" | custom-call | flops 2684354560 | bytes 6291456 | tf_op jit(solution)/shard_map/pallas_call | solution.py:285
  976.0 3.7 convolution_convert_fusion.6
  984.9 3.9 convolution_convert_fusion.3
  989.1 22.7 %collective-permute-done.77 = bf16[4,4,64,640]{3,2,0,1:T(8,128)(2,1)S(1)} collective-permute-done((bf16[4,4,64,640]{3,2,0,1:T(8,128)(2,1)S(1)}, bf16[4,4,64,640]{3,2,0,1:T(8,128)(2,1)S(1)}, u32[]{:S(2)}, u32[]{:S(2)}) %collective-permute-start.77) | collective-permute-done | bytes 1310752 | tf_op jit(solution)/shard_map/ppermute | solution.py:63
  1014.4 19.3 %collective-permute-done.84 = bf16[4,64,2048]{2,1,0:T(8,128)(2,1)S(1)} collective-permute-done((bf16[4,64,2048]{2,1,0:T(8,128)(2,1)S(1)}, bf16[4,64,2048]{2,1,0:T(8,128)(2,1)S(1)}, u32[]{:S(2)}, u32[]{:S(2)}) %collective-permute-start.84) | collective-permute-done | bytes 1048608 | tf_op jit(solution)/shard_map/ppermute | solution.py:63
  1034.4 15.7 %collective-permute-done.79 = bf16[4,64,640]{2,1,0:T(8,128)(2,1)S(1)} collective-permute-done((bf16[4,64,640]{2,1,0:T(8,128)(2,1)S(1)}, bf16[4,64,640]{2,1,0:T(8,128)(2,1)S(1)}, u32[]{:S(2)}, u32[]{:S(2)}) %collective-permute-start.79) | collective-permute-done | bytes 327712 | tf_op jit(solution)/shard_map/ppermute | solution.py:63
  1050.5 11.9 %collective-permute-done.86 = bf16[64,2048]{1,0:T(8,128)(2,1)S(1)} collective-permute-done((bf16[64,2048]{1,0:T(8,128)(2,1)S(1)}, bf16[64,2048]{1,0:T(8,128)(2,1)S(1)}, u32[]{:S(2)}, u32[]{:S(2)}) %collective-permute-start.86) | collective-permute-done | bytes 262176 | tf_op jit(solution)/shard_map/ppermute | solution.py:63
  1064.2 4.1 collective-permute-done.82
  1078.1 14.7 %collective-permute-done.76 = bf16[256,2048]{1,0:T(8,128)(2,1)} collective-permute-done((bf16[256,2048]{1,0:T(8,128)(2,1)}, bf16[256,2048]{1,0:T(8,128)(2,1)}, u32[]{:S(2)}, u32[]{:S(2)}) %collective-permute-start.76) | collective-permute-done | bytes 1048608 | tf_op jit(solution)/shard_map/ppermute | solution.py:63
  (518 shorter events, 230.8 us)
Async XLA Ops:
  1.9 31.4 %collective-permute-start.3 = (bf16[2,64]{1,0:T(2,128)(2,1)}, bf16[2,64]{1,0:T(2,128)(2,1)}, u32[]{:S(2)}, u32[]{:S(2)}) collective-permute-start(bf16[2,64]{1,0:T(2,128)(2,1)} %pad_maximum_fusion.1), channel_id=1, source_target_pairs={{0,8},{8,0},{16,24},{24,16},{1,9},{9,1},{17,25},{25,17},{2,10},{10... | collective-permute-start | bytes 776 | tf_op jit(solution)/shard_map/ppermute | solution.py:63
  2.4 30.9 %collective-permute-start.4 = (bf16[2,64]{1,0:T(2,128)(2,1)}, bf16[2,64]{1,0:T(2,128)(2,1)S(1)}, u32[]{:S(2)}, u32[]{:S(2)}) collective-permute-start(bf16[2,64]{1,0:T(2,128)(2,1)} %pad_maximum_fusion.1), channel_id=1, source_target_pairs={{0,16},{8,24},{16,0},{24,8},{1,17},{9,25},{17,1},{25,9},{2,18},{10... | collective-permute-start | bytes 776 | tf_op jit(solution)/shard_map/ppermute | solution.py:63
  5.6 42.1 %collective-permute-start.23 = (s32[2,256]{1,0:T(2,128)S(1)}, s32[2,256]{1,0:T(2,128)}, u32[]{:S(2)}, u32[]{:S(2)}) collective-permute-start(s32[2,256]{1,0:T(2,128)S(1)} %get-tuple-element.87), channel_id=1, source_target_pairs={{0,8},{8,0},{16,24},{24,16},{1,9},{9,1},{17,25},{25,17},{2,10},{10... | collective-permute-start | bytes 6152 | tf_op jit(solution)/shard_map/ppermute | solution.py:63
  5.8 42.6 %collective-permute-start.24 = (s32[2,256]{1,0:T(2,128)S(1)}, s32[2,256]{1,0:T(2,128)S(1)}, u32[]{:S(2)}, u32[]{:S(2)}) collective-permute-start(s32[2,256]{1,0:T(2,128)S(1)} %get-tuple-element.87), channel_id=1, source_target_pairs={{0,16},{8,24},{16,0},{24,8},{1,17},{9,25},{17,1},{25,9},{2,18},{10... | collective-permute-start | bytes 6152 | tf_op jit(solution)/shard_map/ppermute | solution.py:63
  47.7 208.2 %collective-permute-start = (bf16[256,2048]{1,0:T(8,128)(2,1)S(1)}, bf16[256,2048]{1,0:T(8,128)(2,1)}, u32[]{:S(2)}, u32[]{:S(2)}) collective-permute-start(bf16[256,2048]{1,0:T(8,128)(2,1)S(1)} %bitcast.456), channel_id=1, source_target_pairs={{0,8},{8,0},{16,24},{24,16},{1,9},{9,1},{17,25},{25,17},{2,10},{10... | collective-permute-start | bytes 3145736 | tf_op jit(solution)/shard_map/ppermute | solution.py:63
  48.4 209.9 %collective-permute-start.1 = (bf16[256,2048]{1,0:T(8,128)(2,1)S(1)}, bf16[256,2048]{1,0:T(8,128)(2,1)}, u32[]{:S(2)}, u32[]{:S(2)}) collective-permute-start(bf16[256,2048]{1,0:T(8,128)(2,1)S(1)} %bitcast.457), channel_id=1, source_target_pairs={{0,16},{8,24},{16,0},{24,8},{1,17},{9,25},{17,1},{25,9},{2,18},{10... | collective-permute-start | bytes 3145736 | tf_op jit(solution)/shard_map/ppermute | solution.py:63
  50.1 66.0 %collective-permute-start.26 = (bf16[64,2048]{1,0:T(8,128)(2,1)}, bf16[64,2048]{1,0:T(8,128)(2,1)}, u32[]{:S(2)}, u32[]{:S(2)}) collective-permute-start(bf16[64,2048]{1,0:T(8,128)(2,1)} %param.23), channel_id=1, source_target_pairs={{0,1},{1,0},{2,3},{3,2},{4,5},{5,4},{6,7},{7,6},{8,9},{9,8},{10,11... | collective-permute-start | bytes 786440 | tf_op jit(solution)/shard_map/ppermute | solution.py:63
  51.6 66.8 %collective-permute-start.27 = (bf16[64,2048]{1,0:T(8,128)(2,1)}, bf16[64,2048]{1,0:T(8,128)(2,1)}, u32[]{:S(2)}, u32[]{:S(2)}) collective-permute-start(bf16[64,2048]{1,0:T(8,128)(2,1)} %param.23), channel_id=1, source_target_pairs={{0,2},{1,3},{2,4},{3,5},{4,6},{5,7},{6,0},{7,1},{8,10},{9,11},{10,... | collective-permute-start | bytes 786440 | tf_op jit(solution)/shard_map/ppermute | solution.py:63
  56.2 19.6 %collective-permute-start.14 = (bf16[1,64,640]{2,1,0:T(8,128)(2,1)}, bf16[1,64,640]{2,1,0:T(8,128)(2,1)S(1)}, u32[]{:S(2)}, u32[]{:S(2)}) collective-permute-start(bf16[1,64,640]{2,1,0:T(8,128)(2,1)} %get-tuple-element.77), channel_id=1, source_target_pairs={{0,16},{8,24},{16,0},{24,8},{1,17},{9,25},{17,1},{25,9},{2,18},{10... | collective-permute-start | bytes 245768 | tf_op jit(solution)/shard_map/ppermute | solution.py:63
  111.1 24.1 %collective-permute-start.29 = (bf16[64,2048]{1,0:T(8,128)(2,1)S(1)}, bf16[64,2048]{1,0:T(8,128)(2,1)S(1)}, u32[]{:S(2)}, u32[]{:S(2)}) collective-permute-start(bf16[64,2048]{1,0:T(8,128)(2,1)S(1)} %copy-done.47), channel_id=1, source_target_pairs={{0,4},{1,5},{2,6},{3,7},{4,0},{5,1},{6,2},{7,3},{8,12},{9,13},{10,... | collective-permute-start | bytes 786440 | tf_op jit(solution)/shard_map/ppermute | solution.py:63
  135.2 29.6 %collective-permute-start.58 = (bf16[176,2048]{1,0:T(8,128)(2,1)S(1)}, bf16[176,2048]{1,0:T(8,128)(2,1)S(1)}, u32[]{:S(2)}, u32[]{:S(2)}) collective-permute-start(bf16[176,2048]{1,0:T(8,128)(2,1)S(1)} %copy-done.42), channel_id=1, source_target_pairs={{0,1},{1,0},{2,3},{3,2},{4,5},{5,4},{6,7},{7,6},{8,9},{9,8},{10,11... | collective-permute-start | bytes 2162696 | tf_op jit(solution)/shard_map/ppermute | solution.py:63
  136.0 21.6 %collective-permute-start.30 = (bf16[64,2048]{1,0:T(8,128)(2,1)S(1)}, bf16[64,2048]{1,0:T(8,128)(2,1)S(1)}, u32[]{:S(2)}, u32[]{:S(2)}) collective-permute-start(bf16[64,2048]{1,0:T(8,128)(2,1)S(1)} %collective-permute-done.29), channel_id=1, source_target_pairs={{0,1},{1,0},{2,3},{3,2},{4,5},{5,4},{6,7},{7,6},{8,9},{9,8},{10,11... | collective-permute-start | bytes 786440 | tf_op jit(solution)/shard_map/ppermute | solution.py:63
  139.9 28.2 %collective-permute-start.59 = (bf16[176,2048]{1,0:T(8,128)(2,1)S(1)}, bf16[176,2048]{1,0:T(8,128)(2,1)S(1)}, u32[]{:S(2)}, u32[]{:S(2)}) collective-permute-start(bf16[176,2048]{1,0:T(8,128)(2,1)S(1)} %copy-done.42), channel_id=1, source_target_pairs={{0,2},{1,3},{2,4},{3,5},{4,6},{5,7},{6,0},{7,1},{8,10},{9,11},{10,... | collective-permute-start | bytes 2162696 | tf_op jit(solution)/shard_map/ppermute | solution.py:63
  164.0 99.5 %collective-permute-start.67 = (bf16[256,2048]{1,0:T(8,128)(2,1)S(1)}, bf16[256,2048]{1,0:T(8,128)(2,1)S(1)}, u32[]{:S(2)}, u32[]{:S(2)}) collective-permute-start(bf16[256,2048]{1,0:T(8,128)(2,1)S(1)} %copy-done.39), channel_id=1, source_target_pairs={{0,8},{8,0},{16,24},{24,16},{1,9},{9,1},{17,25},{25,17},{2,10},{10... | collective-permute-start | bytes 3145736 | tf_op jit(solution)/shard_map/ppermute | solution.py:63
  193.1 24.7 %collective-permute-start.51 = (bf16[4,64,1408]{2,1,0:T(8,128)(2,1)S(1)}, bf16[4,64,1408]{2,1,0:T(8,128)(2,1)S(1)}, u32[]{:S(2)}, u32[]{:S(2)}) collective-permute-start(bf16[4,64,1408]{2,1,0:T(8,128)(2,1)S(1)} %constant_dynamic-update-slice_fusion.9), channel_id=1, source_target_pairs={{0,1},{1,0},{2,3},{3,2},{4,5},{5,4},{6,7},{7,6},{8,9},{9,8},{10,11... | collective-permute-start | bytes 2162696 | tf_op jit(solution)/shard_map/ppermute | solution.py:63
  195.7 22.1 %collective-permute-start.22 = (bf16[4,64,640]{2,1,0:T(8,128)(2,1)S(1)}, bf16[4,64,640]{2,1,0:T(8,128)(2,1)S(1)}, u32[]{:S(2)}, u32[]{:S(2)}) collective-permute-start(bf16[4,64,640]{2,1,0:T(8,128)(2,1)S(1)} %collective-permute-done.21), channel_id=1, source_target_pairs={{0,1},{1,0},{2,3},{3,2},{4,5},{5,4},{6,7},{7,6},{8,9},{9,8},{10,11... | collective-permute-start | bytes 983048 | tf_op jit(solution)/shard_map/ppermute | solution.py:63
  217.9 19.8 %collective-permute-start.41 = (bf16[4,64,1408]{2,1,0:T(8,128)(2,1)}, bf16[4,64,1408]{2,1,0:T(8,128)(2,1)S(1)}, u32[]{:S(2)}, u32[]{:S(2)}) collective-permute-start(bf16[4,64,1408]{2,1,0:T(8,128)(2,1)} %constant_dynamic-update-slice_fusion.12), channel_id=1, source_target_pairs={{0,1},{1,0},{2,3},{3,2},{4,5},{5,4},{6,7},{7,6},{8,9},{9,8},{10,11... | collective-permute-start | bytes 2162696 | tf_op jit(solution)/shard_map/ppermute | solution.py:63
  237.7 27.6 %collective-permute-start.68 = (bf16[256,2048]{1,0:T(8,128)(2,1)S(1)}, bf16[256,2048]{1,0:T(8,128)(2,1)S(1)}, u32[]{:S(2)}, u32[]{:S(2)}) collective-permute-start(bf16[256,2048]{1,0:T(8,128)(2,1)S(1)} %copy-done.39), channel_id=1, source_target_pairs={{0,16},{8,24},{16,0},{24,8},{1,17},{9,25},{17,1},{25,9},{2,18},{10... | collective-permute-start | bytes 3145736 | tf_op jit(solution)/shard_map/ppermute | solution.py:63
  255.7 32.2 %collective-permute-start.61 = (bf16[176,2048]{1,0:T(8,128)(2,1)S(1)}, bf16[176,2048]{1,0:T(8,128)(2,1)S(1)}, u32[]{:S(2)}, u32[]{:S(2)}) collective-permute-start(bf16[176,2048]{1,0:T(8,128)(2,1)S(1)} %copy-done.42), channel_id=1, source_target_pairs={{0,4},{1,5},{2,6},{3,7},{4,0},{5,1},{6,2},{7,3},{8,12},{9,13},{10,... | collective-permute-start | bytes 2162696 | tf_op jit(solution)/shard_map/ppermute | solution.py:63
  255.8 34.5 %collective-permute-start.63 = (bf16[176,2048]{1,0:T(8,128)(2,1)S(1)}, bf16[176,2048]{1,0:T(8,128)(2,1)S(1)}, u32[]{:S(2)}, u32[]{:S(2)}) collective-permute-start(bf16[176,2048]{1,0:T(8,128)(2,1)S(1)} %copy-done.42), channel_id=1, source_target_pairs={{0,6},{1,7},{2,0},{3,1},{4,2},{5,3},{6,4},{7,5},{8,14},{9,15},{10,... | collective-permute-start | bytes 2162696 | tf_op jit(solution)/shard_map/ppermute | solution.py:63
  258.3 121.8 %collective-permute-start.54 = (bf16[4,64,1408]{2,1,0:T(8,128)(2,1)S(1)}, bf16[4,64,1408]{2,1,0:T(8,128)(2,1)}, u32[]{:S(2)}, u32[]{:S(2)}) collective-permute-start(bf16[4,64,1408]{2,1,0:T(8,128)(2,1)S(1)} %constant_dynamic-update-slice_fusion.9), channel_id=1, source_target_pairs={{0,4},{1,5},{2,6},{3,7},{4,0},{5,1},{6,2},{7,3},{8,12},{9,13},{10,... | collective-permute-start | bytes 2162696 | tf_op jit(solution)/shard_map/ppermute | solution.py:63
  263.5 27.4 %collective-permute-start.60 = (bf16[176,2048]{1,0:T(8,128)(2,1)S(1)}, bf16[176,2048]{1,0:T(8,128)(2,1)S(1)}, u32[]{:S(2)}, u32[]{:S(2)}) collective-permute-start(bf16[176,2048]{1,0:T(8,128)(2,1)S(1)} %collective-permute-done.59), channel_id=1, source_target_pairs={{0,1},{1,0},{2,3},{3,2},{4,5},{5,4},{6,7},{7,6},{8,9},{9,8},{10,11... | collective-permute-start | bytes 2162696 | tf_op jit(solution)/shard_map/ppermute | solution.py:63
  265.2 153.7 %collective-permute-start.56 = (bf16[4,64,1408]{2,1,0:T(8,128)(2,1)S(1)}, bf16[4,64,1408]{2,1,0:T(8,128)(2,1)}, u32[]{:S(2)}, u32[]{:S(2)}) collective-permute-start(bf16[4,64,1408]{2,1,0:T(8,128)(2,1)S(1)} %constant_dynamic-update-slice_fusion.9), channel_id=1, source_target_pairs={{0,6},{1,7},{2,0},{3,1},{4,2},{5,3},{6,4},{7,5},{8,14},{9,15},{10,... | collective-permute-start | bytes 2162696 | tf_op jit(solution)/shard_map/ppermute | solution.py:63
  287.9 131.6 %collective-permute-start.44 = (bf16[4,64,1408]{2,1,0:T(8,128)(2,1)}, bf16[4,64,1408]{2,1,0:T(8,128)(2,1)}, u32[]{:S(2)}, u32[]{:S(2)}) collective-permute-start(bf16[4,64,1408]{2,1,0:T(8,128)(2,1)} %constant_dynamic-update-slice_fusion.12), channel_id=1, source_target_pairs={{0,4},{1,5},{2,6},{3,7},{4,0},{5,1},{6,2},{7,3},{8,12},{9,13},{10,... | collective-permute-start | bytes 2162696 | tf_op jit(solution)/shard_map/ppermute | solution.py:63
  290.9 30.3 %collective-permute-start.64 = (bf16[176,2048]{1,0:T(8,128)(2,1)S(1)}, bf16[176,2048]{1,0:T(8,128)(2,1)S(1)}, u32[]{:S(2)}, u32[]{:S(2)}) collective-permute-start(bf16[176,2048]{1,0:T(8,128)(2,1)S(1)} %collective-permute-done.63), channel_id=1, source_target_pairs={{0,1},{1,0},{2,3},{3,2},{4,5},{5,4},{6,7},{7,6},{8,9},{9,8},{10,11... | collective-permute-start | bytes 2162696 | tf_op jit(solution)/shard_map/ppermute | solution.py:63
  309.4 71.2 %collective-permute-start.2 = (bf16[256,2048]{1,0:T(8,128)(2,1)}, bf16[256,2048]{1,0:T(8,128)(2,1)S(1)}, u32[]{:S(2)}, u32[]{:S(2)}) collective-permute-start(bf16[256,2048]{1,0:T(8,128)(2,1)} %collective-permute-done.1), channel_id=1, source_target_pairs={{0,8},{8,0},{16,24},{24,16},{1,9},{9,1},{17,25},{25,17},{2,10},{10... | collective-permute-start | bytes 3145736 | tf_op jit(solution)/shard_map/ppermute | solution.py:63
  321.2 99.8 %collective-permute-start.46 = (bf16[4,64,1408]{2,1,0:T(8,128)(2,1)}, bf16[4,64,1408]{2,1,0:T(8,128)(2,1)}, u32[]{:S(2)}, u32[]{:S(2)}) collective-permute-start(bf16[4,64,1408]{2,1,0:T(8,128)(2,1)} %constant_dynamic-update-slice_fusion.12), channel_id=1, source_target_pairs={{0,6},{1,7},{2,0},{3,1},{4,2},{5,3},{6,4},{7,5},{8,14},{9,15},{10,... | collective-permute-start | bytes 2162696 | tf_op jit(solution)/shard_map/ppermute | solution.py:63
  380.1 34.5 %collective-permute-start.53 = (bf16[4,64,1408]{2,1,0:T(8,128)(2,1)}, bf16[4,64,1408]{2,1,0:T(8,128)(2,1)}, u32[]{:S(2)}, u32[]{:S(2)}) collective-permute-start(bf16[4,64,1408]{2,1,0:T(8,128)(2,1)} %collective-permute-done.52), channel_id=1, source_target_pairs={{0,1},{1,0},{2,3},{3,2},{4,5},{5,4},{6,7},{7,6},{8,9},{9,8},{10,11... | collective-permute-start | bytes 2162696 | tf_op jit(solution)/shard_map/ppermute | solution.py:63
  380.7 40.9 %collective-permute-start.55 = (bf16[4,64,1408]{2,1,0:T(8,128)(2,1)}, bf16[4,64,1408]{2,1,0:T(8,128)(2,1)}, u32[]{:S(2)}, u32[]{:S(2)}) collective-permute-start(bf16[4,64,1408]{2,1,0:T(8,128)(2,1)} %collective-permute-done.54), channel_id=1, source_target_pairs={{0,1},{1,0},{2,3},{3,2},{4,5},{5,4},{6,7},{7,6},{8,9},{9,8},{10,11... | collective-permute-start | bytes 2162696 | tf_op jit(solution)/shard_map/ppermute | solution.py:63
  414.6 23.4 %collective-permute-start.33 = (bf16[2,256,2048]{2,1,0:T(8,128)(2,1)S(1)}, bf16[2,256,2048]{2,1,0:T(8,128)(2,1)S(1)}, u32[]{:S(2)}, u32[]{:S(2)}) collective-permute-start(bf16[2,256,2048]{2,1,0:T(8,128)(2,1)S(1)} %dynamic-slice_bitcast_fusion.4), channel_id=1, source_target_pairs={{0,8},{8,0},{16,24},{24,16},{1,9},{9,1},{17,25},{25,17},{2,10},{10... | collective-permute-start | bytes 6291464 | tf_op jit(solution)/shard_map/ppermute | solution.py:63
  419.5 53.5 %collective-permute-start.57 = (bf16[4,64,1408]{2,1,0:T(8,128)(2,1)}, bf16[4,64,1408]{2,1,0:T(8,128)(2,1)S(1)}, u32[]{:S(2)}, u32[]{:S(2)}) collective-permute-start(bf16[4,64,1408]{2,1,0:T(8,128)(2,1)} %collective-permute-done.56), channel_id=1, source_target_pairs={{0,1},{1,0},{2,3},{3,2},{4,5},{5,4},{6,7},{7,6},{8,9},{9,8},{10,11... | collective-permute-start | bytes 2162696 | tf_op jit(solution)/shard_map/ppermute | solution.py:63
  421.0 47.8 %collective-permute-start.45 = (bf16[4,64,1408]{2,1,0:T(8,128)(2,1)}, bf16[4,64,1408]{2,1,0:T(8,128)(2,1)S(1)}, u32[]{:S(2)}, u32[]{:S(2)}) collective-permute-start(bf16[4,64,1408]{2,1,0:T(8,128)(2,1)} %collective-permute-done.44), channel_id=1, source_target_pairs={{0,1},{1,0},{2,3},{3,2},{4,5},{5,4},{6,7},{7,6},{8,9},{9,8},{10,11... | collective-permute-start | bytes 2162696 | tf_op jit(solution)/shard_map/ppermute | solution.py:63
  421.5 62.2 %collective-permute-start.47 = (bf16[4,64,1408]{2,1,0:T(8,128)(2,1)}, bf16[4,64,1408]{2,1,0:T(8,128)(2,1)S(1)}, u32[]{:S(2)}, u32[]{:S(2)}) collective-permute-start(bf16[4,64,1408]{2,1,0:T(8,128)(2,1)} %collective-permute-done.46), channel_id=1, source_target_pairs={{0,1},{1,0},{2,3},{3,2},{4,5},{5,4},{6,7},{7,6},{8,9},{9,8},{10,11... | collective-permute-start | bytes 2162696 | tf_op jit(solution)/shard_map/ppermute | solution.py:63
  437.9 45.9 %collective-permute-start.69 = (bf16[256,2048]{1,0:T(8,128)(2,1)S(1)}, bf16[256,2048]{1,0:T(8,128)(2,1)S(1)}, u32[]{:S(2)}, u32[]{:S(2)}) collective-permute-start(bf16[256,2048]{1,0:T(8,128)(2,1)S(1)} %copy-done.38), channel_id=1, source_target_pairs={{0,8},{8,0},{16,24},{24,16},{1,9},{9,1},{17,25},{25,17},{2,10},{10... | collective-permute-start | bytes 3145736 | tf_op jit(solution)/shard_map/ppermute | solution.py:63
  439.0 31.2 %collective-permute-start.34 = (bf16[256,2048]{1,0:T(8,128)(2,1)S(1)}, bf16[256,2048]{1,0:T(8,128)(2,1)S(1)}, u32[]{:S(2)}, u32[]{:S(2)}) collective-permute-start(bf16[256,2048]{1,0:T(8,128)(2,1)S(1)} %dynamic-slice_bitcast_fusion.9), channel_id=1, source_target_pairs={{0,16},{8,24},{16,0},{24,8},{1,17},{9,25},{17,1},{25,9},{2,18},{10... | collective-permute-start | bytes 3145736 | tf_op jit(solution)/shard_map/ppermute | solution.py:63
  472.1 24.1 %collective-permute-start.36 = (bf16[256,2048]{1,0:T(8,128)(2,1)S(1)}, bf16[256,2048]{1,0:T(8,128)(2,1)S(1)}, u32[]{:S(2)}, u32[]{:S(2)}) collective-permute-start(bf16[256,2048]{1,0:T(8,128)(2,1)S(1)} %get-tuple-element.25), channel_id=1, source_target_pairs={{0,16},{8,24},{16,0},{24,8},{1,17},{9,25},{17,1},{25,9},{2,18},{10... | collective-permute-start | bytes 3145736 | tf_op jit(solution)/shard_map/ppermute | solution.py:63
  484.0 23.2 %collective-permute-start.35 = (bf16[256,2048]{1,0:T(8,128)(2,1)S(1)}, bf16[256,2048]{1,0:T(8,128)(2,1)S(1)}, u32[]{:S(2)}, u32[]{:S(2)}) collective-permute-start(bf16[256,2048]{1,0:T(8,128)(2,1)S(1)} %get-tuple-element.25), channel_id=1, source_target_pairs={{0,8},{8,0},{16,24},{24,16},{1,9},{9,1},{17,25},{25,17},{2,10},{10... | collective-permute-start | bytes 3145736 | tf_op jit(solution)/shard_map/ppermute | solution.py:63
  568.6 45.9 %collective-permute-start.70 = (bf16[2,256,2048]{2,1,0:T(8,128)(2,1)}, bf16[2,256,2048]{2,1,0:T(8,128)(2,1)}, u32[]{:S(2)}, u32[]{:S(2)}) collective-permute-start(bf16[2,256,2048]{2,1,0:T(8,128)(2,1)} %dynamic-slice_bitcast_fusion.2), channel_id=1, source_target_pairs={{0,8},{8,0},{16,24},{24,16},{1,9},{9,1},{17,25},{25,17},{2,10},{10... | collective-permute-start | bytes 6291464 | tf_op jit(solution)/shard_map/ppermute | solution.py:63
  583.2 35.8 %collective-permute-start.65 = (bf16[2,256,2048]{2,1,0:T(8,128)(2,1)}, bf16[2,256,2048]{2,1,0:T(8,128)(2,1)}, u32[]{:S(2)}, u32[]{:S(2)}) collective-permute-start(bf16[2,256,2048]{2,1,0:T(8,128)(2,1)} %dynamic-slice_bitcast_fusion.3), channel_id=1, source_target_pairs={{0,8},{8,0},{16,24},{24,16},{1,9},{9,1},{17,25},{25,17},{2,10},{10... | collective-permute-start | bytes 6291464 | tf_op jit(solution)/shard_map/ppermute | solution.py:63
  596.5 65.7 %collective-permute-start.88 = (bf16[4,4,64,1408]{3,2,0,1:T(8,128)(2,1)}, bf16[4,4,64,1408]{3,2,0,1:T(8,128)(2,1)}, u32[]{:S(2)}, u32[]{:S(2)}) collective-permute-start(bf16[4,4,64,1408]{3,2,0,1:T(8,128)(2,1)} %bitcast.442), channel_id=1, source_target_pairs={{0,1},{1,0},{2,3},{3,2},{4,5},{5,4},{6,7},{7,6},{8,9},{9,8},{10,11... | collective-permute-start | bytes 8650760 | tf_op jit(solution)/shard_map/ppermute | solution.py:63
  607.3 116.7 %collective-permute-start.102 = (bf16[4,176,2048]{2,1,0:T(8,128)(2,1)}, bf16[4,176,2048]{2,1,0:T(8,128)(2,1)}, u32[]{:S(2)}, u32[]{:S(2)}) collective-permute-start(bf16[4,176,2048]{2,1,0:T(8,128)(2,1)} %dynamic-slice_bitcast_fusion), channel_id=1, source_target_pairs={{0,1},{1,0},{2,3},{3,2},{4,5},{5,4},{6,7},{7,6},{8,9},{9,8},{10,11... | collective-permute-start | bytes 8650760 | tf_op jit(solution)/shard_map/ppermute | solution.py:63
  614.0 170.7 %collective-permute-start.95 = (bf16[4,4,64,1408]{3,2,0,1:T(8,128)(2,1)}, bf16[4,4,64,1408]{3,2,0,1:T(8,128)(2,1)S(1)}, u32[]{:S(2)}, u32[]{:S(2)}) collective-permute-start(bf16[4,4,64,1408]{3,2,0,1:T(8,128)(2,1)} %bitcast.441), channel_id=1, source_target_pairs={{0,1},{1,0},{2,3},{3,2},{4,5},{5,4},{6,7},{7,6},{8,9},{9,8},{10,11... | collective-permute-start | bytes 8650760 | tf_op jit(solution)/shard_map/ppermute | solution.py:63
  618.1 169.0 %collective-permute-start.71 = (bf16[256,2048]{1,0:T(8,128)(2,1)S(1)}, bf16[256,2048]{1,0:T(8,128)(2,1)S(1)}, u32[]{:S(2)}, u32[]{:S(2)}) collective-permute-start(bf16[256,2048]{1,0:T(8,128)(2,1)S(1)} %dynamic-slice_bitcast_fusion.7), channel_id=1, source_target_pairs={{0,16},{8,24},{16,0},{24,8},{1,17},{9,25},{17,1},{25,9},{2,18},{10... | collective-permute-start | bytes 3145736 | tf_op jit(solution)/shard_map/ppermute | solution.py:63
  621.5 169.2 %collective-permute-start.66 = (bf16[256,2048]{1,0:T(8,128)(2,1)S(1)}, bf16[256,2048]{1,0:T(8,128)(2,1)S(1)}, u32[]{:S(2)}, u32[]{:S(2)}) collective-permute-start(bf16[256,2048]{1,0:T(8,128)(2,1)S(1)} %dynamic-slice_bitcast_fusion.8), channel_id=1, source_target_pairs={{0,16},{8,24},{16,0},{24,8},{1,17},{9,25},{17,1},{25,9},{2,18},{10... | collective-permute-start | bytes 3145736 | tf_op jit(solution)/shard_map/ppermute | solution.py:63
  666.1 130.4 %collective-permute-start.91 = (bf16[4,64,1408]{2,1,0:T(8,128)(2,1)}, bf16[4,64,1408]{2,1,0:T(8,128)(2,1)}, u32[]{:S(2)}, u32[]{:S(2)}) collective-permute-start(bf16[4,64,1408]{2,1,0:T(8,128)(2,1)} %get-tuple-element.42), channel_id=1, source_target_pairs={{0,6},{1,7},{2,0},{3,1},{4,2},{5,3},{6,4},{7,5},{8,14},{9,15},{10,... | collective-permute-start | bytes 2162696 | tf_op jit(solution)/shard_map/ppermute | solution.py:63
  723.9 73.0 %collective-permute-start.90 = (bf16[4,64,1408]{2,1,0:T(8,128)(2,1)}, bf16[4,64,1408]{2,1,0:T(8,128)(2,1)}, u32[]{:S(2)}, u32[]{:S(2)}) collective-permute-start(bf16[4,64,1408]{2,1,0:T(8,128)(2,1)} %get-tuple-element.43), channel_id=1, source_target_pairs={{0,4},{1,5},{2,6},{3,7},{4,0},{5,1},{6,2},{7,3},{8,12},{9,13},{10,... | collective-permute-start | bytes 2162696 | tf_op jit(solution)/shard_map/ppermute | solution.py:63
  784.7 21.0 %collective-permute-start.89 = (bf16[4,64,1408]{2,1,0:T(8,128)(2,1)S(1)}, bf16[4,64,1408]{2,1,0:T(8,128)(2,1)}, u32[]{:S(2)}, u32[]{:S(2)}) collective-permute-start(bf16[4,64,1408]{2,1,0:T(8,128)(2,1)S(1)} %get-tuple-element.41), channel_id=1, source_target_pairs={{0,2},{1,3},{2,4},{3,5},{4,6},{5,7},{6,0},{7,1},{8,10},{9,11},{10,... | collective-permute-start | bytes 2162696 | tf_op jit(solution)/shard_map/ppermute | solution.py:63
  787.1 51.5 %collective-permute-start.98 = (bf16[4,64,1408]{2,1,0:T(8,128)(2,1)}, bf16[4,64,1408]{2,1,0:T(8,128)(2,1)S(1)}, u32[]{:S(2)}, u32[]{:S(2)}) collective-permute-start(bf16[4,64,1408]{2,1,0:T(8,128)(2,1)} %get-tuple-element.39), channel_id=1, source_target_pairs={{0,6},{1,7},{2,0},{3,1},{4,2},{5,3},{6,4},{7,5},{8,14},{9,15},{10,... | collective-permute-start | bytes 2162696 | tf_op jit(solution)/shard_map/ppermute | solution.py:63
  790.8 76.7 %collective-permute-start.97 = (bf16[4,64,1408]{2,1,0:T(8,128)(2,1)S(1)}, bf16[4,64,1408]{2,1,0:T(8,128)(2,1)S(1)}, u32[]{:S(2)}, u32[]{:S(2)}) collective-permute-start(bf16[4,64,1408]{2,1,0:T(8,128)(2,1)S(1)} %get-tuple-element.40), channel_id=1, source_target_pairs={{0,4},{1,5},{2,6},{3,7},{4,0},{5,1},{6,2},{7,3},{8,12},{9,13},{10,... | collective-permute-start | bytes 2162696 | tf_op jit(solution)/shard_map/ppermute | solution.py:63
  796.5 71.0 %collective-permute-start.96 = (bf16[4,64,1408]{2,1,0:T(8,128)(2,1)S(1)}, bf16[4,64,1408]{2,1,0:T(8,128)(2,1)S(1)}, u32[]{:S(2)}, u32[]{:S(2)}) collective-permute-start(bf16[4,64,1408]{2,1,0:T(8,128)(2,1)S(1)} %get-tuple-element.38), channel_id=1, source_target_pairs={{0,2},{1,3},{2,4},{3,5},{4,6},{5,7},{6,0},{7,1},{8,10},{9,11},{10,... | collective-permute-start | bytes 2162696 | tf_op jit(solution)/shard_map/ppermute | solution.py:63
  796.9 72.9 %collective-permute-start.105 = (bf16[176,2048]{1,0:T(8,128)(2,1)S(1)}, bf16[176,2048]{1,0:T(8,128)(2,1)S(1)}, u32[]{:S(2)}, u32[]{:S(2)}) collective-permute-start(bf16[176,2048]{1,0:T(8,128)(2,1)S(1)} %get-tuple-element.36), channel_id=1, source_target_pairs={{0,6},{1,7},{2,0},{3,1},{4,2},{5,3},{6,4},{7,5},{8,14},{9,15},{10,... | collective-permute-start | bytes 2162696 | tf_op jit(solution)/shard_map/ppermute | solution.py:63
  805.7 121.6 %collective-permute-start.104 = (bf16[176,2048]{1,0:T(8,128)(2,1)S(1)}, bf16[176,2048]{1,0:T(8,128)(2,1)S(1)}, u32[]{:S(2)}, u32[]{:S(2)}) collective-permute-start(bf16[176,2048]{1,0:T(8,128)(2,1)S(1)} %get-tuple-element.37), channel_id=1, source_target_pairs={{0,4},{1,5},{2,6},{3,7},{4,0},{5,1},{6,2},{7,3},{8,12},{9,13},{10,... | collective-permute-start | bytes 2162696 | tf_op jit(solution)/shard_map/ppermute | solution.py:63
  839.5 88.6 %collective-permute-start.103 = (bf16[176,2048]{1,0:T(8,128)(2,1)S(1)}, bf16[176,2048]{1,0:T(8,128)(2,1)S(1)}, u32[]{:S(2)}, u32[]{:S(2)}) collective-permute-start(bf16[176,2048]{1,0:T(8,128)(2,1)S(1)} %get-tuple-element.35), channel_id=1, source_target_pairs={{0,2},{1,3},{2,4},{3,5},{4,6},{5,7},{6,0},{7,1},{8,10},{9,11},{10,... | collective-permute-start | bytes 2162696 | tf_op jit(solution)/shard_map/ppermute | solution.py:63
  867.4 79.9 %collective-permute-start.72 = (bf16[256,2048]{1,0:T(8,128)(2,1)S(1)}, bf16[256,2048]{1,0:T(8,128)(2,1)S(1)}, u32[]{:S(2)}, u32[]{:S(2)}) collective-permute-start(bf16[256,2048]{1,0:T(8,128)(2,1)S(1)} %get-tuple-element.22), channel_id=1, source_target_pairs={{0,8},{8,0},{16,24},{24,16},{1,9},{9,1},{17,25},{25,17},{2,10},{10... | collective-permute-start | bytes 3145736 | tf_op jit(solution)/shard_map/ppermute | solution.py:63
  867.5 78.5 %collective-permute-start.73 = (bf16[256,2048]{1,0:T(8,128)(2,1)S(1)}, bf16[256,2048]{1,0:T(8,128)(2,1)S(1)}, u32[]{:S(2)}, u32[]{:S(2)}) collective-permute-start(bf16[256,2048]{1,0:T(8,128)(2,1)S(1)} %get-tuple-element.22), channel_id=1, source_target_pairs={{0,16},{8,24},{16,0},{24,8},{1,17},{9,25},{17,1},{25,9},{2,18},{10... | collective-permute-start | bytes 3145736 | tf_op jit(solution)/shard_map/ppermute | solution.py:63
  869.8 60.6 %collective-permute-start.92 = (bf16[1,64,1408]{2,1,0:T(8,128)(2,1)S(1)}, bf16[1,64,1408]{2,1,0:T(8,128)(2,1)S(1)}, u32[]{:S(2)}, u32[]{:S(2)}) collective-permute-start(bf16[1,64,1408]{2,1,0:T(8,128)(2,1)S(1)} %get-tuple-element.60), channel_id=1, source_target_pairs={{0,8},{8,0},{16,24},{24,16},{1,9},{9,1},{17,25},{25,17},{2,10},{10... | collective-permute-start | bytes 540680 | tf_op jit(solution)/shard_map/ppermute | solution.py:63
  980.2 31.7 %collective-permute-start.77 = (bf16[4,4,64,640]{3,2,0,1:T(8,128)(2,1)S(1)}, bf16[4,4,64,640]{3,2,0,1:T(8,128)(2,1)S(1)}, u32[]{:S(2)}, u32[]{:S(2)}) collective-permute-start(bf16[4,4,64,640]{3,2,0,1:T(8,128)(2,1)S(1)} %bitcast.496), channel_id=1, source_target_pairs={{0,1},{1,0},{2,3},{3,2},{4,5},{5,4},{6,7},{7,6},{8,9},{9,8},{10,11... | collective-permute-start | bytes 3932168 | tf_op jit(solution)/shard_map/ppermute | solution.py:63
  983.5 50.3 %collective-permute-start.84 = (bf16[4,64,2048]{2,1,0:T(8,128)(2,1)S(1)}, bf16[4,64,2048]{2,1,0:T(8,128)(2,1)S(1)}, u32[]{:S(2)}, u32[]{:S(2)}) collective-permute-start(bf16[4,64,2048]{2,1,0:T(8,128)(2,1)S(1)} %dynamic-slice_bitcast_fusion.5), channel_id=1, source_target_pairs={{0,1},{1,0},{2,3},{3,2},{4,5},{5,4},{6,7},{7,6},{8,9},{9,8},{10,11... | collective-permute-start | bytes 3145736 | tf_op jit(solution)/shard_map/ppermute | solution.py:63
  989.0 79.3 %collective-permute-start.75 = (bf16[2,256,2048]{2,1,0:T(8,128)(2,1)S(1)}, bf16[2,256,2048]{2,1,0:T(8,128)(2,1)S(1)}, u32[]{:S(2)}, u32[]{:S(2)}) collective-permute-start(bf16[2,256,2048]{2,1,0:T(8,128)(2,1)S(1)} %dynamic-slice_bitcast_fusion.1), channel_id=1, source_target_pairs={{0,8},{8,0},{16,24},{24,16},{1,9},{9,1},{17,25},{25,17},{2,10},{10... | collective-permute-start | bytes 6291464 | tf_op jit(solution)/shard_map/ppermute | solution.py:63
  1012.3 22.0 %collective-permute-start.80 = (bf16[4,64,640]{2,1,0:T(8,128)(2,1)S(1)}, bf16[4,64,640]{2,1,0:T(8,128)(2,1)S(1)}, u32[]{:S(2)}, u32[]{:S(2)}) collective-permute-start(bf16[4,64,640]{2,1,0:T(8,128)(2,1)S(1)} %get-tuple-element.49), channel_id=1, source_target_pairs={{0,6},{1,7},{2,0},{3,1},{4,2},{5,3},{6,4},{7,5},{8,14},{9,15},{10,... | collective-permute-start | bytes 983048 | tf_op jit(solution)/shard_map/ppermute | solution.py:63
  1012.4 37.7 %collective-permute-start.79 = (bf16[4,64,640]{2,1,0:T(8,128)(2,1)S(1)}, bf16[4,64,640]{2,1,0:T(8,128)(2,1)S(1)}, u32[]{:S(2)}, u32[]{:S(2)}) collective-permute-start(bf16[4,64,640]{2,1,0:T(8,128)(2,1)S(1)} %get-tuple-element.50), channel_id=1, source_target_pairs={{0,4},{1,5},{2,6},{3,7},{4,0},{5,1},{6,2},{7,3},{8,12},{9,13},{10,... | collective-permute-start | bytes 983048 | tf_op jit(solution)/shard_map/ppermute | solution.py:63
  1012.5 37.6 %collective-permute-start.78 = (bf16[4,64,640]{2,1,0:T(8,128)(2,1)S(1)}, bf16[4,64,640]{2,1,0:T(8,128)(2,1)S(1)}, u32[]{:S(2)}, u32[]{:S(2)}) collective-permute-start(bf16[4,64,640]{2,1,0:T(8,128)(2,1)S(1)} %get-tuple-element.48), channel_id=1, source_target_pairs={{0,2},{1,3},{2,4},{3,5},{4,6},{5,7},{6,0},{7,1},{8,10},{9,11},{10,... | collective-permute-start | bytes 983048 | tf_op jit(solution)/shard_map/ppermute | solution.py:63
  1034.3 28.1 %collective-permute-start.86 = (bf16[64,2048]{1,0:T(8,128)(2,1)S(1)}, bf16[64,2048]{1,0:T(8,128)(2,1)S(1)}, u32[]{:S(2)}, u32[]{:S(2)}) collective-permute-start(bf16[64,2048]{1,0:T(8,128)(2,1)S(1)} %get-tuple-element.53), channel_id=1, source_target_pairs={{0,4},{1,5},{2,6},{3,7},{4,0},{5,1},{6,2},{7,3},{8,12},{9,13},{10,... | collective-permute-start | bytes 786440 | tf_op jit(solution)/shard_map/ppermute | solution.py:63
  1070.2 22.5 %collective-permute-start.76 = (bf16[256,2048]{1,0:T(8,128)(2,1)}, bf16[256,2048]{1,0:T(8,128)(2,1)}, u32[]{:S(2)}, u32[]{:S(2)}) collective-permute-start(bf16[256,2048]{1,0:T(8,128)(2,1)} %dynamic-slice_bitcast_fusion.6), channel_id=1, source_target_pairs={{0,16},{8,24},{16,0},{24,8},{1,17},{9,25},{17,1},{25,9},{2,18},{10... | collective-permute-start | bytes 3145736 | tf_op jit(solution)/shard_map/ppermute | solution.py:63
  (104 other events, 1237.3 us)

commit v2 on v1

--- a/solution.py
+++ b/solution.py
@@ -133,50 +133,6 @@
         query_pos = lax.broadcasted_iota(jnp.int32, (rows, length), 1)
         allowed = (keys == queries) & (key_pos <= query_pos)
         bias_ref[start : start + rows, :] = jnp.where(allowed, 0.0, MASKED_SCORE)
-
-
-def attend_kernel(
-    qblock,
-    q_ref,
-    kv_ref,
-    cos_ref,
-    sin_ref,
-    seg_row_ref,
-    seg_col_ref,
-    o_ref,
-    qr_ref,
-    kvr_ref,
-    lse_ref,
-    bias_ref,
-):
-    length = q_ref.shape[0]
-    cosine = cos_ref[...]
-    sine = sin_ref[...]
-
-    @pl.when(pl.program_id(0) == 0)
-    def _():
-        mask_bias(bias_ref, seg_row_ref, seg_col_ref, length)
-        kv = kv_ref[...]
-        rotated = kv * cosine + rotate_lanes(kv, 1.0) * sine
-        lane = lax.broadcasted_iota(jnp.int32, kv.shape, 1)
-        kvr_ref[...] = jnp.where(lane < HEAD_DIM, rotated, kv).astype(BF16)
-
-    q = q_ref[...]
-    qr_ref[...] = (q * cosine + rotate_lanes(q, 1.0) * sine).astype(BF16)
-    for start in range(0, length, qblock):
-        stop = start + qblock
-        keys = kvr_ref[:stop, :HEAD_DIM]
-        values = kvr_ref[:stop, HEAD_DIM:]
-        for head in range(2):
-            lanes = slice(head * HEAD_DIM, (head + 1) * HEAD_DIM)
-            queries = qr_ref[start:stop, lanes] * SCALE
-            scores = product_cols(keys, queries.astype(BF16)) + bias_ref[:stop, start:stop]
-            top = jnp.max(scores, axis=0, keepdims=True)
-            grown = jnp.exp(scores - top)
-            total = jnp.sum(grown, axis=0, keepdims=True)
-            probs = (grown * (1.0 / total)).astype(BF16)
-            lse_ref[0, head : head + 1, start:stop] = top + jnp.log(total)
-            o_ref[start:stop, lanes] = product_rows(probs, values).astype(BF16)
 
 
 def attend_back_kernel(
@@ -239,43 +195,6 @@
 
 def whole_spec(shape):
     return pl.BlockSpec(shape, lambda j: (0,) * len(shape))
-
-
-def attend(qkv, cosine, sine, seg_row, seg_col):
-    length, width = qkv.shape
-    pairs = width // 128 - 1
-    qblock = min(256, length)
-    return pl.pallas_call(
-        functools.partial(attend_kernel, qblock),
-        grid=(pairs,),
-        in_specs=[
-            pl.BlockSpec((length, 128), lambda j: (0, j)),
-            pl.BlockSpec((length, 128), lambda j: (0, pairs)),
-            whole_spec((length, 128)),
-            whole_spec((length, 128)),
-            whole_spec((1, length)),
-            whole_spec((length, 1)),
-        ],
-        out_specs=[
-            pl.BlockSpec((length, 128), lambda j: (0, j)),
-            pl.BlockSpec((length, 128), lambda j: (0, j)),
-            whole_spec((length, 128)),
-            pl.BlockSpec((1, 2, length), lambda j: (j, 0, 0)),
-        ],
-        out_shape=[
-            jax.ShapeDtypeStruct((length, pairs * 128), BF16),
-            jax.ShapeDtypeStruct((length, pairs * 128), BF16),
-            jax.ShapeDtypeStruct((length, 128), BF16),
-            jax.ShapeDtypeStruct((pairs, 2, length), F32),
-        ],
-        scratch_shapes=[pltpu.VMEM((length, length), F32)],
-        compiler_params=pltpu.CompilerParams(vmem_limit_bytes=48 * 1024 * 1024),
-        cost_estimate=pl.CostEstimate(
-            flops=pairs * 2 * length * length * HEAD_DIM * 2,
-            bytes_accessed=8 * length * width,
-            transcendentals=pairs * length * length,
-        ),
-    )(qkv, qkv, cosine, sine, seg_row, seg_col)
 
 
 def attend_back(qr, kvr, grads, lse, cosine, sine, seg_row, seg_col):
@@ -312,6 +231,430 @@
     )(qr, kvr, grads, lse, cosine, sine, seg_row, seg_col)
 
 
+MESH = pl.DeviceIdType.MESH
+
+
+class Place:
+    def __init__(self, sizes):
+        self.ny, self.nc, self.nz, self.nx = sizes
+        self.s = lax.axis_index("seq")
+        self.b = lax.axis_index("batch")
+        self.y, self.c = self.s // self.nc, self.s % self.nc
+        self.z, self.x = self.b // self.nx, self.b % self.nx
+
+    def seq_at(self, dy, dc):
+        return (self.y + dy + self.ny) % self.ny * self.nc + (self.c + dc + self.nc) % self.nc
+
+    def batch_at(self, dz, dx):
+        return (self.z + dz + self.nz) % self.nz * self.nx + (self.x + dx + self.nx) % self.nx
+
+
+class Wires:
+    def __init__(self, send_sems, recv_sems):
+        self.send_sems, self.recv_sems = send_sems, recv_sems
+        self.started = []
+        self.count = 0
+
+    def push(self, source, target, device):
+        index = self.count
+        self.count += 1
+        copy = pltpu.make_async_remote_copy(
+            src_ref=source,
+            dst_ref=target,
+            send_sem=self.send_sems.at[index],
+            recv_sem=self.recv_sems.at[index],
+            device_id=device,
+            device_id_type=MESH,
+        )
+        copy.start()
+        self.started.append(copy)
+        return index, device
+
+    def wait(self, ticket, landed):
+        index, device = ticket
+        pltpu.make_async_remote_copy(
+            src_ref=landed,
+            dst_ref=landed,
+            send_sem=self.send_sems.at[index],
+            recv_sem=self.recv_sems.at[index],
+            device_id=device,
+            device_id_type=MESH,
+        ).wait_recv()
+
+    def close(self):
+        for copy in self.started:
+            copy.wait_send()
+
+
+class Gather:
+    def __init__(self, wires, slot, own, outer, inner, at, device):
+        self.wires, self.slot, self.own = wires, slot, own
+        self.outer, self.inner, self.at, self.device = outer, inner, at, device
+        self.first, self.second = {}, {}
+
+    def start(self):
+        mine = self.at(0, 0)
+        for k in range(1, self.outer):
+            self.first[k] = self.wires.push(self.own, self.slot(mine), self.device(self.at(k, 0)))
+        for m in range(1, self.inner):
+            self.second[0, m] = self.wires.push(
+                self.own, self.slot(mine), self.device(self.at(0, m))
+            )
+
+    def pass_on(self, k):
+        came = self.slot(self.at(-k, 0))
+        self.wires.wait(self.first[k], came)
+        for m in range(1, self.inner):
+            self.second[k, m] = self.wires.push(came, came, self.device(self.at(0, m)))
+
+    def finish(self):
+        for (k, m), ticket in self.second.items():
+            self.wires.wait(ticket, self.slot(self.at(-k, -m)))
+
+
+def enter(place):
+    peers = [
+        (place.seq_at(dy, dc), place.b)
+        for dy in range(place.ny)
+        for dc in range(place.nc)
+        if (dy, dc) != (0, 0)
+    ]
+    peers += [(place.s, place.batch_at(k, 0)) for k in range(1, place.nz)]
+    peers += [(place.s, place.batch_at(0, m)) for m in range(1, place.nx)]
+    barrier = pltpu.get_barrier_semaphore()
+    for peer in peers:
+        pl.semaphore_signal(barrier, inc=1, device_id=peer, device_id_type=MESH)
+    pl.semaphore_wait(barrier, len(peers))
+
+
+def front_kernel(
+    sizes,
+    pairs,
+    x_ref,
+    gb_ref,
+    table_ref,
+    gain_ref,
+    qkv_ref,
+    out_ref,
+    gate_ref,
+    up_ref,
+    down_ref,
+    wqkv_ref,
+    wo_ref,
+    wg_ref,
+    wu_ref,
+    wd_ref,
+    gb_all_ref,
+    n1_ref,
+    n2_ref,
+    residual_ref,
+    heads_ref,
+    qr_ref,
+    kvr_ref,
+    lse_ref,
+    tables_ref,
+    gains_ref,
+    x_all_ref,
+    table_all_ref,
+    gain_all_ref,
+    qkv_proj_ref,
+    bias_ref,
+    part_ref,
+    core_in_ref,
+    far_in_ref,
+    n2_own_ref,
+    send_sems,
+    recv_sems,
+    copy_sems,
+):
+    place = Place(sizes)
+    ny, nc, nz, nx = sizes
+    s, b = place.s, place.b
+    n_seq, n_batch = ny * nc, nz * nx
+    length, width = x_ref.shape
+    total_len = n_seq * length
+    wires = Wires(send_sems, recv_sems)
+    copies = []
+
+    def local(source, target):
+        copy = pltpu.make_async_copy(source, target, copy_sems.at[len(copies)])
+        copy.start()
+        copies.append(copy)
+        return copy
+
+    def over_batch(slot, own):
+        return Gather(wires, slot, own, nz, nx, place.batch_at, lambda j: (s, j))
+
+    def over_seq(slot, own):
+        return Gather(wires, slot, own, ny, nc, place.seq_at, lambda j: (j, b))
+
+    def columns(ref):
+        return lambda j: ref.at[:, j]
+
+    def blocks(ref):
+        return lambda j: ref.at[j]
+
+    class Exchange:
+        def __init__(self, parts, target, many=True):
+            self.target = target
+            part = (lambda j: parts.at[j]) if many else (lambda j: parts)
+            self.copy = local(part(s), target.at[s, b])
+            self.tickets = {}
+            for dy in range(ny):
+                for dc in range(nc):
+                    if (dy, dc) != (0, 0):
+                        j = place.seq_at(dy, dc)
+                        self.tickets[dy, dc] = wires.push(part(j), target.at[s, b], (j, b))
+
+        def finish(self):
+            self.copy.wait()
+            for (dy, dc), ticket in self.tickets.items():
+                wires.wait(ticket, self.target.at[place.seq_at(-dy, -dc), b])
+
+    enter(place)
+    qkv_parts = Exchange(qkv_ref, wqkv_ref)
+    gain_parts = Exchange(gain_ref, gain_all_ref, many=False)
+    own_table = local(table_ref, table_all_ref.at[s])
+    own_x = local(x_ref, x_all_ref.at[s])
+    own_out = local(out_ref, wo_ref.at[b])
+    own_down = local(down_ref, wd_ref.at[b])
+    own_gb = local(gb_ref, gb_all_ref.at[s])
+    table_all = over_seq(blocks(table_all_ref), table_ref)
+    table_all.start()
+    x_all = over_seq(blocks(x_all_ref), x_ref)
+    x_all.start()
+    wo = over_batch(blocks(wo_ref), out_ref)
+    wo.start()
+    gate_parts = Exchange(gate_ref, wg_ref)
+    up_parts = Exchange(up_ref, wu_ref)
+    wqkv = over_batch(columns(wqkv_ref), wqkv_ref.at[:, b])
+    gains = over_batch(columns(gain_all_ref), gain_all_ref.at[:, b])
+    wg = over_batch(columns(wg_ref), wg_ref.at[:, b])
+    wu = over_batch(columns(wu_ref), wu_ref.at[:, b])
+    wd = over_batch(blocks(wd_ref), down_ref)
+    gb_all = over_seq(blocks(gb_all_ref), gb_ref)
+
+    qkv_parts.finish()
+    wqkv.start()
+    gain_parts.finish()
+    gains.start()
+    for k in range(1, ny):
+        table_all.pass_on(k)
+        x_all.pass_on(k)
+    for k in range(1, nz):
+        wo.pass_on(k)
+        gains.pass_on(k)
+    for k in range(1, nz):
+        wqkv.pass_on(k)
+    gate_parts.finish()
+    wg.start()
+    gb_all.start()
+
+    own_table.wait()
+    table_all.finish()
+    own_x.wait()
+    x_all.finish()
+    gains.finish()
+    pieces = [(i, j) for i in range(n_seq) for j in range(n_batch)]
+    rows = width // (n_seq * n_batch)
+    for g in range(2):
+        gains_ref[g : g + 1, :] = jnp.concatenate(
+            [gain_all_ref[i, j, g : g + 1, :rows] for i, j in pieces], axis=1
+        )
+    gain_one = gains_ref[0:1, :]
+
+    def norm_rows(i, unused):
+        part = x_all_ref[i // 2, pl.ds(i % 2 * (length // 2), length // 2), :].astype(F32)
+        at = pl.ds(pl.multiple_of(i * (length // 2), length // 2), length // 2)
+        n1_ref[at, :] = (part * rms_scale(part) * gain_one).astype(BF16)
+        return unused
+
+    lax.fori_loop(0, 2 * n_seq, norm_rows, 0)
+    for j in range(n_seq):
+        at = slice(j * length, (j + 1) * length)
+        table = table_all_ref[j]
+        cos_part, sin_part = table[:, :HALF], table[:, HALF:HEAD_DIM]
+        tables_ref[0, at, :] = jnp.concatenate([cos_part] * 4, axis=1)
+        tables_ref[1, at, :] = jnp.concatenate([sin_part] * 4, axis=1)
+    flipped = [jnp.transpose(table_all_ref[j])[HEAD_DIM : HEAD_DIM + 1, :] for j in range(n_seq)]
+    query_seg = jnp.concatenate(flipped, axis=1)
+    for j in range(n_seq):
+        key_seg = table_all_ref[j][:, HEAD_DIM : HEAD_DIM + 1]
+        key_pos = j * length + lax.broadcasted_iota(jnp.int32, (length, total_len), 0)
+        query_pos = lax.broadcasted_iota(jnp.int32, (length, total_len), 1)
+        allowed = (key_seg == query_seg) & (key_pos <= query_pos)
+        bias_ref[j * length : (j + 1) * length, :] = jnp.where(allowed, 0.0, MASKED_SCORE).astype(
+            bias_ref.dtype
+        )
+
+    wqkv.finish()
+    weights = wqkv_ref[...].reshape(width, wqkv_ref.shape[3])
+
+    def project(i, unused):
+        at = pl.ds(pl.multiple_of(i * length, length), length)
+        qkv_proj_ref[at, :] = product(n1_ref[at, :], weights)
+        return unused
+
+    lax.fori_loop(0, n_seq, project, 0)
+    cosine, sine = tables_ref[0], tables_ref[1]
+    kv = qkv_proj_ref[:, pairs * 128 :]
+    lane = lax.broadcasted_iota(jnp.int32, kv.shape, 1)
+    rotated = kv * cosine + rotate_lanes(kv, 1.0) * sine
+    kvr_ref[...] = jnp.where(lane < HEAD_DIM, rotated, kv).astype(BF16)
+
+    def attend_pair(pair, unused):
+        at = pl.ds(pl.multiple_of(pair * 128, 128), 128)
+        q = qkv_proj_ref[:, at]
+        qr = (q * tables_ref[0] + rotate_lanes(q, 1.0) * tables_ref[1]).astype(BF16)
+        qr_ref[:, at] = qr
+        low = (qr * SCALE).astype(BF16)
+        for start in range(0, total_len, length):
+            stop = start + length
+            outs = []
+            for head in range(2):
+                queries = low[start:stop, head * HEAD_DIM : (head + 1) * HEAD_DIM]
+                scores = product_cols(kvr_ref[:stop, :HEAD_DIM], queries)
+                scores = scores + bias_ref[:stop, start:stop].astype(F32)
+                top = jnp.max(scores, axis=0, keepdims=True)
+                grown = jnp.exp(scores - top)
+                total = jnp.sum(grown, axis=0, keepdims=True)
+                probs = (grown * (1.0 / total)).astype(BF16)
+                lse_ref[pair, head : head + 1, start:stop] = top + jnp.log(total)
+                outs.append(product_rows(probs, kvr_ref[:stop, HEAD_DIM:]))
+            heads_ref[start:stop, at] = jnp.concatenate(outs, axis=1).astype(BF16)
+        return unused
+
+    lax.fori_loop(0, pairs // 2, attend_pair, 0)
+    wg.pass_on(1)
+    lax.fori_loop(pairs // 2, pairs, attend_pair, 0)
+
+    own_out.wait()
+    wo.finish()
+    out_weights = wo_ref[...].reshape(n_batch * wo_ref.shape[1], width)
+
+    def out_part(j):
+        at = pl.ds(pl.multiple_of(j * length, length), length)
+        return product(heads_ref[at, :], out_weights)
+
+    to_core = {}
+    for dy in range(ny):
+        for dc in range(1, nc):
+            j = place.seq_at(dy, dc)
+            part_ref[j] = out_part(j).astype(BF16)
+            to_core[dy, dc] = wires.push(
+                part_ref.at[j], core_in_ref.at[dc - 1, dy], (place.seq_at(0, dc), b)
+            )
+
+    def with_core(dy):
+        total = out_part(place.seq_at(dy, 0))
+        for dc in range(1, nc):
+            wires.wait(to_core[dy, dc], core_in_ref.at[dc - 1, dy])
+            total = total + core_in_ref[dc - 1, dy].astype(F32)
+        return total
+
+    to_far = {}
+    for dy in range(1, ny):
+        j = place.seq_at(dy, 0)
+        part_ref[j] = with_core(dy).astype(BF16)
+        to_far[dy] = wires.push(part_ref.at[j], far_in_ref.at[dy - 1], (j, b))
+    total = with_core(0) + x_all_ref[s].astype(F32)
+    wg.pass_on(2)
+    up_parts.finish()
+    wu.start()
+    for dy in range(1, ny):
+        wires.wait(to_far[dy], far_in_ref.at[dy - 1])
+        total = total + far_in_ref[dy - 1].astype(F32)
+    residual_ref[...] = total
+    n2_own_ref[...] = (total * rms_scale(total) * gains_ref[1:2, :]).astype(BF16)
+    own_n2 = local(n2_own_ref, n2_ref.at[s])
+    n2 = over_seq(blocks(n2_ref), n2_own_ref)
+    n2.start()
+    wg.pass_on(3)
+    for k in range(4, nz):
+        wg.pass_on(k)
+    wu.pass_on(1)
+    wd.start()
+    for k in range(1, ny):
+        n2.pass_on(k)
+        gb_all.pass_on(k)
+    for k in range(2, nz):
+        wu.pass_on(k)
+    for k in range(1, nz):
+        wd.pass_on(k)
+    n2.finish()
+    gb_all.finish()
+    wg.finish()
+    wu.finish()
+    wd.finish()
+    own_down.wait()
+    own_gb.wait()
+    own_n2.wait()
+    wires.close()
+
+
+def front(sizes, x, gb, table, gain, qkv, w_out, gate, up, down):
+    ny, nc, nz, nx = sizes
+    n_seq, n_batch = ny * nc, nz * nx
+    length, width = x.shape
+    total_len = n_seq * length
+    pairs = qkv.shape[2] // 128 - 1
+    rows = w_out.shape[0]
+    hbm = pl.BlockSpec(memory_space=pl.ANY)
+    vmem = pl.BlockSpec(memory_space=pltpu.VMEM)
+
+    def shape(dims, kind):
+        return jax.ShapeDtypeStruct(dims, kind)
+
+    results = [
+        (vmem, shape((n_seq, n_batch, rows, qkv.shape[2]), BF16)),
+        (vmem, shape((n_batch, rows, width), BF16)),
+        (hbm, shape((n_seq, n_batch, rows, gate.shape[2]), BF16)),
+        (hbm, shape((n_seq, n_batch, rows, up.shape[2]), BF16)),
+        (hbm, shape((n_batch,) + down.shape, BF16)),
+        (hbm, shape((n_seq, length, width), BF16)),
+        (vmem, shape((total_len, width), BF16)),
+        (hbm, shape((n_seq, length, width), BF16)),
+        (vmem, shape((length, width), F32)),
+        (vmem, shape((total_len, pairs * 128), BF16)),
+        (vmem, shape((total_len, pairs * 128), BF16)),
+        (vmem, shape((total_len, 128), BF16)),
+        (vmem, shape((pairs, 2, total_len), F32)),
+        (vmem, shape((2, total_len, 128), F32)),
+        (vmem, shape((2, width), F32)),
+    ]
+    seq_copies = ny - 1 + (nc - 1) * ny
+    batch_copies = nz - 1 + (nx - 1) * nz
+    wires = 4 * (n_seq - 1) + 4 * seq_copies + 6 * batch_copies + seq_copies
+    return pl.pallas_call(
+        functools.partial(front_kernel, sizes, pairs),
+        in_specs=[hbm] * 9,
+        out_specs=[spec for spec, unused in results],
+        out_shape=[kind for unused, kind in results],
+        scratch_shapes=[
+            pltpu.VMEM((n_seq, length, width), BF16),
+            pltpu.VMEM((n_seq, length, 128), F32),
+            pltpu.VMEM((n_seq, n_batch, 8, 128), F32),
+            pltpu.VMEM((total_len, qkv.shape[2]), F32),
+            pltpu.VMEM((total_len, total_len), F32 if total_len <= 1024 else BF16),
+            pltpu.VMEM((n_seq, length, width), BF16),
+            pltpu.VMEM((nc - 1, ny, length, width), BF16),
+            pltpu.VMEM((ny - 1, length, width), BF16),
+            pltpu.VMEM((length, width), BF16),
+            pltpu.SemaphoreType.DMA((wires,)),
+            pltpu.SemaphoreType.DMA((wires,)),
+            pltpu.SemaphoreType.DMA((16,)),
+        ],
+        compiler_params=pltpu.CompilerParams(
+            collective_id=0, has_side_effects=True, vmem_limit_bytes=60 * 1024 * 1024
+        ),
+        cost_estimate=pl.CostEstimate(
+            flops=2 * total_len * width * (qkv.shape[2] + rows * n_batch),
+            bytes_accessed=100 * 1024 * 1024,
+            transcendentals=pairs * total_len * total_len,
+        ),
+    )(x, gb, table, gain, qkv, w_out, gate, up, down)
+
+
 def per_device(
     tokens,
     cotangent,
@@ -343,10 +686,6 @@
     value_parts = jnp.repeat(w_value.reshape(rows, KV_HEADS, HEAD_DIM), sharers, axis=1)
     qkv_parts = jnp.concatenate([query_parts, key_parts, value_parts], axis=2).transpose(1, 0, 2)
 
-    def spread(parts):
-        mine = seq.exchange(parts)
-        return batch.gather(mine, 1).reshape(n_seq * n_batch * rows, parts.shape[2])
-
     def collect(grad):
         parts = grad.astype(BF16).reshape(n_seq, n_batch, rows, grad.shape[1])
         return seq.exchange(batch.scatter_sum(parts, 1).astype(BF16)).astype(F32)
@@ -354,37 +693,64 @@
     def by_columns(weight):
         return weight.reshape(rows, n_seq, weight.shape[1] // n_seq).transpose(1, 0, 2)
 
-    places = seq.gather(jnp.stack([segments[0], positions[0]]), 1)
-    seg_all = places[0].reshape(total_len)
-    pos_all = places[1].reshape(total_len)
-    gains = batch.gather(seq.gather(jnp.stack([gain_attn, gain_mlp]), 1), 2)
-    gain_one = gains[0].reshape(1, width).astype(F32)
-    gain_two = gains[1].reshape(1, width).astype(F32)
-    x_all = seq.gather(tokens[0], 0).reshape(total_len, width).astype(F32)
-    w_qkv = spread(qkv_parts)
-    wo = batch.gather(w_out, 0).reshape(n_batch * rows, width)
-    wg = spread(by_columns(w_gate))
-    wu = spread(by_columns(w_up))
-    wd = batch.gather(w_down, 0).reshape(n_batch * w_down.shape[0], width)
-
     grad_out_row = cotangent[0].astype(F32) * selection[0].astype(F32)[:, None]
-    grad_low = seq.gather(grad_out_row.astype(BF16), 0).reshape(total_len, width)
-
+    frequency = 10000.0 ** (-(jnp.arange(HALF, dtype=F32) * 2.0 / HEAD_DIM))
+    angles = positions[0].astype(F32)[:, None] * frequency[None, :]
+    table = jnp.concatenate(
+        [
+            jnp.cos(angles),
+            jnp.sin(angles),
+            jnp.broadcast_to(segments[0].astype(F32)[:, None], (length, 128 - HEAD_DIM)),
+        ],
+        axis=1,
+    )
+    gain_tile = jnp.pad(
+        jnp.stack([gain_attn, gain_mlp]).astype(F32), ((0, 6), (0, 128 - gain_attn.shape[0]))
+    )
+    sizes = (n_seq // 2, 2, 4, n_batch // 4)
+    (
+        w_qkv,
+        wo,
+        wg,
+        wu,
+        wd,
+        grad_low,
+        normed1,
+        normed2,
+        residual,
+        heads_out,
+        query_rot,
+        kv_rot,
+        lse,
+        rotary,
+        gains,
+    ) = front(
+        sizes,
+        tokens[0],
+        grad_out_row.astype(BF16),
+        table,
+        gain_tile,
+        qkv_parts,
+        w_out,
+        by_columns(w_gate),
+        by_columns(w_up),
+        w_down,
+    )
+    gain_one, gain_two = gains[0:1], gains[1:2]
+    w_qkv = w_qkv.reshape(width, w_qkv.shape[3])
+    wo = wo.reshape(n_batch * rows, width)
+    wg = wg.reshape(width, wg.shape[3])
+    wu = wu.reshape(width, wu.shape[3])
+    wd = wd.reshape(n_batch * w_down.shape[0], width)
+    grad_low = grad_low.reshape(total_len, width)
+    normed2 = normed2.reshape(total_len, width)
+    cosine, sine = rotary[0], rotary[1]
+    seg_all = seq.gather(segments[0], 0).reshape(total_len)
+    seg_row, seg_col = seg_all[None, :], seg_all[:, None]
     row_input = tokens[0].astype(F32)
     inv_attn = rms_scale(row_input)
-    normed1 = (x_all * rms_scale(x_all) * gain_one).astype(BF16)
-    qkv = product(normed1, w_qkv)
-    frequency = 10000.0 ** (-(jnp.arange(HALF, dtype=F32) * 2.0 / HEAD_DIM))
-    angles = pos_all.astype(F32)[:, None] * jnp.tile(frequency, 4)[None, :]
-    cosine, sine = jnp.cos(angles), jnp.sin(angles)
-    seg_row, seg_col = seg_all[None, :], seg_all[:, None]
-    heads_out, query_rot, kv_rot, lse = attend(qkv, cosine, sine, seg_row, seg_col)
-    attn_part = product(heads_out, wo).astype(BF16).reshape(n_seq, length, width)
-    residual = row_input + seq.scatter_sum(attn_part, 0)
 
     inv_mlp = rms_scale(residual)
-    normed2_own = (residual * inv_mlp * gain_two).astype(BF16)
-    normed2 = seq.gather(normed2_own, 0).reshape(total_len, width)
     gate_proj = product(normed2, wg)
     up_proj = product(normed2, wu)
     sigma = jax.nn.sigmoid(gate_proj)

time: 1110 us -> 972 us (0.88)
  waiting for transfers between devices: 599 us -> 282 us
  Pallas kernels: 38.4 us -> 302 us
  starting transfers between devices: 183 us -> 121 us
    ppermute x106 -> x41, waiting for transfers between devices: 599 us -> 282 us  [shift(): return lax.ppermute(value, self.name, pairs)]
    pallas_call x1, Pallas kernels: 15.6 us -> 279 us  [front(): pl.pallas_call(functools.partial(front_kernel, sizes, pairs), in_specs=[h...]
    ppermute x106 -> x41, starting transfers between devices: 183 us -> 121 us  [shift(): return lax.ppermute(value, self.name, pairs)]
    dynamic_update_slice x21 -> x12, local copies, waits for them, and re-layouts: 5.86 us -> 59.1 us  [exchange(): out = lax.dynamic_update_slice_in_dim(out, got, self.before(k, m), 0)]
    dynamic_update_slice x69 -> x7, local copies, waits for them, and re-layouts: 41.1 us -> 4.32 us  [gather(): lax.dynamic_update_slice_in_dim(out, jnp.expand_dims(piece, dim), self.be...]
    dynamic_slice x5 -> x0, local copies, waits for them, and re-layouts: 15 us -> none  [inner_part(): lax.dynamic_slice_in_dim(grid, i, 1, dim + 1)]
    dot_general x5 -> x3, matrix products: 40.3 us -> 29.3 us  [product(): return jnp.dot(left, right, preferred_element_type=F32)]
  transfers between devices with their start and end apart: 106 -> 41, of which waited for: 45 -> 15; matrix products, arithmetic and copies ran while one was open for 17% -> 24% of each run, Pallas kernels for 1% -> 29%
where the time goes in v2:
time: 972 us; the launch traced here: 960 us
  Pallas kernels  302 us (31%)
  waiting for transfers between devices  282 us (29%)
  starting transfers between devices  121 us (12%)
  local copies, waits for them, and re-layouts  107 us (11%)
  matrix products  104 us (11%)
  other arithmetic  41.8 us (4%)
    ppermute x41, waiting for transfers between devices, shift(): return lax.ppermute(value, self.name, pairs)  282 us
    pallas_call x1, Pallas kernels, front(): pl.pallas_call(functools.partial(front_kernel, sizes, pairs), in_specs=[h...  279 us
    ppermute x41, starting transfers between devices, shift(): return lax.ppermute(value, self.name, pairs)  121 us
    dynamic_update_slice x12, local copies, waits for them, and re-layouts, exchange(): out = lax.dynamic_update_slice_in_dim(out, got, self.before(k, m), 0)  59.1 us
    dot_general x5, matrix products, product_cols(): lax.dot_general(left, right, CONTRACT_COLS, preferred_element_type=F32)  41.5 us
    dot_general x5, matrix products, product_rows(): lax.dot_general(left, right, CONTRACT_ROWS, preferred_element_type=F32)  32.9 us
    dot_general x3, matrix products, product(): return jnp.dot(left, right, preferred_element_type=F32)  29.3 us
    pallas_call x1, Pallas kernels, attend_back(): pl.pallas_call(functools.partial(attend_back_kernel, qblock), grid=(pairs...  22.7 us
  transfers between devices with their start and end apart: 41, of which 15 were waited for; matrix products, arithmetic and copies ran while one was open for 24% of the time, Pallas kernels for 29%

profile of v2, /device:TPU:0, one launch (start us, length us, event | category | flops | bytes accessed | tf_op | source)
XLA Modules:
  0.0 959.8 jit_solution(6011083786526657218)
XLA Ops:
  6.0 2.4 fusion.20.gb_ref
  12.5 279.3 %shard_map.221 = (bf16[4,8,64,640]{3,2,1,0:T(8,128)(2,1)}, bf16[8,64,2048]{2,1,0:T(8,128)(2,1)}, bf16[4,8,64,1408]{3,2,1,0:T(8,128)(2,1)}, bf16[4,8,64,1408]{3,2...) custom-call(bf16[256,2048]{1,0:T(8,128)(2,1)} %bitcast.247, ...), custom_call_target="tpu_custom_call" | custom-call | flops 4831838208 | bytes 104857600 | tf_op jit(solution)/shard_map/pallas_call | solution.py:628
  291.9 12.0 %fusion.45 = f32[1024,1408]{1,0:T(8,128)} fusion(bf16[1024,2048]{1,0:T(8,128)(2,1)} %bitcast.291, bf16[2048,1408]{1,0:T(8,128)(2,1)} %bitcast.289), kind=kOutput, calls=%fused_computation.148 | convolution fusion | flops 5905580032 | bytes 15728640 | tf_op jit(solution)/shard_map/dot_general | solution.py:25
  303.9 8.4 fusion.46
  312.4 14.7 %multiply_convert_fusion = (bf16[1024,1408]{1,0:T(8,128)(2,1)}, bf16[1024,1408]{1,0:T(8,128)(2,1)}, bf16[1024,1408]{1,0:T(8,128)(2,1)S(1)}) fusion(f32[1024,1408]{1,0:T(8,128)} %fusion.45, f32[1024,1408]{1,0:T(8,128)} %fusion.46, bf16[1024,2048]{1,0:T(8,128)(2,1)} %bitcast.295, bf16[1408,2048]{1,0:T(8,128)(2,1)S(1)} %bitcast.286), kind=kOutput, calls=%fused_computation.10 | convolution fusion | flops 5927206912 | bytes 30146560 | tf_op jit(solution)/shard_map/dot_general | solution.py:33
  327.1 9.7 %fusion.47 = f32[1024,2048]{1,0:T(8,128)S(1)} fusion(bf16[1024,1408]{1,0:T(8,128)(2,1)} %get-tuple-element.49, bf16[2048,1408]{1,0:T(8,128)(2,1)} %bitcast.290), kind=kOutput, calls=%fused_computation.150 | convolution fusion | flops 5905580032 | bytes 17039360 | tf_op jit(solution)/shard_map/dot_general | solution.py:33
  336.9 11.0 %add_convert_fusion = bf16[1024,2048]{1,0:T(8,128)(2,1)} fusion(f32[1024,2048]{1,0:T(8,128)S(1)} %fusion.47, bf16[1024,1408]{1,0:T(8,128)(2,1)S(1)} %copy-done.41, bf16[2048,1408]{1,0:T(8,128)(2,1)} %bitcast.287), kind=kOutput, calls=%fused_computation | convolution fusion | flops 5909774336 | bytes 21233664 | tf_op jit(solution)/shard_map/dot_general | solution.py:33
  347.9 3.2 dynamic-slice_bitcast_fusion.4
  351.1 8.9 convolution_convert_fusion.4
  360.0 2.0 copy-done.9
  364.1 11.1 %convolution_convert_fusion.2 = bf16[2048,1408]{1,0:T(8,128)(2,1)} fusion(bf16[1024,2048]{1,0:T(8,128)(2,1)} %bitcast.292, bf16[1024,1408]{1,0:T(8,128)(2,1)} %get-tuple-element.49), kind=kOutput, calls=%fused_computation.3 | convolution fusion | flops 5908463616 | bytes 12845056 | tf_op jit(solution)/shard_map/dot_general | solution.py:29
  375.1 3.9 dynamic-slice_bitcast_fusion.2
  379.6 6.4 convolution_convert_fusion
  387.8 2.5 copy-done.5
  391.8 9.0 convolution_convert_fusion.1
  400.9 3.6 dynamic-slice_bitcast_fusion.1
  404.6 2.2 collective-permute-start.8
  410.7 3.2 fusion.5
  414.0 2.1 collective-permute-start.3
  416.1 2.4 fusion.6
  418.9 25.8 %collective-permute-done.23 = bf16[4,4,64,1408]{3,2,1,0:T(8,128)(2,1)} collective-permute-done((bf16[4,4,64,1408]{3,2,1,0:T(8,128)(2,1)}, bf16[4,4,64,1408]{3,2,1,0:T(8,128)(2,1)}, u32[]{:S(2)}, u32[]{:S(2)}) %collective-permute-start.23) | collective-permute-done | bytes 2883616 | tf_op jit(solution)/shard_map/ppermute | solution.py:63
  444.7 2.6 fusion.2
  448.4 30.4 %collective-permute-start.26 = (bf16[4,64,1408]{2,1,0:T(8,128)(2,1)}, bf16[4,64,1408]{2,1,0:T(8,128)(2,1)}, u32[]{:S(2)}, u32[]{:S(2)}) collective-permute-start(bf16[4,64,1408]{2,1,0:T(8,128)(2,1)} %get-tuple-element.58), channel_id=1, source_target_pairs={{0,6},{1,7},{2,0},{3,1},{4,2},{5,3},{6,4},{7,5},{8,14},{9,15},{10,... | collective-permute-start | bytes 2162696 | tf_op jit(solution)/shard_map/ppermute | solution.py:63
  478.8 27.6 %collective-permute-done.37 = bf16[4,176,2048]{2,1,0:T(8,128)(2,1)} collective-permute-done((bf16[4,176,2048]{2,1,0:T(8,128)(2,1)}, bf16[4,176,2048]{2,1,0:T(8,128)(2,1)}, u32[]{:S(2)}, u32[]{:S(2)}) %collective-permute-start.37) | collective-permute-done | bytes 2883616 | tf_op jit(solution)/shard_map/ppermute | solution.py:63
  506.5 14.1 %collective-permute-start.25 = (bf16[4,64,1408]{2,1,0:T(8,128)(2,1)S(1)}, bf16[4,64,1408]{2,1,0:T(8,128)(2,1)}, u32[]{:S(2)}, u32[]{:S(2)}) collective-permute-start(bf16[4,64,1408]{2,1,0:T(8,128)(2,1)S(1)} %get-tuple-element.59), channel_id=1, source_target_pairs={{0,4},{1,5},{2,6},{3,7},{4,0},{5,1},{6,2},{7,3},{8,12},{9,13},{10,... | collective-permute-start | bytes 2162696 | tf_op jit(solution)/shard_map/ppermute | solution.py:63
  520.6 3.0 fusion
  523.8 43.5 %collective-permute-done.30 = bf16[4,4,64,1408]{3,2,1,0:T(8,128)(2,1)} collective-permute-done((bf16[4,4,64,1408]{3,2,1,0:T(8,128)(2,1)}, bf16[4,4,64,1408]{3,2,1,0:T(8,128)(2,1)}, u32[]{:S(2)}, u32[]{:S(2)}) %collective-permute-start.30) | collective-permute-done | bytes 2883616 | tf_op jit(solution)/shard_map/ppermute | solution.py:63
  567.3 13.3 %collective-permute-start.24 = (bf16[4,64,1408]{2,1,0:T(8,128)(2,1)S(1)}, bf16[4,64,1408]{2,1,0:T(8,128)(2,1)S(1)}, u32[]{:S(2)}, u32[]{:S(2)}) collective-permute-start(bf16[4,64,1408]{2,1,0:T(8,128)(2,1)S(1)} %get-tuple-element.57), channel_id=1, source_target_pairs={{0,2},{1,3},{2,4},{3,5},{4,6},{5,7},{6,0},{7,1},{8,10},{9,11},{10,... | collective-permute-start | bytes 2162696 | tf_op jit(solution)/shard_map/ppermute | solution.py:63
  580.6 2.6 fusion.1
  583.4 17.3 %collective-permute-start.33 = (bf16[4,64,1408]{2,1,0:T(8,128)(2,1)S(1)}, bf16[4,64,1408]{2,1,0:T(8,128)(2,1)S(1)}, u32[]{:S(2)}, u32[]{:S(2)}) collective-permute-start(bf16[4,64,1408]{2,1,0:T(8,128)(2,1)S(1)} %get-tuple-element.55), channel_id=1, source_target_pairs={{0,6},{1,7},{2,0},{3,1},{4,2},{5,3},{6,4},{7,5},{8,14},{9,15},{10,... | collective-permute-start | bytes 2162696 | tf_op jit(solution)/shard_map/ppermute | solution.py:63
  601.3 2.1 multiply_reduce_fusion.1
  603.4 2.2 collective-permute-start.31
  606.1 2.7 bitcast_dynamic-update-slice_fusion.3
  610.7 4.1 collective-permute-done.24
  614.9 15.6 %collective-permute-start.39 = (bf16[176,2048]{1,0:T(8,128)(2,1)S(1)}, bf16[176,2048]{1,0:T(8,128)(2,1)S(1)}, u32[]{:S(2)}, u32[]{:S(2)}) collective-permute-start(bf16[176,2048]{1,0:T(8,128)(2,1)S(1)} %get-tuple-element.53), channel_id=1, source_target_pairs={{0,4},{1,5},{2,6},{3,7},{4,0},{5,1},{6,2},{7,3},{8,12},{9,13},{10,... | collective-permute-start | bytes 2162696 | tf_op jit(solution)/shard_map/ppermute | solution.py:63
  632.1 2.5 collective-permute-start.38
  634.7 42.1 %collective-permute-done.32 = bf16[4,64,1408]{2,1,0:T(8,128)(2,1)S(1)} collective-permute-done((bf16[4,64,1408]{2,1,0:T(8,128)(2,1)S(1)}, bf16[4,64,1408]{2,1,0:T(8,128)(2,1)S(1)}, u32[]{:S(2)}, u32[]{:S(2)}) %collective-permute-start.32) | collective-permute-done | bytes 720928 | tf_op jit(solution)/shard_map/ppermute | solution.py:63
  679.0 57.9 %collective-permute-done.39 = bf16[176,2048]{1,0:T(8,128)(2,1)S(1)} collective-permute-done((bf16[176,2048]{1,0:T(8,128)(2,1)S(1)}, bf16[176,2048]{1,0:T(8,128)(2,1)S(1)}, u32[]{:S(2)}, u32[]{:S(2)}) %collective-permute-start.39) | collective-permute-done | bytes 720928 | tf_op jit(solution)/shard_map/ppermute | solution.py:63
  739.8 4.4 collective-permute-done.28
  751.4 5.0 dynamic_update_slice.72
  756.6 5.0 dynamic_update_slice.76
  763.1 5.0 dynamic_update_slice.73
  769.3 5.0 dynamic_update_slice.74
  775.5 5.0 dynamic_update_slice.75
  782.2 7.1 dynamic_update_slice.77
  790.5 7.1 dynamic_update_slice.78
  798.9 7.1 dynamic_update_slice.79
  812.6 2.4 convolution_convert_fusion.7.do_ref
  815.0 22.7 %shard_map.222 = bf16[1024,640]{1,0:T(8,128)(2,1)S(1)} custom-call(bf16[1024,512]{1,0:T(8,128)(2,1)S(1)} %copy-done, bf16[1024,128]{1,0:T(8,128)(2,1)S(1)} %copy-done.1, bf16[1024,512]{1,0:T(8,128)(2,1)S(1)} %convolution_convert_fusion.7.do_ref, f32[4,2,1024]{2,1,0:T(2,128)S(1)} %copy-done.2, f32[1024,128]{1,0:T(8,128)S(1)} %get-tuple-element.68.cos_ref, ...), custom_call_target="tpu_custom_call" | custom-call | flops 2684354560 | bytes 6291456 | tf_op jit(solution)/shard_map/pallas_call | solution.py:204
  837.7 3.7 convolution_convert_fusion.3
  843.6 4.0 convolution_convert_fusion.5
  848.5 2.4 convolution_convert_fusion.6
  853.5 25.9 %collective-permute-done.12 = bf16[4,4,64,640]{3,2,1,0:T(8,128)(2,1)S(1)} collective-permute-done((bf16[4,4,64,640]{3,2,1,0:T(8,128)(2,1)S(1)}, bf16[4,4,64,640]{3,2,1,0:T(8,128)(2,1)S(1)}, u32[]{:S(2)}, u32[]{:S(2)}) %collective-permute-start.12) | collective-permute-done | bytes 1310752 | tf_op jit(solution)/shard_map/ppermute | solution.py:63
  880.1 1.9 collective-permute-start.13
  882.0 19.5 %collective-permute-done.19 = bf16[4,64,2048]{2,1,0:T(8,128)(2,1)S(1)} collective-permute-done((bf16[4,64,2048]{2,1,0:T(8,128)(2,1)S(1)}, bf16[4,64,2048]{2,1,0:T(8,128)(2,1)S(1)}, u32[]{:S(2)}, u32[]{:S(2)}) %collective-permute-start.19) | collective-permute-done | bytes 1048608 | tf_op jit(solution)/shard_map/ppermute | solution.py:63
  902.2 15.5 %collective-permute-done.14 = bf16[4,64,640]{2,1,0:T(8,128)(2,1)S(1)} collective-permute-done((bf16[4,64,640]{2,1,0:T(8,128)(2,1)S(1)}, bf16[4,64,640]{2,1,0:T(8,128)(2,1)S(1)}, u32[]{:S(2)}, u32[]{:S(2)}) %collective-permute-start.14) | collective-permute-done | bytes 327712 | tf_op jit(solution)/shard_map/ppermute | solution.py:63
  922.3 8.1 collective-permute-done.21
  932.0 2.6 dynamic_update_slice.68
  934.8 2.6 dynamic_update_slice.69
  938.3 3.8 dynamic_update_slice.70
  943.7 3.7 dynamic_update_slice.71
  951.1 3.3 collective-permute-done.11
  954.4 1.9 fusion.8
  956.4 3.0 fusion.30
  (252 shorter events, 72.2 us)
Async XLA Ops:
  0.7 403.9 %collective-permute-start.7 = (s32[256]{0:T(256)}, s32[256]{0:T(256)S(1)}, u32[]{:S(2)}, u32[]{:S(2)}) collective-permute-start(s32[256]{0:T(256)} %bitcast.275), channel_id=1, source_target_pairs={{0,8},{8,0},{16,24},{24,16},{1,9},{9,1},{17,25},{25,17},{2,10},{10... | collective-permute-start | bytes 3080 | tf_op jit(solution)/shard_map/ppermute | solution.py:63
  291.9 12.0 %copy-start.33 = (bf16[4,8,64,1408]{3,2,1,0:T(8,128)(2,1)S(1)}, bf16[4,8,64,1408]{3,2,1,0:T(8,128)(2,1)}, u32[]{:S(2)}) copy-start(bf16[4,8,64,1408]{3,2,1,0:T(8,128)(2,1)} %get-tuple-element.29) | copy-start | bytes 17301508
  291.9 12.0 %copy-start.34 = (bf16[4,256,2048]{2,1,0:T(8,128)(2,1)S(1)}, bf16[4,256,2048]{2,1,0:T(8,128)(2,1)}, u32[]{:S(2)}) copy-start(bf16[4,256,2048]{2,1,0:T(8,128)(2,1)} %get-tuple-element.27) | copy-start | bytes 12582916
  291.9 20.5 %slice-start.6 = ((s8[5767168]{0:T(1024)(128)(4,1)}), s8[4194304]{0:T(1024)(128)(4,1)S(1)}, s32[]{:S(2)}) async-start(s8[5767168]{0:T(1024)(128)(4,1)} %bitcast.284), calls=%async_computation.6 | async-start | bytes 8388608
  351.1 59.6 %collective-permute-start.2 = (bf16[2,256,2048]{2,1,0:T(8,128)(2,1)}, bf16[2,256,2048]{2,1,0:T(8,128)(2,1)}, u32[]{:S(2)}, u32[]{:S(2)}) collective-permute-start(bf16[2,256,2048]{2,1,0:T(8,128)(2,1)} %dynamic-slice_bitcast_fusion.4), channel_id=1, source_target_pairs={{0,8},{8,0},{16,24},{24,16},{1,9},{9,1},{17,25},{25,17},{2,10},{10... | collective-permute-start | bytes 6291464 | tf_op jit(solution)/shard_map/ppermute | solution.py:63
  363.6 52.5 %collective-permute-start = (bf16[2,256,2048]{2,1,0:T(8,128)(2,1)}, bf16[2,256,2048]{2,1,0:T(8,128)(2,1)}, u32[]{:S(2)}, u32[]{:S(2)}) collective-permute-start(bf16[2,256,2048]{2,1,0:T(8,128)(2,1)} %dynamic-slice_bitcast_fusion.5), channel_id=1, source_target_pairs={{0,8},{8,0},{16,24},{24,16},{1,9},{9,1},{17,25},{25,17},{2,10},{10... | collective-permute-start | bytes 6291464 | tf_op jit(solution)/shard_map/ppermute | solution.py:63
  379.0 65.7 %collective-permute-start.23 = (bf16[4,4,64,1408]{3,2,1,0:T(8,128)(2,1)}, bf16[4,4,64,1408]{3,2,1,0:T(8,128)(2,1)}, u32[]{:S(2)}, u32[]{:S(2)}) collective-permute-start(bf16[4,4,64,1408]{3,2,1,0:T(8,128)(2,1)} %dynamic-slice_bitcast_fusion.2), channel_id=1, source_target_pairs={{0,1},{1,0},{2,3},{3,2},{4,5},{5,4},{6,7},{7,6},{8,9},{9,8},{10,11... | collective-permute-start | bytes 8650760 | tf_op jit(solution)/shard_map/ppermute | solution.py:63
  379.6 12.2 %copy-start.42 = (bf16[1024,1408]{1,0:T(8,128)(2,1)S(1)}, bf16[1024,1408]{1,0:T(8,128)(2,1)}, u32[]{:S(2)}) copy-start(bf16[1024,1408]{1,0:T(8,128)(2,1)} %get-tuple-element.48) | copy-start | bytes 8650756
  390.3 10.6 %copy-start.27 = (f32[2,2048]{1,0:T(2,128)S(1)}, f32[2,2048]{1,0:T(2,128)}, u32[]{:S(2)}) copy-start(f32[2,2048]{1,0:T(2,128)} %get-tuple-element.31) | copy-start | bytes 49156
  390.3 116.2 %collective-permute-start.37 = (bf16[4,176,2048]{2,1,0:T(8,128)(2,1)}, bf16[4,176,2048]{2,1,0:T(8,128)(2,1)}, u32[]{:S(2)}, u32[]{:S(2)}) collective-permute-start(bf16[4,176,2048]{2,1,0:T(8,128)(2,1)} %dynamic-slice_bitcast_fusion), channel_id=1, source_target_pairs={{0,1},{1,0},{2,3},{3,2},{4,5},{5,4},{6,7},{7,6},{8,9},{9,8},{10,11... | collective-permute-start | bytes 8650760 | tf_op jit(solution)/shard_map/ppermute | solution.py:63
  404.6 3.7 collective-permute-start.8
  408.3 1.1 collective-permute-start.9
  409.5 157.8 %collective-permute-start.30 = (bf16[4,4,64,1408]{3,2,1,0:T(8,128)(2,1)}, bf16[4,4,64,1408]{3,2,1,0:T(8,128)(2,1)}, u32[]{:S(2)}, u32[]{:S(2)}) collective-permute-start(bf16[4,4,64,1408]{3,2,1,0:T(8,128)(2,1)} %dynamic-slice_bitcast_fusion.1), channel_id=1, source_target_pairs={{0,1},{1,0},{2,3},{3,2},{4,5},{5,4},{6,7},{7,6},{8,9},{9,8},{10,11... | collective-permute-start | bytes 8650760 | tf_op jit(solution)/shard_map/ppermute | solution.py:63
  413.8 30.8 %slice-start.4 = ((s8[5767168]{0:T(1024)(128)(4,1)}), s8[4194304]{0:T(1024)(128)(4,1)S(1)}, s32[]{:S(2)}) async-start(s8[5767168]{0:T(1024)(128)(4,1)} %bitcast.238), calls=%async_computation.4 | async-start | bytes 8388608
  414.0 30.7 %slice-start.5 = ((s8[5767168]{0:T(1024)(128)(4,1)}), s8[1572864]{0:T(1024)(128)(4,1)S(1)}, s32[]{:S(2)}) async-start(s8[5767168]{0:T(1024)(128)(4,1)} %bitcast.238), calls=%async_computation.5 | async-start | bytes 3145728
  414.0 169.5 %collective-permute-start.3 = (bf16[256,2048]{1,0:T(8,128)(2,1)S(1)}, bf16[256,2048]{1,0:T(8,128)(2,1)S(1)}, u32[]{:S(2)}, u32[]{:S(2)}) collective-permute-start(bf16[256,2048]{1,0:T(8,128)(2,1)S(1)} %dynamic-slice_bitcast_fusion.9), channel_id=1, source_target_pairs={{0,16},{8,24},{16,0},{24,8},{1,17},{9,25},{17,1},{25,9},{2,18},{10... | collective-permute-start | bytes 3145736 | tf_op jit(solution)/shard_map/ppermute | solution.py:63
  418.4 102.1 %slice-start.2 = ((s8[5767168]{0:T(1024)(128)(4,1)}), s8[4194304]{0:T(1024)(128)(4,1)S(1)}, s32[]{:S(2)}) async-start(s8[5767168]{0:T(1024)(128)(4,1)} %bitcast.234), calls=%async_computation.2 | async-start | bytes 8388608
  418.6 102.0 %slice-start.3 = ((s8[5767168]{0:T(1024)(128)(4,1)}), s8[1572864]{0:T(1024)(128)(4,1)S(1)}, s32[]{:S(2)}) async-start(s8[5767168]{0:T(1024)(128)(4,1)} %bitcast.234), calls=%async_computation.3 | async-start | bytes 3145728
  418.6 182.1 %collective-permute-start.1 = (bf16[256,2048]{1,0:T(8,128)(2,1)S(1)}, bf16[256,2048]{1,0:T(8,128)(2,1)S(1)}, u32[]{:S(2)}, u32[]{:S(2)}) collective-permute-start(bf16[256,2048]{1,0:T(8,128)(2,1)S(1)} %dynamic-slice_bitcast_fusion.10), channel_id=1, source_target_pairs={{0,16},{8,24},{16,0},{24,8},{1,17},{9,25},{17,1},{25,9},{2,18},{10... | collective-permute-start | bytes 3145736 | tf_op jit(solution)/shard_map/ppermute | solution.py:63
  447.3 133.2 %slice-start = ((s8[5767168]{0:T(1024)(128)(4,1)}), s8[4194304]{0:T(1024)(128)(4,1)S(1)}, s32[]{:S(2)}) async-start(s8[5767168]{0:T(1024)(128)(4,1)} %bitcast.230), calls=%async_computation | async-start | bytes 8388608
  448.4 155.0 %collective-permute-start.26 = (bf16[4,64,1408]{2,1,0:T(8,128)(2,1)}, bf16[4,64,1408]{2,1,0:T(8,128)(2,1)}, u32[]{:S(2)}, u32[]{:S(2)}) collective-permute-start(bf16[4,64,1408]{2,1,0:T(8,128)(2,1)} %get-tuple-element.58), channel_id=1, source_target_pairs={{0,6},{1,7},{2,0},{3,1},{4,2},{5,3},{6,4},{7,5},{8,14},{9,15},{10,... | collective-permute-start | bytes 2162696 | tf_op jit(solution)/shard_map/ppermute | solution.py:63
  506.5 74.1 %slice-start.1 = ((s8[5767168]{0:T(1024)(128)(4,1)}), s8[1572864]{0:T(1024)(128)(4,1)S(1)}, s32[]{:S(2)}) async-start(s8[5767168]{0:T(1024)(128)(4,1)} %bitcast.230), calls=%async_computation.1 | async-start | bytes 3145728
  506.5 102.4 %collective-permute-start.25 = (bf16[4,64,1408]{2,1,0:T(8,128)(2,1)S(1)}, bf16[4,64,1408]{2,1,0:T(8,128)(2,1)}, u32[]{:S(2)}, u32[]{:S(2)}) collective-permute-start(bf16[4,64,1408]{2,1,0:T(8,128)(2,1)S(1)} %get-tuple-element.59), channel_id=1, source_target_pairs={{0,4},{1,5},{2,6},{3,7},{4,0},{5,1},{6,2},{7,3},{8,12},{9,13},{10,... | collective-permute-start | bytes 2162696 | tf_op jit(solution)/shard_map/ppermute | solution.py:63
  567.3 47.6 %collective-permute-start.24 = (bf16[4,64,1408]{2,1,0:T(8,128)(2,1)S(1)}, bf16[4,64,1408]{2,1,0:T(8,128)(2,1)S(1)}, u32[]{:S(2)}, u32[]{:S(2)}) collective-permute-start(bf16[4,64,1408]{2,1,0:T(8,128)(2,1)S(1)} %get-tuple-element.57), channel_id=1, source_target_pairs={{0,2},{1,3},{2,4},{3,5},{4,6},{5,7},{6,0},{7,1},{8,10},{9,11},{10,... | collective-permute-start | bytes 2162696 | tf_op jit(solution)/shard_map/ppermute | solution.py:63
  583.2 18.1 %copy-start.3 = (f32[256,2048]{1,0:T(8,128)S(1)}, f32[256,2048]{1,0:T(8,128)}, u32[]{:S(2)}) copy-start(f32[256,2048]{1,0:T(8,128)} %get-tuple-element.26) | copy-start | bytes 6291460
  583.4 48.7 %collective-permute-start.33 = (bf16[4,64,1408]{2,1,0:T(8,128)(2,1)S(1)}, bf16[4,64,1408]{2,1,0:T(8,128)(2,1)S(1)}, u32[]{:S(2)}, u32[]{:S(2)}) collective-permute-start(bf16[4,64,1408]{2,1,0:T(8,128)(2,1)S(1)} %get-tuple-element.55), channel_id=1, source_target_pairs={{0,6},{1,7},{2,0},{3,1},{4,2},{5,3},{6,4},{7,5},{8,14},{9,15},{10,... | collective-permute-start | bytes 2162696 | tf_op jit(solution)/shard_map/ppermute | solution.py:63
  600.7 76.0 %collective-permute-start.32 = (bf16[4,64,1408]{2,1,0:T(8,128)(2,1)S(1)}, bf16[4,64,1408]{2,1,0:T(8,128)(2,1)S(1)}, u32[]{:S(2)}, u32[]{:S(2)}) collective-permute-start(bf16[4,64,1408]{2,1,0:T(8,128)(2,1)S(1)} %get-tuple-element.56), channel_id=1, source_target_pairs={{0,4},{1,5},{2,6},{3,7},{4,0},{5,1},{6,2},{7,3},{8,12},{9,13},{10,... | collective-permute-start | bytes 2162696 | tf_op jit(solution)/shard_map/ppermute | solution.py:63
  603.4 73.3 %collective-permute-start.31 = (bf16[4,64,1408]{2,1,0:T(8,128)(2,1)S(1)}, bf16[4,64,1408]{2,1,0:T(8,128)(2,1)S(1)}, u32[]{:S(2)}, u32[]{:S(2)}) collective-permute-start(bf16[4,64,1408]{2,1,0:T(8,128)(2,1)S(1)} %get-tuple-element.54), channel_id=1, source_target_pairs={{0,2},{1,3},{2,4},{3,5},{4,6},{5,7},{6,0},{7,1},{8,10},{9,11},{10,... | collective-permute-start | bytes 2162696 | tf_op jit(solution)/shard_map/ppermute | solution.py:63
  608.8 69.7 %copy-start.11 = (bf16[4,256,2048]{2,1,0:T(8,128)(2,1)}, bf16[4,256,2048]{2,1,0:T(8,128)(2,1)S(1)}, u32[]{:S(2)}) copy-start(bf16[4,256,2048]{2,1,0:T(8,128)(2,1)S(1)} %get-tuple-element.45) | copy-start | bytes 12582916
  608.8 69.8 %collective-permute-start.40 = (bf16[176,2048]{1,0:T(8,128)(2,1)S(1)}, bf16[176,2048]{1,0:T(8,128)(2,1)S(1)}, u32[]{:S(2)}, u32[]{:S(2)}) collective-permute-start(bf16[176,2048]{1,0:T(8,128)(2,1)S(1)} %get-tuple-element.52), channel_id=1, source_target_pairs={{0,6},{1,7},{2,0},{3,1},{4,2},{5,3},{6,4},{7,5},{8,14},{9,15},{10,... | collective-permute-start | bytes 2162696 | tf_op jit(solution)/shard_map/ppermute | solution.py:63
  614.9 121.9 %collective-permute-start.39 = (bf16[176,2048]{1,0:T(8,128)(2,1)S(1)}, bf16[176,2048]{1,0:T(8,128)(2,1)S(1)}, u32[]{:S(2)}, u32[]{:S(2)}) collective-permute-start(bf16[176,2048]{1,0:T(8,128)(2,1)S(1)} %get-tuple-element.53), channel_id=1, source_target_pairs={{0,4},{1,5},{2,6},{3,7},{4,0},{5,1},{6,2},{7,3},{8,12},{9,13},{10,... | collective-permute-start | bytes 2162696 | tf_op jit(solution)/shard_map/ppermute | solution.py:63
  632.1 106.2 %collective-permute-start.38 = (bf16[176,2048]{1,0:T(8,128)(2,1)S(1)}, bf16[176,2048]{1,0:T(8,128)(2,1)S(1)}, u32[]{:S(2)}, u32[]{:S(2)}) collective-permute-start(bf16[176,2048]{1,0:T(8,128)(2,1)S(1)} %get-tuple-element.51), channel_id=1, source_target_pairs={{0,2},{1,3},{2,4},{3,5},{4,6},{5,7},{6,0},{7,1},{8,10},{9,11},{10,... | collective-permute-start | bytes 2162696 | tf_op jit(solution)/shard_map/ppermute | solution.py:63
  676.7 130.7 %collective-permute-start.4 = (bf16[256,2048]{1,0:T(8,128)(2,1)}, bf16[256,2048]{1,0:T(8,128)(2,1)}, u32[]{:S(2)}, u32[]{:S(2)}) collective-permute-start(bf16[256,2048]{1,0:T(8,128)(2,1)} %get-tuple-element.46), channel_id=1, source_target_pairs={{0,8},{8,0},{16,24},{24,16},{1,9},{9,1},{17,25},{25,17},{2,10},{10... | collective-permute-start | bytes 3145736 | tf_op jit(solution)/shard_map/ppermute | solution.py:63
  676.7 72.3 %collective-permute-start.5 = (bf16[256,2048]{1,0:T(8,128)(2,1)}, bf16[256,2048]{1,0:T(8,128)(2,1)}, u32[]{:S(2)}, u32[]{:S(2)}) collective-permute-start(bf16[256,2048]{1,0:T(8,128)(2,1)} %get-tuple-element.46), channel_id=1, source_target_pairs={{0,16},{8,24},{16,0},{24,8},{1,17},{9,25},{17,1},{25,9},{2,18},{10... | collective-permute-start | bytes 3145736 | tf_op jit(solution)/shard_map/ppermute | solution.py:63
  678.7 60.5 %collective-permute-start.27 = (bf16[1,64,1408]{2,1,0:T(8,128)(2,1)S(1)}, bf16[1,64,1408]{2,1,0:T(8,128)(2,1)S(1)}, u32[]{:S(2)}, u32[]{:S(2)}) collective-permute-start(bf16[1,64,1408]{2,1,0:T(8,128)(2,1)S(1)} %get-tuple-element.75), channel_id=1, source_target_pairs={{0,8},{8,0},{16,24},{24,16},{1,9},{9,1},{17,25},{25,17},{2,10},{10... | collective-permute-start | bytes 540680 | tf_op jit(solution)/shard_map/ppermute | solution.py:63
  736.8 7.4 collective-permute-start.28
  738.3 8.8 collective-permute-start.29
  739.1 11.7 %copy-start.22 = (bf16[1,64,1408]{2,1,0:T(8,128)(2,1)}, bf16[1,64,1408]{2,1,0:T(8,128)(2,1)S(1)}, u32[]{:S(2)}) copy-start(bf16[1,64,1408]{2,1,0:T(8,128)(2,1)S(1)} %collective-permute-done.27) | copy-start | bytes 540676
  739.1 41.7 %collective-permute-start.34 = (bf16[1,64,1408]{2,1,0:T(8,128)(2,1)}, bf16[1,64,1408]{2,1,0:T(8,128)(2,1)}, u32[]{:S(2)}, u32[]{:S(2)}) collective-permute-start(bf16[1,64,1408]{2,1,0:T(8,128)(2,1)} %get-tuple-element.71), channel_id=1, source_target_pairs={{0,8},{8,0},{16,24},{24,16},{1,9},{9,1},{17,25},{25,17},{2,10},{10... | collective-permute-start | bytes 540680 | tf_op jit(solution)/shard_map/ppermute | solution.py:63
  744.2 45.1 %collective-permute-start.35 = (bf16[1,64,1408]{2,1,0:T(8,128)(2,1)}, bf16[1,64,1408]{2,1,0:T(8,128)(2,1)}, u32[]{:S(2)}, u32[]{:S(2)}) collective-permute-start(bf16[1,64,1408]{2,1,0:T(8,128)(2,1)} %get-tuple-element.70), channel_id=1, source_target_pairs={{0,16},{8,24},{16,0},{24,8},{1,17},{9,25},{17,1},{25,9},{2,18},{10... | collective-permute-start | bytes 540680 | tf_op jit(solution)/shard_map/ppermute | solution.py:63
  747.1 50.6 %collective-permute-start.36 = (bf16[1,64,1408]{2,1,0:T(8,128)(2,1)}, bf16[1,64,1408]{2,1,0:T(8,128)(2,1)}, u32[]{:S(2)}, u32[]{:S(2)}) collective-permute-start(bf16[1,64,1408]{2,1,0:T(8,128)(2,1)} %get-tuple-element.69), channel_id=1, source_target_pairs={{0,24},{8,16},{16,8},{24,0},{1,25},{9,17},{17,9},{25,1},{2,26},{10... | collective-permute-start | bytes 540680 | tf_op jit(solution)/shard_map/ppermute | solution.py:63
  749.0 62.2 %collective-permute-start.6 = (bf16[256,2048]{1,0:T(8,128)(2,1)}, bf16[256,2048]{1,0:T(8,128)(2,1)}, u32[]{:S(2)}, u32[]{:S(2)}) collective-permute-start(bf16[256,2048]{1,0:T(8,128)(2,1)} %collective-permute-done.5), channel_id=1, source_target_pairs={{0,8},{8,0},{16,24},{24,16},{1,9},{9,1},{17,25},{25,17},{2,10},{10... | collective-permute-start | bytes 3145736 | tf_op jit(solution)/shard_map/ppermute | solution.py:63
  761.6 19.0 %copy-start.18 = (bf16[4,64,1408]{2,0,1:T(4,128)(2,1)}, bf16[4,64,1408]{2,0,1:T(4,128)(2,1)S(1)}, u32[]{:S(2)}) copy-start(bf16[4,64,1408]{2,0,1:T(4,128)(2,1)S(1)} %dynamic_update_slice.76) | copy-start | bytes 2162692
  780.8 71.7 %copy-start.6 = (f32[8,8,4,1408]{3,1,2,0:T(8,128)}, f32[8,8,4,1408]{3,1,2,0:T(8,128)S(1)}, u32[]{:S(2)}) copy-start(f32[8,8,4,1408]{3,1,2,0:T(8,128)S(1)} %copy.98) | copy-start | bytes 4325380
  807.4 45.3 %copy-start.7 = (f32[8,8,4,1408]{3,1,2,0:T(8,128)}, f32[8,8,4,1408]{3,1,2,0:T(8,128)S(1)}, u32[]{:S(2)}) copy-start(f32[8,8,4,1408]{3,1,2,0:T(8,128)S(1)} %copy.99) | copy-start | bytes 4325380
  815.0 22.7 %copy-start.37 = (bf16[4,8,64,640]{3,2,1,0:T(8,128)(2,1)S(1)}, bf16[4,8,64,640]{3,2,1,0:T(8,128)(2,1)}, u32[]{:S(2)}) copy-start(bf16[4,8,64,640]{3,2,1,0:T(8,128)(2,1)} %get-tuple-element.38) | copy-start | bytes 7864324
  841.7 76.8 %collective-permute-start.10 = (bf16[2,256,2048]{2,1,0:T(8,128)(2,1)S(1)}, bf16[2,256,2048]{2,1,0:T(8,128)(2,1)S(1)}, u32[]{:S(2)}, u32[]{:S(2)}) collective-permute-start(bf16[2,256,2048]{2,1,0:T(8,128)(2,1)S(1)} %dynamic-slice_bitcast_fusion.3), channel_id=1, source_target_pairs={{0,8},{8,0},{16,24},{24,16},{1,9},{9,1},{17,25},{25,17},{2,10},{10... | collective-permute-start | bytes 6291464 | tf_op jit(solution)/shard_map/ppermute | solution.py:63
  847.8 31.6 %collective-permute-start.12 = (bf16[4,4,64,640]{3,2,1,0:T(8,128)(2,1)S(1)}, bf16[4,4,64,640]{3,2,1,0:T(8,128)(2,1)S(1)}, u32[]{:S(2)}, u32[]{:S(2)}) collective-permute-start(bf16[4,4,64,640]{3,2,1,0:T(8,128)(2,1)S(1)} %dynamic-slice_bitcast_fusion.6), channel_id=1, source_target_pairs={{0,1},{1,0},{2,3},{3,2},{4,5},{5,4},{6,7},{7,6},{8,9},{9,8},{10,11... | collective-permute-start | bytes 3932168 | tf_op jit(solution)/shard_map/ppermute | solution.py:63
  851.0 50.6 %collective-permute-start.19 = (bf16[4,64,2048]{2,1,0:T(8,128)(2,1)S(1)}, bf16[4,64,2048]{2,1,0:T(8,128)(2,1)S(1)}, u32[]{:S(2)}, u32[]{:S(2)}) collective-permute-start(bf16[4,64,2048]{2,1,0:T(8,128)(2,1)S(1)} %dynamic-slice_bitcast_fusion.7), channel_id=1, source_target_pairs={{0,1},{1,0},{2,3},{3,2},{4,5},{5,4},{6,7},{7,6},{8,9},{9,8},{10,11... | collective-permute-start | bytes 3145736 | tf_op jit(solution)/shard_map/ppermute | solution.py:63
  879.9 22.1 %collective-permute-start.15 = (bf16[4,64,640]{2,1,0:T(8,128)(2,1)S(1)}, bf16[4,64,640]{2,1,0:T(8,128)(2,1)S(1)}, u32[]{:S(2)}, u32[]{:S(2)}) collective-permute-start(bf16[4,64,640]{2,1,0:T(8,128)(2,1)S(1)} %get-tuple-element.62), channel_id=1, source_target_pairs={{0,6},{1,7},{2,0},{3,1},{4,2},{5,3},{6,4},{7,5},{8,14},{9,15},{10,... | collective-permute-start | bytes 983048 | tf_op jit(solution)/shard_map/ppermute | solution.py:63
  880.0 37.7 %collective-permute-start.14 = (bf16[4,64,640]{2,1,0:T(8,128)(2,1)S(1)}, bf16[4,64,640]{2,1,0:T(8,128)(2,1)S(1)}, u32[]{:S(2)}, u32[]{:S(2)}) collective-permute-start(bf16[4,64,640]{2,1,0:T(8,128)(2,1)S(1)} %get-tuple-element.63), channel_id=1, source_target_pairs={{0,4},{1,5},{2,6},{3,7},{4,0},{5,1},{6,2},{7,3},{8,12},{9,13},{10,... | collective-permute-start | bytes 983048 | tf_op jit(solution)/shard_map/ppermute | solution.py:63
  880.1 37.6 %collective-permute-start.13 = (bf16[4,64,640]{2,1,0:T(8,128)(2,1)S(1)}, bf16[4,64,640]{2,1,0:T(8,128)(2,1)S(1)}, u32[]{:S(2)}, u32[]{:S(2)}) collective-permute-start(bf16[4,64,640]{2,1,0:T(8,128)(2,1)S(1)} %get-tuple-element.61), channel_id=1, source_target_pairs={{0,2},{1,3},{2,4},{3,5},{4,6},{5,7},{6,0},{7,1},{8,10},{9,11},{10,... | collective-permute-start | bytes 983048 | tf_op jit(solution)/shard_map/ppermute | solution.py:63
  902.0 18.9 %collective-permute-start.22 = (bf16[64,2048]{1,0:T(8,128)(2,1)S(1)}, bf16[64,2048]{1,0:T(8,128)(2,1)S(1)}, u32[]{:S(2)}, u32[]{:S(2)}) collective-permute-start(bf16[64,2048]{1,0:T(8,128)(2,1)S(1)} %get-tuple-element.65), channel_id=1, source_target_pairs={{0,6},{1,7},{2,0},{3,1},{4,2},{5,3},{6,4},{7,5},{8,14},{9,15},{10,... | collective-permute-start | bytes 786440 | tf_op jit(solution)/shard_map/ppermute | solution.py:63
  902.1 28.3 %collective-permute-start.21 = (bf16[64,2048]{1,0:T(8,128)(2,1)S(1)}, bf16[64,2048]{1,0:T(8,128)(2,1)S(1)}, u32[]{:S(2)}, u32[]{:S(2)}) collective-permute-start(bf16[64,2048]{1,0:T(8,128)(2,1)S(1)} %get-tuple-element.66), channel_id=1, source_target_pairs={{0,4},{1,5},{2,6},{3,7},{4,0},{5,1},{6,2},{7,3},{8,12},{9,13},{10,... | collective-permute-start | bytes 786440 | tf_op jit(solution)/shard_map/ppermute | solution.py:63
  917.7 13.2 %collective-permute-start.20 = (bf16[64,2048]{1,0:T(8,128)(2,1)S(1)}, bf16[64,2048]{1,0:T(8,128)(2,1)S(1)}, u32[]{:S(2)}, u32[]{:S(2)}) collective-permute-start(bf16[64,2048]{1,0:T(8,128)(2,1)S(1)} %get-tuple-element.64), channel_id=1, source_target_pairs={{0,2},{1,3},{2,4},{3,5},{4,6},{5,7},{6,0},{7,1},{8,10},{9,11},{10,... | collective-permute-start | bytes 786440 | tf_op jit(solution)/shard_map/ppermute | solution.py:63
  918.5 16.2 %collective-permute-start.16 = (bf16[1,64,640]{2,1,0:T(8,128)(2,1)S(1)}, bf16[1,64,640]{2,1,0:T(8,128)(2,1)S(1)}, u32[]{:S(2)}, u32[]{:S(2)}) collective-permute-start(bf16[1,64,640]{2,1,0:T(8,128)(2,1)S(1)} %get-tuple-element.81), channel_id=1, source_target_pairs={{0,8},{8,0},{16,24},{24,16},{1,9},{9,1},{17,25},{25,17},{2,10},{10... | collective-permute-start | bytes 245768 | tf_op jit(solution)/shard_map/ppermute | solution.py:63
  918.5 18.9 %collective-permute-start.17 = (bf16[1,64,640]{2,1,0:T(8,128)(2,1)S(1)}, bf16[1,64,640]{2,1,0:T(8,128)(2,1)S(1)}, u32[]{:S(2)}, u32[]{:S(2)}) collective-permute-start(bf16[1,64,640]{2,1,0:T(8,128)(2,1)S(1)} %get-tuple-element.80), channel_id=1, source_target_pairs={{0,16},{8,24},{16,0},{24,8},{1,17},{9,25},{17,1},{25,9},{2,18},{10... | collective-permute-start | bytes 245768 | tf_op jit(solution)/shard_map/ppermute | solution.py:63
  920.9 21.1 %collective-permute-start.18 = (bf16[1,64,640]{2,1,0:T(8,128)(2,1)}, bf16[1,64,640]{2,1,0:T(8,128)(2,1)}, u32[]{:S(2)}, u32[]{:S(2)}) collective-permute-start(bf16[1,64,640]{2,1,0:T(8,128)(2,1)} %get-tuple-element.79), channel_id=1, source_target_pairs={{0,24},{8,16},{16,8},{24,0},{1,25},{9,17},{17,9},{25,1},{2,26},{10... | collective-permute-start | bytes 245768 | tf_op jit(solution)/shard_map/ppermute | solution.py:63
  930.3 24.1 %collective-permute-start.11 = (bf16[256,2048]{1,0:T(8,128)(2,1)}, bf16[256,2048]{1,0:T(8,128)(2,1)}, u32[]{:S(2)}, u32[]{:S(2)}) collective-permute-start(bf16[256,2048]{1,0:T(8,128)(2,1)} %dynamic-slice_bitcast_fusion.8), channel_id=1, source_target_pairs={{0,16},{8,24},{16,0},{24,8},{1,17},{9,25},{17,1},{25,9},{2,18},{10... | collective-permute-start | bytes 3145736 | tf_op jit(solution)/shard_map/ppermute | solution.py:63
  934.7 14.3 %copy-start.25 = (bf16[64,256]{1,0:T(8,128)(2,1)S(1)}, bf16[64,256]{1,0:T(8,128)(2,1)}, u32[]{:S(2)}) copy-start(bf16[64,256]{1,0:T(8,128)(2,1)} %param.22) | copy-start | bytes 98308
  934.7 14.4 %copy-start.26 = (bf16[64,256]{1,0:T(8,128)(2,1)S(1)}, bf16[64,256]{1,0:T(8,128)(2,1)}, u32[]{:S(2)}) copy-start(bf16[64,256]{1,0:T(8,128)(2,1)} %param.21) | copy-start | bytes 98308
  938.3 12.3 %copy-start.30 = (bf16[64]{0:T(256)(128)(2,1)S(1)}, bf16[64]{0:T(256)(128)(2,1)}, u32[]{:S(2)}) copy-start(bf16[64]{0:T(256)(128)(2,1)} %param.19) | copy-start | bytes 388
  938.3 16.2 %copy-start.8 = (bf16[1,256,2048]{2,1,0:T(8,128)(2,1)S(1)}, bf16[1,256,2048]{2,1,0:T(8,128)(2,1)}, u32[]{:S(2)}) copy-start(bf16[1,256,2048]{2,1,0:T(8,128)(2,1)} %param.14) | copy-start | bytes 3145732
  948.8 10.6 %copy-start.20 = (f32[64,256]{1,0:T(8,128)}, f32[64,256]{1,0:T(8,128)S(1)}, u32[]{:S(2)}) copy-start(f32[64,256]{1,0:T(8,128)S(1)} %reshape.187) | copy-start | bytes 196612
  (28 other events, 148.7 us)

commit v3 on v1

--- a/solution.py
+++ b/solution.py
@@ -312,7 +312,1181 @@
     )(qr, kvr, grads, lse, cosine, sine, seg_row, seg_col)
 
 
-def per_device(
+MESH = pl.DeviceIdType.MESH
+HBM = pl.BlockSpec(memory_space=pl.ANY)
+VMEM = pl.BlockSpec(memory_space=pltpu.VMEM)
+VMEM_BYTES = 62 * 1024 * 1024
+STEP = 16
+
+
+class Place:
+    def __init__(self, sizes):
+        self.ny, self.nc, self.nz, self.nx = sizes
+        self.s = lax.axis_index("seq")
+        self.b = lax.axis_index("batch")
+        self.y, self.c = self.s // self.nc, self.s % self.nc
+        self.z, self.x = self.b // self.nx, self.b % self.nx
+
+    def seq_at(self, dy, dc):
+        return (self.y + dy + self.ny) % self.ny * self.nc + (self.c + dc + self.nc) % self.nc
+
+    def z_at(self, dz):
+        return (self.z + dz + self.nz) % self.nz
+
+    def batch_at(self, dz, dx):
+        return self.z_at(dz) * self.nx + (self.x + dx + self.nx) % self.nx
+
+    def enter(self):
+        peers = [
+            (self.seq_at(dy, dc), self.b)
+            for dy in range(self.ny)
+            for dc in range(self.nc)
+            if (dy, dc) != (0, 0)
+        ]
+        peers += [(self.s, self.batch_at(k, 0)) for k in range(1, self.nz)]
+        peers += [(self.s, self.batch_at(0, m)) for m in range(1, self.nx)]
+        barrier = pltpu.get_barrier_semaphore()
+        for peer in peers:
+            pl.semaphore_signal(barrier, inc=1, device_id=peer, device_id_type=MESH)
+        pl.semaphore_wait(barrier, len(peers))
+
+
+class Wires:
+    def __init__(self, send_sems, recv_sems):
+        self.send_sems, self.recv_sems = send_sems, recv_sems
+        self.ends = []
+        self.open = []
+
+    def describe(self, index, source, target):
+        return pltpu.make_async_remote_copy(
+            src_ref=source,
+            dst_ref=target,
+            send_sem=self.send_sems.at[index],
+            recv_sem=self.recv_sems.at[index],
+            device_id=self.ends[index][2](),
+            device_id_type=MESH,
+        )
+
+    def push(self, source, target, device):
+        index = len(self.ends)
+        self.ends.append((source, target, device))
+        self.open.append(index)
+        self.describe(index, source(), target()).start()
+        return index
+
+    def wait(self, index, landed):
+        self.describe(index, landed, landed).wait_recv()
+
+    def sent(self, index):
+        self.open.remove(index)
+        source, target, unused = self.ends[index]
+        self.describe(index, source(), target()).wait_send()
+
+    def close(self):
+        for index in list(self.open):
+            self.sent(index)
+
+
+class Copies:
+    def __init__(self, sems):
+        self.sems = sems
+        self.count = 0
+
+    def start(self, source, target):
+        copy = pltpu.make_async_copy(source, target, self.sems.at[self.count])
+        self.count += 1
+        copy.start()
+        return copy
+
+
+class Gather:
+    def __init__(self, wires, slot, own, outer, inner, at, device):
+        self.wires, self.slot, self.own = wires, slot, own
+        self.outer, self.inner, self.at, self.device = outer, inner, at, device
+        self.first, self.second = {}, {}
+
+    def push(self, source, target, k, m):
+        return self.wires.push(source, target, lambda: self.device(self.at(k, m)))
+
+    def start(self):
+        mine = lambda: self.slot(self.at(0, 0))
+        for k in range(1, self.outer):
+            self.first[k] = self.push(self.own, mine, k, 0)
+        for m in range(1, self.inner):
+            self.second[0, m] = self.push(self.own, mine, 0, m)
+
+    def pass_on(self, k):
+        came = lambda: self.slot(self.at(-k, 0))
+        self.wires.wait(self.first[k], came())
+        for m in range(1, self.inner):
+            self.second[k, m] = self.push(came, came, 0, m)
+
+    def finish(self):
+        for (k, m), ticket in self.second.items():
+            self.wires.wait(ticket, self.slot(self.at(-k, -m)))
+
+
+class RowSum:
+    def __init__(self, wires, place, part_ref, core_in, far_in):
+        self.wires, self.place = wires, place
+        self.part_ref, self.core_in, self.far_in = part_ref, core_in, far_in
+        self.tickets = {}
+
+    def slot(self, t):
+        return self.place.seq_at((t + 1) % 2, (3 - t) // 2)
+
+    def push(self, t, source, target, dy, dc):
+        self.tickets[t] = self.wires.push(
+            lambda: self.part_ref.at[source],
+            lambda: target(),
+            lambda: (self.place.seq_at(dy, dc), self.place.b),
+        )
+
+    def compute(self, part):
+        def body(t, unused):
+            self.part_ref[t] = part(self.slot(t)).astype(BF16)
+
+            @pl.when(t == 0)
+            def _():
+                self.push(0, 0, lambda: self.core_in.at[1], 0, 1)
+
+            @pl.when(t == 1)
+            def _():
+                self.push(1, 1, lambda: self.core_in.at[0], 0, 1)
+
+            @pl.when(t == 2)
+            def _():
+                self.wires.wait(self.tickets[0], self.core_in.at[1])
+                mine = self.part_ref.at[2]
+                add_up(mine, [mine, self.core_in.at[1]])
+                self.push(2, 2, lambda: self.far_in, 1, 0)
+
+            return unused
+
+        lax.fori_loop(0, 4, body, 0)
+
+    def finish(self, target, extra=()):
+        self.wires.wait(self.tickets[1], self.core_in.at[0])
+        self.wires.wait(self.tickets[2], self.far_in)
+        add_up(target, [self.part_ref.at[3], self.core_in.at[0], self.far_in] + list(extra))
+
+    def sent(self):
+        for ticket in self.tickets.values():
+            self.wires.sent(ticket)
+
+
+class Rotating:
+    def __init__(self, copies):
+        self.sems, self.base = copies.sems, copies.count
+        copies.count += 2
+
+    def copy(self, i, source, target):
+        return pltpu.make_async_copy(source, target, self.sems.at[self.base + i % 2])
+
+
+def add_up(target, sources):
+    shape = target.shape
+    steps = shape[-2] // STEP
+
+    def body(i, unused):
+        at = pl.ds(pl.multiple_of(i % steps * STEP, STEP), STEP)
+        where = (at, slice(None)) if len(shape) == 2 else (i // steps, at, slice(None))
+        total = sources[0][where].astype(F32)
+        for source in sources[1:]:
+            total = total + source[where].astype(F32)
+        target[where] = total.astype(target.dtype)
+        return unused
+
+    lax.fori_loop(0, steps * (1 if len(shape) == 2 else shape[0]), body, 0)
+
+
+def front_kernel(
+    sizes,
+    pairs,
+    x_ref,
+    gb_ref,
+    table_ref,
+    gain_ref,
+    qkv_ref,
+    out_ref,
+    gate_ref,
+    up_ref,
+    down_ref,
+    wqkv_ref,
+    wo_ref,
+    wg_ref,
+    wu_ref,
+    wd_ref,
+    gb_all_ref,
+    n1t_ref,
+    n2t_ref,
+    residual_ref,
+    headst_ref,
+    qr_ref,
+    kvr_ref,
+    lse_ref,
+    tables_ref,
+    gains_ref,
+    bias_ref,
+    gate_proj_ref,
+    up_proj_ref,
+    grad_down_ref,
+    hidden_out_ref,
+    x_all_ref,
+    table_all_ref,
+    gain_all_ref,
+    core_in_ref,
+    far_in_ref,
+    n2_own_ref,
+    n2_ref,
+    send_sems,
+    recv_sems,
+    copy_sems,
+):
+    place = Place(sizes)
+    ny, nc, nz, nx = sizes
+    s, b = place.s, place.b
+    n_seq, n_batch = ny * nc, nz * nx
+    length, width = x_ref.shape
+    total_len = n_seq * length
+    ff = gate_ref.shape[2]
+    wires = Wires(send_sems, recv_sems)
+    copies = Copies(copy_sems)
+    row_others = [(dy, dc) for dy in range(ny) for dc in range(nc) if dy or dc]
+
+    def over_batch(slot, own):
+        return Gather(wires, slot, own, nz, nx, place.batch_at, lambda j: (s, j))
+
+    def over_seq(slot, own):
+        return Gather(wires, slot, own, ny, nc, place.seq_at, lambda j: (j, b))
+
+    def columns(ref):
+        return lambda j: ref.at[:, j]
+
+    def blocks(ref):
+        return lambda j: ref.at[j]
+
+    class Exchange:
+        def __init__(self, parts, target, many=True):
+            self.target = target
+            part = (lambda j: parts.at[j]) if many else (lambda j: parts)
+            self.copy = copies.start(part(s), target.at[s, b])
+            self.tickets = {}
+            for away in row_others:
+                self.tickets[away] = wires.push(
+                    lambda away=away: part(place.seq_at(*away)),
+                    lambda: target.at[s, b],
+                    lambda away=away: (place.seq_at(*away), b),
+                )
+
+        def finish(self):
+            self.copy.wait()
+            for (dy, dc), ticket in self.tickets.items():
+                wires.wait(ticket, self.target.at[place.seq_at(-dy, -dc), b])
+
+    place.enter()
+    qkv_parts = Exchange(qkv_ref, wqkv_ref)
+    gain_parts = Exchange(gain_ref, gain_all_ref, many=False)
+    own_table = copies.start(table_ref, table_all_ref.at[s])
+    own_x = copies.start(x_ref, x_all_ref.at[s])
+    own_out = copies.start(out_ref, wo_ref.at[b])
+    own_down = copies.start(down_ref, wd_ref.at[b])
+    own_gb = copies.start(gb_ref, gb_all_ref.at[s])
+    table_all = over_seq(blocks(table_all_ref), lambda: table_ref)
+    table_all.start()
+    x_all = over_seq(blocks(x_all_ref), lambda: x_ref)
+    x_all.start()
+    wo = over_batch(blocks(wo_ref), lambda: out_ref)
+    wo.start()
+    gate_parts = Exchange(gate_ref, wg_ref)
+    up_parts = Exchange(up_ref, wu_ref)
+    wqkv = over_batch(columns(wqkv_ref), lambda: wqkv_ref.at[:, b])
+    gains = over_batch(columns(gain_all_ref), lambda: gain_all_ref.at[:, b])
+    wg = over_batch(columns(wg_ref), lambda: wg_ref.at[:, b])
+    wu = over_batch(columns(wu_ref), lambda: wu_ref.at[:, b])
+    wd = over_batch(blocks(wd_ref), lambda: down_ref)
+    gb_all = over_seq(blocks(gb_all_ref), lambda: gb_ref)
+
+    qkv_parts.finish()
+    wqkv.start()
+    gain_parts.finish()
+    gains.start()
+    for k in range(1, ny):
+        table_all.pass_on(k)
+        x_all.pass_on(k)
+    for k in range(1, nz):
+        wo.pass_on(k)
+        gains.pass_on(k)
+    for k in range(1, nz):
+        wqkv.pass_on(k)
+    gate_parts.finish()
+    wg.start()
+    gb_all.start()
+
+    def attention(n1_ref, qkv_proj_ref, part_ref):
+        own_table.wait()
+        table_all.finish()
+        own_x.wait()
+        x_all.finish()
+        gains.finish()
+        rows = width // (n_seq * n_batch)
+        for g in range(2):
+            gains_ref[g : g + 1, :] = jnp.concatenate(
+                [gain_all_ref[i, j, g : g + 1, :rows] for i in range(n_seq) for j in range(n_batch)],
+                axis=1,
+            )
+        gain_one = gains_ref[0:1, :]
+        half = length // 2
+
+        def norm_rows(i, unused):
+            part = x_all_ref[i // 2, pl.ds(i % 2 * half, half), :].astype(F32)
+            at = pl.ds(pl.multiple_of(i * half, half), half)
+            n1_ref[at, :] = (part * rms_scale(part) * gain_one).astype(BF16)
+            return unused
+
+        lax.fori_loop(0, 2 * n_seq, norm_rows, 0)
+        for j in range(n_seq):
+            at = slice(j * length, (j + 1) * length)
+            table = table_all_ref[j]
+            cos_part, sin_part = table[:, :HALF], table[:, HALF:HEAD_DIM]
+            tables_ref[0, at, :] = jnp.concatenate([cos_part] * 4, axis=1)
+            tables_ref[1, at, :] = jnp.concatenate([sin_part] * 4, axis=1)
+        flipped = [
+            jnp.transpose(table_all_ref[j])[HEAD_DIM : HEAD_DIM + 1, :] for j in range(n_seq)
+        ]
+        query_seg = jnp.concatenate(flipped, axis=1)
+        for j in range(n_seq):
+            key_seg = table_all_ref[j][:, HEAD_DIM : HEAD_DIM + 1]
+            key_pos = j * length + lax.broadcasted_iota(jnp.int32, (length, total_len), 0)
+            query_pos = lax.broadcasted_iota(jnp.int32, (length, total_len), 1)
+            allowed = (key_seg == query_seg) & (key_pos <= query_pos)
+            bias_ref[j * length : (j + 1) * length, :] = jnp.where(
+                allowed, 0.0, MASKED_SCORE
+            ).astype(BF16)
+
+        wqkv.finish()
+        weights = wqkv_ref[...].reshape(width, wqkv_ref.shape[3])
+
+        def project(i, unused):
+            at = pl.ds(pl.multiple_of(i * length, length), length)
+            qkv_proj_ref[at, :] = product(n1_ref[at, :], weights)
+            return unused
+
+        lax.fori_loop(0, n_seq, project, 0)
+        kv = qkv_proj_ref[:, pairs * 128 :]
+        lane = lax.broadcasted_iota(jnp.int32, kv.shape, 1)
+        rotated = kv * tables_ref[0] + rotate_lanes(kv, 1.0) * tables_ref[1]
+        kvr_ref[...] = jnp.where(lane < HEAD_DIM, rotated, kv).astype(BF16)
+
+        def attend_pair(pair, unused):
+            at = pl.ds(pl.multiple_of(pair * 128, 128), 128)
+            q = qkv_proj_ref[:, at]
+            qr = (q * tables_ref[0] + rotate_lanes(q, 1.0) * tables_ref[1]).astype(BF16)
+            qr_ref[:, at] = qr
+            low = (qr * SCALE).astype(BF16)
+            for start in range(0, total_len, length):
+                stop = start + length
+                outs = []
+                for head in range(2):
+                    queries = low[start:stop, head * HEAD_DIM : (head + 1) * HEAD_DIM]
+                    scores = product_cols(kvr_ref[:stop, :HEAD_DIM], queries)
+                    scores = scores + bias_ref[:stop, start:stop].astype(F32)
+                    top = jnp.max(scores, axis=0, keepdims=True)
+                    grown = jnp.exp(scores - top)
+                    total = jnp.sum(grown, axis=0, keepdims=True)
+                    probs = (grown * (1.0 / total)).astype(BF16)
+                    lse_ref[pair, head : head + 1, start:stop] = top + jnp.log(total)
+                    outs.append(product_rows(probs, kvr_ref[:stop, HEAD_DIM:]))
+                headst_ref[at, start:stop] = jnp.transpose(
+                    jnp.concatenate(outs, axis=1).astype(BF16)
+                )
+            return unused
+
+        lax.fori_loop(0, pairs, attend_pair, 0)
+        wg.pass_on(1)
+
+        own_out.wait()
+        wo.finish()
+        out_weights = wo_ref[...].reshape(n_batch * wo_ref.shape[1], width)
+
+        def out_part(j):
+            at = pl.ds(pl.multiple_of(j * length, length), length)
+            return product_rows(headst_ref[:, at], out_weights)
+
+        row_sum = RowSum(wires, place, part_ref, core_in_ref, far_in_ref)
+        row_sum.compute(out_part)
+        wg.pass_on(2)
+        up_parts.finish()
+        wu.start()
+
+        def flip_rows(i, unused):
+            at = pl.ds(pl.multiple_of(i * length, length), length)
+            n1t_ref[:, at] = jnp.transpose(n1_ref[at, :])
+            return unused
+
+        lax.fori_loop(0, n_seq, flip_rows, 0)
+        row_sum.finish(residual_ref, [x_all_ref.at[s]])
+
+        def norm_own(i, unused):
+            at = pl.ds(pl.multiple_of(i * 32, 32), 32)
+            total = residual_ref[at, :]
+            n2_own_ref[at, :] = (total * rms_scale(total) * gains_ref[1:2, :]).astype(BF16)
+            return unused
+
+        lax.fori_loop(0, length // 32, norm_own, 0)
+        row_sum.sent()
+
+    pl.run_scoped(
+        attention,
+        pltpu.VMEM((total_len, width), BF16),
+        pltpu.VMEM((total_len, wqkv_ref.shape[3]), F32),
+        pltpu.VMEM((n_seq, length, width), BF16),
+    )
+    own_n2 = copies.start(n2_own_ref, n2_ref.at[s])
+    n2 = over_seq(blocks(n2_ref), lambda: n2_own_ref)
+    n2.start()
+    wg.pass_on(3)
+    wu.pass_on(1)
+    wd.start()
+    for k in range(1, ny):
+        n2.pass_on(k)
+        gb_all.pass_on(k)
+
+    def feed_forward(weight_ref, gate_buf, up_buf, hidden_ref, gb_buf, grad_buf):
+        own_n2.wait()
+        n2.finish()
+        for j in range(n_seq):
+            n2t_ref[:, j * length : (j + 1) * length] = jnp.transpose(n2_ref[j])
+        wu.pass_on(2)
+        wg.finish()
+        copies.start(wg_ref, weight_ref).wait()
+        weights = (width, ff)
+
+        def gate_rows(j, unused):
+            at = pl.ds(pl.multiple_of(j * length, length), length)
+            gate_buf[at, :] = product(n2_ref[j], weight_ref[...].reshape(weights))
+            return unused
+
+        lax.fori_loop(0, n_seq, gate_rows, 0)
+        outs = [copies.start(gate_buf, gate_proj_ref)]
+        wu.pass_on(3)
+        own_gb.wait()
+        gb_all.finish()
+        gb_in = copies.start(gb_all_ref, gb_buf)
+        wd.pass_on(1)
+        wu.finish()
+        copies.start(wu_ref, weight_ref).wait()
+        up_out = Rotating(copies)
+
+        def up_copy(j):
+            at = pl.ds(pl.multiple_of(j * length, length), length)
+            return up_out.copy(j, up_buf.at[j % 2], up_proj_ref.at[at])
+
+        def up_rows(j, unused):
+            at = pl.ds(pl.multiple_of(j * length, length), length)
+
+            @pl.when(j >= 2)
+            def _():
+                up_copy(j - 2).wait()
+
+            up = product(n2_ref[j], weight_ref[...].reshape(weights))
+            up_buf[j % 2] = up
+            up_copy(j).start()
+            gate = gate_buf[at, :]
+            hidden_ref[at, :] = (gate * jax.nn.sigmoid(gate) * up).astype(BF16)
+            return unused
+
+        lax.fori_loop(0, n_seq, up_rows, 0)
+        outs.append(copies.start(hidden_ref, hidden_out_ref))
+        gb_in.wait()
+        wd.pass_on(2)
+        grads = gb_buf[...].reshape(total_len, width)
+        grad_out = Rotating(copies)
+
+        def grad_copy(i):
+            at = pl.ds(pl.multiple_of(i * 256, 256), 256)
+            return grad_out.copy(i, grad_buf.at[i % 2], grad_down_ref.at[at])
+
+        def grad_rows(i, unused):
+            at = pl.ds(pl.multiple_of(i * 256, 256), 256)
+
+            @pl.when(i >= 2)
+            def _():
+                grad_copy(i - 2).wait()
+
+            grad_buf[i % 2] = product_rows(hidden_ref[:, at], grads).astype(BF16)
+            grad_copy(i).start()
+            return unused
+
+        whole = ff // 256
+        lax.fori_loop(0, whole, grad_rows, 0)
+        up_copy(n_seq - 2).wait()
+        up_copy(n_seq - 1).wait()
+        grad_copy(whole - 2).wait()
+        grad_copy(whole - 1).wait()
+        rest = ff - whole * 256
+        if rest:
+            grad_buf[0, :rest] = product_rows(hidden_ref[:, whole * 256 :], grads).astype(BF16)
+            outs.append(
+                copies.start(grad_buf.at[0, :rest], grad_down_ref.at[pl.ds(whole * 256, rest)])
+            )
+        wd.pass_on(3)
+        for copy in outs:
+            copy.wait()
+
+    pl.run_scoped(
+        feed_forward,
+        pltpu.VMEM(wg_ref.shape, BF16),
+        pltpu.VMEM((total_len, ff), F32),
+        pltpu.VMEM((2, length, ff), F32),
+        pltpu.VMEM((total_len, ff), BF16),
+        pltpu.VMEM((n_seq, length, width), BF16),
+        pltpu.VMEM((2, 256, width), BF16),
+    )
+    wd.finish()
+    own_down.wait()
+    wires.close()
+
+
+def shape_of(dims, kind):
+    return jax.ShapeDtypeStruct(dims, kind)
+
+
+def front(sizes, x, gb, table, gain, qkv, w_out, gate, up, down):
+    ny, nc, nz, nx = sizes
+    n_seq, n_batch = ny * nc, nz * nx
+    length, width = x.shape
+    total_len = n_seq * length
+    pairs = qkv.shape[2] // 128 - 1
+    rows = w_out.shape[0]
+    ff = gate.shape[2]
+    results = [
+        (VMEM, shape_of((n_seq, n_batch, rows, qkv.shape[2]), BF16)),
+        (VMEM, shape_of((n_batch, rows, width), BF16)),
+        (HBM, shape_of((n_seq, n_batch, rows, ff), BF16)),
+        (HBM, shape_of((n_seq, n_batch, rows, ff), BF16)),
+        (HBM, shape_of((n_batch,) + down.shape, BF16)),
+        (HBM, shape_of((n_seq, length, width), BF16)),
+        (VMEM, shape_of((width, total_len), BF16)),
+        (VMEM, shape_of((width, total_len), BF16)),
+        (VMEM, shape_of((length, width), F32)),
+        (VMEM, shape_of((pairs * 128, total_len), BF16)),
+        (VMEM, shape_of((total_len, pairs * 128), BF16)),
+        (VMEM, shape_of((total_len, 128), BF16)),
+        (VMEM, shape_of((pairs, 2, total_len), F32)),
+        (VMEM, shape_of((2, total_len, 128), F32)),
+        (VMEM, shape_of((2, width), F32)),
+        (VMEM, shape_of((total_len, total_len), BF16)),
+        (HBM, shape_of((total_len, ff), F32)),
+        (HBM, shape_of((total_len, ff), F32)),
+        (HBM, shape_of((ff, width), BF16)),
+        (HBM, shape_of((total_len, ff), BF16)),
+    ]
+    seq_copies = ny - 1 + (nc - 1) * ny
+    batch_copies = nz - 1 + (nx - 1) * nz
+    wires = 4 * (n_seq - 1) + 5 * seq_copies + 6 * batch_copies
+    return pl.pallas_call(
+        functools.partial(front_kernel, sizes, pairs),
+        in_specs=[HBM] * 9,
+        out_specs=[spec for spec, unused in results],
+        out_shape=[kind for unused, kind in results],
+        scratch_shapes=[
+            pltpu.VMEM((n_seq, length, width), BF16),
+            pltpu.VMEM((n_seq, length, 128), F32),
+            pltpu.VMEM((n_seq, n_batch, 8, 128), F32),
+            pltpu.VMEM((ny, length, width), BF16),
+            pltpu.VMEM((length, width), BF16),
+            pltpu.VMEM((length, width), BF16),
+            pltpu.VMEM((n_seq, length, width), BF16),
+            pltpu.SemaphoreType.DMA((wires,)),
+            pltpu.SemaphoreType.DMA((wires,)),
+            pltpu.SemaphoreType.DMA((40,)),
+        ],
+        compiler_params=pltpu.CompilerParams(
+            collective_id=0, has_side_effects=True, vmem_limit_bytes=VMEM_BYTES
+        ),
+        cost_estimate=pl.CostEstimate(
+            flops=2 * total_len * width * (qkv.shape[2] + rows * n_batch + 3 * ff),
+            bytes_accessed=100 * 1024 * 1024,
+            transcendentals=pairs * total_len * total_len,
+        ),
+    )(x, gb, table, gain, qkv, w_out, gate, up, down)
+
+
+class Reduce:
+    def __init__(self, wires, place, copies, to_z, from_x, from_z, stage):
+        self.wires, self.place, self.copies = wires, place, copies
+        self.to_z, self.from_x, self.from_z, self.stage = to_z, from_x, from_z, stage
+        self.x_tickets, self.z_tickets = {}, {}
+
+    def send(self, k, chunk):
+        place = self.place
+        self.x_tickets[k] = self.wires.push(
+            lambda: chunk(place.z_at(k)),
+            lambda: self.from_x.at[place.z_at(k)],
+            lambda: (place.s, place.batch_at(0, 1)),
+        )
+
+    def add(self, k):
+        place = self.place
+        zz = place.z_at(k)
+        self.wires.wait(self.x_tickets[k], self.from_x.at[zz])
+        self.copies.start(self.from_x.at[zz], self.stage).wait()
+        add_up(self.to_z.at[zz], [self.to_z.at[zz], self.stage])
+        if k:
+            self.z_tickets[k] = self.wires.push(
+                lambda: self.to_z.at[place.z_at(k)],
+                lambda: self.from_z.at[k - 1],
+                lambda: (place.s, place.batch_at(k, 0)),
+            )
+
+    def finish(self, target=None):
+        mine = self.to_z.at[self.place.z]
+        nz = self.place.nz
+
+        def body(stages):
+            loads = []
+            for k in range(1, nz):
+                self.wires.wait(self.z_tickets[k], self.from_z.at[k - 1])
+                loads.append(self.copies.start(self.from_z.at[k - 1], stages.at[k - 1]))
+            for load in loads:
+                load.wait()
+            add_up(
+                mine if target is None else target,
+                [mine] + [stages.at[k] for k in range(nz - 1)],
+            )
+
+        pl.run_scoped(body, pltpu.VMEM((nz - 1,) + self.stage.shape, BF16))
+        return mine
+
+
+def norm_back_rows(grad_ref, input_ref, gain, base_ref, target_ref, low_ref):
+    rows = 32
+
+    def body(i, unused):
+        at = pl.ds(pl.multiple_of(i * rows, rows), rows)
+        inputs = input_ref[at, :].astype(F32)
+        back = norm_back(grad_ref[at, :], inputs, rms_scale(inputs), gain)
+        total = base_ref[at, :].astype(F32) + back
+        if target_ref is not None:
+            target_ref[at, :] = total
+        low_ref[at, :] = total.astype(BF16)
+        return unused
+
+    lax.fori_loop(0, grad_ref.shape[0] // rows, body, 0)
+
+
+def back_kernel(
+    sizes,
+    pairs,
+    gd_ref,
+    hidden_ref,
+    wd_ref,
+    wg_ref,
+    wu_ref,
+    gate_ref,
+    up_ref,
+    gb_ref,
+    n1t_ref,
+    n2t_ref,
+    headst_ref,
+    residual_ref,
+    qr_ref,
+    kvr_ref,
+    tables_ref,
+    bias_ref,
+    wqkv_ref,
+    wo_ref,
+    x_ref,
+    lse_ref,
+    gains_ref,
+    mixed_ref,
+    tokens_ref,
+    down_own,
+    out_own,
+    gate_own,
+    up_own,
+    qkv_own,
+    x_down,
+    x_gate,
+    x_up,
+    x_out,
+    x_qkv,
+    z_down,
+    z_gate,
+    z_up,
+    z_out,
+    z_qkv,
+    send_gate,
+    send_up,
+    da_all_ref,
+    s_down,
+    s_gate,
+    s_up,
+    s_out,
+    s_qkv,
+    send_out,
+    send_qkv,
+    stage_down,
+    stage_gate,
+    stage_out,
+    stage_qkv,
+    core_in_ref,
+    far_in_ref,
+    mixed_core_in,
+    mixed_far_in,
+    da_own_ref,
+    total_ref,
+    send_sems,
+    recv_sems,
+    copy_sems,
+):
+    place = Place(sizes)
+    ny, nc, nz, nx = sizes
+    s, b = place.s, place.b
+    n_seq, n_batch = ny * nc, nz * nx
+    length, width = x_ref.shape
+    total_len = n_seq * length
+    ff = wg_ref.shape[3]
+    rows = wo_ref.shape[1]
+    wires = Wires(send_sems, recv_sems)
+    copies = Copies(copy_sems)
+    down = Reduce(wires, place, copies, s_down, x_down, z_down, stage_down)
+    gate = Reduce(wires, place, copies, s_gate, x_gate, z_gate, stage_gate)
+    up = Reduce(wires, place, copies, s_up, x_up, z_up, stage_gate)
+    out = Reduce(wires, place, copies, s_out, x_out, z_out, stage_out)
+    qkv = Reduce(wires, place, copies, s_qkv, x_qkv, z_qkv, stage_qkv)
+    order = list(range(1, nz)) + [0]
+    row_others = [(dy, dc) for dy in range(ny) for dc in range(nc) if dy or dc]
+
+    place.enter()
+    own_down = []
+    for k in order:
+        down.send(k, lambda zz: gd_ref.at[zz * nx + (place.x + 1) % nx])
+    for k in order:
+        own_down.append(copies.start(gd_ref.at[place.batch_at(k, 0)], s_down.at[place.z_at(k)]))
+
+    def weight_rows(flipped_ref, grads, k, dx):
+        j = place.batch_at(k, dx)
+        pieces = []
+        for i in range(n_seq):
+            start = pl.multiple_of((i * n_batch + j) * rows, rows)
+            pieces.append(flipped_ref[pl.ds(start, rows), :])
+        value = product(jnp.concatenate(pieces, axis=0), grads)
+        return value.astype(BF16).reshape(n_seq, rows, grads.shape[1])
+
+    def feed_forward(dgate_ref, dup_ref, part_ref):
+        row_sum = RowSum(wires, place, part_ref, core_in_ref, far_in_ref)
+
+        def activations(weight1, gate_buf, up_buf, gb_buf):
+            load1 = copies.start(wd_ref, weight1)
+
+            base = copies.count
+            copies.count += 3
+
+            def load_gb(j):
+                return pltpu.make_async_copy(gb_ref.at[j], gb_buf, copy_sems.at[base])
+
+            def load_gate(j):
+                at = pl.ds(pl.multiple_of(j * length, length), length)
+                return (
+                    pltpu.make_async_copy(gate_ref.at[at], gate_buf, copy_sems.at[base + 1]),
+                    pltpu.make_async_copy(up_ref.at[at], up_buf, copy_sems.at[base + 2]),
+                )
+
+            load_gb(0).start()
+            for copy in load_gate(0):
+                copy.start()
+            load1.wait()
+
+            def rows_back(j, unused):
+                load_gb(j).wait()
+                grad_hidden = product_cols(gb_buf[...], weight1[...].reshape(ff, width))
+
+                @pl.when(j + 1 < n_seq)
+                def _():
+                    load_gb(j + 1).start()
+
+                for copy in load_gate(j):
+                    copy.wait()
+                gate_part, up_part = gate_buf[...], up_buf[...]
+                sigma = jax.nn.sigmoid(gate_part)
+                activated = gate_part * sigma
+                dgate_ref[j] = (
+                    grad_hidden * up_part * sigma * (1.0 + gate_part * (1.0 - sigma))
+                ).astype(BF16)
+                dup_ref[j] = (grad_hidden * activated).astype(BF16)
+
+                @pl.when(j + 1 < n_seq)
+                def _():
+                    for copy in load_gate(j + 1):
+                        copy.start()
+
+                return unused
+
+            lax.fori_loop(0, n_seq, rows_back, 0)
+            for copy in own_down:
+                copy.wait()
+
+        pl.run_scoped(
+            activations,
+            pltpu.VMEM(wd_ref.shape, BF16),
+            pltpu.VMEM((length, ff), F32),
+            pltpu.VMEM((length, ff), F32),
+            pltpu.VMEM((length, width), BF16),
+        )
+
+        def inputs(weight1, weight2):
+            loads = [copies.start(wg_ref, weight1), copies.start(wu_ref, weight2)]
+            down.add(1)
+            for load in loads:
+                load.wait()
+
+            def input_part(j):
+                return product_cols(
+                    dgate_ref[j], weight1[...].reshape(width, ff)
+                ) + product_cols(dup_ref[j], weight2[...].reshape(width, ff))
+
+            row_sum.compute(input_part)
+            down.add(2)
+
+        pl.run_scoped(inputs, pltpu.VMEM(wg_ref.shape, BF16), pltpu.VMEM(wg_ref.shape, BF16))
+
+        def weights(flipped, staging, residual_buf, gb_buf):
+            loads = [
+                copies.start(n2t_ref, flipped),
+                copies.start(residual_ref, residual_buf),
+                copies.start(gb_ref.at[s], gb_buf),
+            ]
+            loads[0].wait()
+
+            def rows_of(reduce, grads_ref):
+                def body(i, unused):
+                    k = (i + 1) % nz
+                    zz = place.z_at(k)
+                    grads = grads_ref[...].reshape(total_len, ff)
+                    staging[zz] = weight_rows(flipped, grads, k, 1)
+                    reduce.to_z[zz] = weight_rows(flipped, grads, k, 0)
+                    return unused
+
+                lax.fori_loop(0, nz, body, 0)
+
+            def send_off(reduce, send_ref):
+                copies.start(staging, send_ref).wait()
+                for k in order:
+                    reduce.send(k, lambda zz: send_ref.at[zz])
+
+            rows_of(gate, dgate_ref)
+            send_off(gate, send_gate)
+            for copy in loads[1:]:
+                copy.wait()
+            row_sum.finish(total_ref)
+            norm_back_rows(
+                total_ref, residual_buf, gains_ref[1:2, :], gb_buf, total_ref, da_own_ref
+            )
+            da.start()
+            down.add(3)
+            rows_of(up, dup_ref)
+            send_off(up, send_up)
+            down.add(0)
+            row_sum.sent()
+
+        pl.run_scoped(
+            weights,
+            pltpu.VMEM(n2t_ref.shape, BF16),
+            pltpu.VMEM((nz, n_seq, rows, ff), BF16),
+            pltpu.VMEM((length, width), F32),
+            pltpu.VMEM((length, width), BF16),
+        )
+
+    own_da = []
+    da = Gather(
+        wires,
+        lambda j: da_all_ref.at[j],
+        lambda: da_own_ref,
+        ny,
+        nc,
+        place.seq_at,
+        lambda j: (j, b),
+    )
+    pl.run_scoped(
+        feed_forward,
+        pltpu.VMEM((n_seq, length, ff), BF16),
+        pltpu.VMEM((n_seq, length, ff), BF16),
+        pltpu.VMEM((n_seq, length, width), BF16),
+    )
+    own_da.append(copies.start(da_own_ref, da_all_ref.at[s]))
+    for k in range(1, ny):
+        da.pass_on(k)
+
+    def attention(
+        da_buf,
+        wo_buf,
+        wqkv_buf,
+        qr_buf,
+        headst_buf,
+        do_buf,
+        kvr_buf,
+        tables_buf,
+        bias_buf,
+        dqkv_buf,
+        n1t_buf,
+        dq_buf,
+        dk_buf,
+        dv_buf,
+        part_ref,
+        x_buf,
+    ):
+        loads = [
+            copies.start(source, target)
+            for source, target in [
+                (wo_ref, wo_buf),
+                (headst_ref, headst_buf),
+                (qr_ref, qr_buf),
+                (kvr_ref, kvr_buf),
+                (tables_ref, tables_buf),
+                (bias_ref, bias_buf),
+                (n1t_ref, n1t_buf),
+                (wqkv_ref, wqkv_buf),
+                (x_ref, x_buf),
+            ]
+        ]
+        gate.add(1)
+        da.finish()
+        own_da[0].wait()
+        copies.start(da_all_ref, da_buf).wait()
+        for load in loads:
+            load.wait()
+        out_weights = wo_buf[...].reshape(n_batch * rows, width)
+
+        def heads_back(j, unused):
+            at = pl.ds(pl.multiple_of(j * length, length), length)
+            do_buf[at, :] = product_cols(da_buf[j], out_weights).astype(BF16)
+            return unused
+
+        lax.fori_loop(0, n_seq, heads_back, 0)
+        branch = da_buf[...].reshape(total_len, width)
+
+        def out_rows(dx):
+            pieces = []
+            for zz in range(nz):
+                start = pl.multiple_of((zz * nx + (place.x + dx) % nx) * rows, rows)
+                pieces.append(headst_buf[pl.ds(start, rows), :])
+            value = product(jnp.concatenate(pieces, axis=0), branch)
+            return value.astype(BF16).reshape(nz, rows, width)
+
+        send_out[...] = out_rows(1)
+        for k in order:
+            out.send(k, lambda zz: send_out.at[zz])
+        s_out[...] = out_rows(0)
+        dk_buf[...] = jnp.zeros_like(dk_buf)
+        dv_buf[...] = jnp.zeros_like(dv_buf)
+
+        def pair_back(pair, unused):
+            at = pl.ds(pl.multiple_of(pair * 128, 128), 128)
+            low = (qr_buf[:, at] * SCALE).astype(BF16)
+            grads_pair = do_buf[:, at]
+            for start in range(0, total_len, length):
+                stop = start + length
+                outs = []
+                for head in range(2):
+                    lanes = slice(head * HEAD_DIM, (head + 1) * HEAD_DIM)
+                    queries = low[start:stop, lanes]
+                    grads = grads_pair[start:stop, lanes]
+                    keys = kvr_buf[:stop, :HEAD_DIM]
+                    values = kvr_buf[:stop, HEAD_DIM:]
+                    scores = product_cols(keys, queries)
+                    scores = scores + bias_buf[:stop, start:stop].astype(F32)
+                    probs = jnp.exp(scores - lse_ref[pair, head : head + 1, start:stop])
+                    dprobs = product_cols(values, grads)
+                    delta = jnp.sum(probs * dprobs, axis=0, keepdims=True)
+                    dscores = (probs * (dprobs - delta)).astype(BF16)
+                    dv_buf[:stop, :] += product(probs.astype(BF16), grads)
+                    dk_buf[:stop, :] += product(dscores, queries)
+                    outs.append(product_rows(dscores, keys) * SCALE)
+                dq_buf[start:stop, :] = jnp.concatenate(outs, axis=1)
+            dq = dq_buf[...]
+            turned = rotate_lanes(dq * tables_buf[1], -1.0)
+            dqkv_buf[:, at] = (dq * tables_buf[0] + turned).astype(BF16)
+            return unused
+
+        gate.add(2)
+        lax.fori_loop(0, pairs, pair_back, 0)
+        gate.add(3)
+        gate.add(0)
+        grads = jnp.concatenate([dk_buf[...], dv_buf[...]], axis=1)
+        back = grads * tables_buf[0] + rotate_lanes(grads * tables_buf[1], -1.0)
+        lane = lax.broadcasted_iota(jnp.int32, grads.shape, 1)
+        dqkv_buf[:, pairs * 128 :] = jnp.where(lane < HEAD_DIM, back, grads).astype(BF16)
+
+        row_sum = RowSum(wires, place, part_ref, core_in_ref, far_in_ref)
+        in_weights = wqkv_buf[...].reshape(width, wqkv_ref.shape[3])
+
+        def input_part(j):
+            at = pl.ds(pl.multiple_of(j * length, length), length)
+            return product_cols(dqkv_buf[at, :], in_weights)
+
+        row_sum.compute(input_part)
+
+        def qkv_rows(zz, unused):
+            k = (zz - place.z + nz) % nz
+            send_qkv[zz] = weight_rows(n1t_buf, dqkv_buf[...], k, 1)
+            s_qkv[zz] = weight_rows(n1t_buf, dqkv_buf[...], k, 0)
+            return unused
+
+        lax.fori_loop(0, nz, qkv_rows, 0)
+        for k in order:
+            qkv.send(k, lambda zz: send_qkv.at[zz])
+        up.add(1)
+
+        def last(grad_ref):
+            row_sum.finish(grad_ref)
+            norm_back_rows(grad_ref, x_buf, gains_ref[0:1, :], total_ref, None, tokens_ref)
+
+        pl.run_scoped(last, pltpu.VMEM((length, width), F32))
+        row_sum.sent()
+
+    pl.run_scoped(
+        attention,
+        pltpu.VMEM((n_seq, length, width), BF16),
+        pltpu.VMEM(wo_ref.shape, BF16),
+        pltpu.VMEM(wqkv_ref.shape, BF16),
+        pltpu.VMEM(qr_ref.shape, BF16),
+        pltpu.VMEM(headst_ref.shape, BF16),
+        pltpu.VMEM(qr_ref.shape, BF16),
+        pltpu.VMEM(kvr_ref.shape, BF16),
+        pltpu.VMEM(tables_ref.shape, F32),
+        pltpu.VMEM(bias_ref.shape, BF16),
+        pltpu.VMEM((total_len, (pairs + 1) * 128), BF16),
+        pltpu.VMEM(n1t_ref.shape, BF16),
+        pltpu.VMEM((total_len, 128), F32),
+        pltpu.VMEM((total_len, HEAD_DIM), F32),
+        pltpu.VMEM((total_len, HEAD_DIM), F32),
+        pltpu.VMEM((n_seq, length, width), BF16),
+        pltpu.VMEM((length, width), BF16),
+    )
+
+    def layer_out(weight_buf, hidden_buf, part_ref, mixed_total):
+        loads = [
+            copies.start(wd_ref, weight_buf),
+            copies.start(hidden_ref, hidden_buf),
+            copies.start(residual_ref, mixed_total),
+        ]
+        up.add(2)
+        for load in loads:
+            load.wait()
+
+        def mixed_part(j):
+            at = pl.ds(pl.multiple_of(j * length, length), length)
+            return product(hidden_buf[at, :], weight_buf[...].reshape(ff, width))
+
+        row_sum = RowSum(wires, place, part_ref, mixed_core_in, mixed_far_in)
+        row_sum.compute(mixed_part)
+        up.add(3)
+        down.finish(down_own)
+        row_sum.finish(mixed_ref, [mixed_total])
+        row_sum.sent()
+
+    pl.run_scoped(
+        layer_out,
+        pltpu.VMEM(wd_ref.shape, BF16),
+        pltpu.VMEM(hidden_ref.shape, BF16),
+        pltpu.VMEM((n_seq, length, width), BF16),
+        pltpu.VMEM((length, width), F32),
+    )
+
+    exchanges = []
+
+    def exchange(reduce, target):
+        mine = reduce.finish()
+        copy = copies.start(mine.at[s], target.at[s])
+        tickets = {}
+        for away in row_others:
+            tickets[away] = wires.push(
+                lambda away=away: mine.at[place.seq_at(*away)],
+                lambda: target.at[s],
+                lambda away=away: (place.seq_at(*away), b),
+            )
+        exchanges.append((copy, target, tickets))
+
+    exchange(gate, gate_own)
+    up.add(0)
+    for k in order:
+        out.add(k)
+    exchange(up, up_own)
+    for k in order:
+        qkv.add(k)
+    out.finish(out_own)
+    exchange(qkv, qkv_own)
+    for copy, target, tickets in exchanges:
+        copy.wait()
+        for (dy, dc), ticket in tickets.items():
+            wires.wait(ticket, target.at[place.seq_at(-dy, -dc)])
+    wires.close()
+
+
+def back(sizes, gd, hidden, wd, wg, wu, gate, up, gb, n1t, n2t, headst, residual, qr, kvr, tables, bias, wqkv, wo, x, lse, gains):
+    ny, nc, nz, nx = sizes
+    n_seq, n_batch = ny * nc, nz * nx
+    length, width = x.shape
+    ff = wg.shape[3]
+    rows = wo.shape[1]
+    pairs = qr.shape[1] // 128
+    chunk_down = gd.shape[1:]
+    chunk_gate = (n_seq, rows, ff)
+    chunk_out = (rows, width)
+    chunk_qkv = (n_seq, rows, wqkv.shape[3])
+    chunks = [chunk_down, chunk_gate, chunk_gate, chunk_out, chunk_qkv]
+    results = [
+        (VMEM, shape_of((length, width), BF16)),
+        (VMEM, shape_of((length, width), BF16)),
+        (VMEM, shape_of(chunk_down, F32)),
+        (VMEM, shape_of(chunk_out, F32)),
+        (HBM, shape_of(chunk_gate, BF16)),
+        (HBM, shape_of(chunk_gate, BF16)),
+        (HBM, shape_of(chunk_qkv, BF16)),
+    ]
+    results += [(HBM, shape_of((nz,) + chunk, BF16)) for chunk in chunks]
+    results += [(HBM, shape_of((nz - 1,) + chunk, BF16)) for chunk in chunks]
+    results += [(HBM, shape_of((nz,) + chunk_gate, BF16))] * 2
+    results += [(HBM, shape_of((n_seq, length, width), BF16))]
+    wires = 5 * (2 * nz - 1) + 3 * 3 + 3 + 3 * (n_seq - 1)
+    row = pltpu.VMEM((length, width), BF16)
+    return pl.pallas_call(
+        functools.partial(back_kernel, sizes, pairs),
+        in_specs=[HBM] * 19 + [VMEM] * 2,
+        out_specs=[spec for spec, unused in results],
+        out_shape=[kind for unused, kind in results],
+        scratch_shapes=[pltpu.VMEM((nz,) + chunk, BF16) for chunk in chunks]
+        + [
+            pltpu.VMEM((nz,) + chunk_out, BF16),
+            pltpu.VMEM((nz,) + chunk_qkv, BF16),
+            pltpu.VMEM(chunk_down, BF16),
+            pltpu.VMEM(chunk_gate, BF16),
+            pltpu.VMEM(chunk_out, BF16),
+            pltpu.VMEM(chunk_qkv, BF16),
+            pltpu.VMEM((ny, length, width), BF16),
+            row,
+            pltpu.VMEM((ny, length, width), BF16),
+            row,
+            row,
+            pltpu.VMEM((length, width), F32),
+            pltpu.SemaphoreType.DMA((wires,)),
+            pltpu.SemaphoreType.DMA((wires,)),
+            pltpu.SemaphoreType.DMA((100,)),
+        ],
+        compiler_params=pltpu.CompilerParams(
+            collective_id=1, has_side_effects=True, vmem_limit_bytes=VMEM_BYTES
+        ),
+        cost_estimate=pl.CostEstimate(
+            flops=12 * n_seq * length * width * ff,
+            bytes_accessed=100 * 1024 * 1024,
+            transcendentals=pairs * (n_seq * length) ** 2,
+        ),
+    )(gd, hidden, wd, wg, wu, gate, up, gb, n1t, n2t, headst, residual, qr, kvr, tables, bias, wqkv, wo, x, lse, gains)
+
+
+def by_permutes(
     tokens,
     cotangent,
     selection,
@@ -456,6 +1630,137 @@
     )
 
 
+def by_kernels(
+    tokens,
+    cotangent,
+    selection,
+    segments,
+    positions,
+    gain_attn,
+    w_query,
+    w_key,
+    w_value,
+    w_out,
+    gain_mlp,
+    w_gate,
+    w_up,
+    w_down,
+):
+    sizes = mesh_sizes()
+    n_seq, n_batch = sizes[0] * sizes[1], sizes[2] * sizes[3]
+    length, width = tokens.shape[1], tokens.shape[2]
+    rows, ff = w_gate.shape
+    q_cols = w_query.shape[1] // n_seq
+
+    def by_columns(weight):
+        return weight.reshape(rows, n_seq, weight.shape[1] // n_seq).transpose(1, 0, 2)
+
+    qkv_parts = jnp.concatenate([by_columns(w) for w in (w_query, w_key, w_value)], axis=2)
+    grad_low = (cotangent[0].astype(F32) * selection[0].astype(F32)[:, None]).astype(BF16)
+    frequency = 10000.0 ** (-(jnp.arange(HALF, dtype=F32) * 2.0 / HEAD_DIM))
+    angles = positions[0].astype(F32)[:, None] * frequency[None, :]
+    documents = jnp.broadcast_to(segments[0].astype(F32)[:, None], (length, 128 - HEAD_DIM))
+    table = jnp.concatenate([jnp.cos(angles), jnp.sin(angles), documents], axis=1)
+    gain_tile = jnp.pad(
+        jnp.stack([gain_attn, gain_mlp]).astype(F32), ((0, 6), (0, 128 - gain_attn.shape[0]))
+    )
+    (
+        w_qkv,
+        wo,
+        wg,
+        wu,
+        wd,
+        gb_all,
+        n1t,
+        n2t,
+        residual,
+        headst,
+        query_rot,
+        kv_rot,
+        lse,
+        rotary,
+        gains,
+        bias,
+        gate_proj,
+        up_proj,
+        grad_down,
+        hidden,
+    ) = front(
+        sizes,
+        tokens[0],
+        grad_low,
+        table,
+        gain_tile,
+        qkv_parts,
+        w_out,
+        by_columns(w_gate),
+        by_columns(w_up),
+        w_down,
+    )
+    mixed, tokens_grad, down_own, out_own, gate_part, up_part, qkv_part = back(
+        sizes,
+        grad_down.reshape(n_batch, w_down.shape[0], width),
+        hidden,
+        wd,
+        wg,
+        wu,
+        gate_proj,
+        up_proj,
+        gb_all,
+        n1t,
+        n2t,
+        headst,
+        residual,
+        query_rot,
+        kv_rot,
+        rotary,
+        bias,
+        w_qkv,
+        wo,
+        tokens[0],
+        lse,
+        gains,
+    )[:7]
+
+    def by_rows(part):
+        return part.astype(F32).transpose(1, 0, 2).reshape(rows, n_seq * part.shape[2])
+
+    query_own = by_rows(qkv_part[:, :, :q_cols])
+    key_own = by_rows(qkv_part[:, :, q_cols : q_cols + HEAD_DIM])
+    value_own = by_rows(qkv_part[:, :, q_cols + HEAD_DIM :])
+    gate_own, up_own = by_rows(gate_part), by_rows(up_part)
+
+    def along(weight, grad):
+        return jnp.sum(weight.astype(F32) * grad, axis=1)
+
+    gain1_own = (
+        along(w_query, query_own) + along(w_key, key_own) + along(w_value, value_own)
+    ) / gain_attn.astype(F32)
+    gain2_own = (along(w_gate, gate_own) + along(w_up, up_own)) / gain_mlp.astype(F32)
+    return (
+        mixed[None],
+        tokens_grad[None],
+        query_own,
+        key_own,
+        value_own,
+        out_own,
+        gate_own,
+        up_own,
+        down_own,
+        gain1_own,
+        gain2_own,
+    )
+
+
+def mesh_sizes():
+    return (lax.axis_size("seq") // 2, 2, 4, lax.axis_size("batch") // 4)
+
+
+def per_device(*args):
+    fits = mesh_sizes() == (2, 2, 4, 2) and args[0].shape[1:] == (256, 2048)
+    return (by_kernels if fits else by_permutes)(*args)
+
+
 def solution(mesh):
     both = ("seq", "batch")
     tokens = P("batch", "seq", None)

time: 1110 us -> 607 us (0.55)
  waiting for transfers between devices: 599 us -> 0 us
  Pallas kernels: 38.4 us -> 578 us
  starting transfers between devices: 183 us -> 0 us
  matrix products: 111 us -> 0 us
  local copies, waits for them, and re-layouts: 113 us -> 10.2 us
  other arithmetic: 50.5 us -> 10.9 us
    ppermute x106 -> x0, waiting for transfers between devices: 599 us -> none  [shift(): return lax.ppermute(value, self.name, pairs)]
    pallas_call x2, Pallas kernels: 38.4 us -> 578 us  [the longest x1 293 us: back(): pl.pallas_call(functools.partial(back_kernel, sizes, pairs), in_specs=[HB...]
    ppermute x106 -> x0, starting transfers between devices: 183 us -> none  [shift(): return lax.ppermute(value, self.name, pairs)]
    dot_general x15 -> x0, matrix products: 111 us -> none  [the longest x5 40.3 us: product(): return jnp.dot(left, right, preferred_element_type=F32)]
    dynamic_update_slice x90 -> x0, local copies, waits for them, and re-layouts: 47 us -> none  [the longest x69 41.1 us: gather(): lax.dynamic_update_slice_in_dim(out, jnp.expand_dims(piece, dim), self.be...]
    convert_element_type x18 -> x4, other arithmetic: 25.9 us -> 3.34 us  [the longest x1 1.21 us: by_kernels(): (cotangent[0].astype(F32) * selection[0].astype(F32)[:, None]).astype(BF16)]
    dynamic_slice x9 -> x0, local copies, waits for them, and re-layouts: 15.9 us -> none  [the longest x5 15 us: inner_part(): lax.dynamic_slice_in_dim(grid, i, 1, dim + 1)]
    another operation x19 -> x0, local copies, waits for them, and re-layouts: 13 us -> none
  transfers between devices with their start and end apart: 106 -> 0, of which waited for: 45 -> 0; matrix products, arithmetic and copies ran while one was open for 17% -> 0% of each run, Pallas kernels for 1% -> 0%
where the time goes in v3:
time: 607 us; the launch traced here: 600 us
  Pallas kernels  578 us (95%)
  other arithmetic  10.9 us (2%)
  local copies, waits for them, and re-layouts  10.2 us (2%)
    pallas_call x1, Pallas kernels, back(): pl.pallas_call(functools.partial(back_kernel, sizes, pairs), in_specs=[HB...  293 us
    pallas_call x1, Pallas kernels, front(): pl.pallas_call(functools.partial(front_kernel, sizes, pairs), in_specs=[H...  284 us

profile of v3, /device:TPU:0, one launch (start us, length us, event | category | flops | bytes accessed | tf_op | source)
XLA Modules:
  0.0 599.7 jit_solution(7302654605157703499)
XLA Ops:
  0.6 0.0 copy-start.8
  0.7 0.8 convert_element_type.70
  1.4 0.7 convert_element_type.75
  2.1 0.7 convert_element_type.73
  2.8 1.3 fusion.7.gain_ref
  4.1 0.9 reshape.97
  4.9 0.9 reshape.98
  5.8 0.1 broadcast_in_dim.6
  5.9 0.0 copy-start.2
  5.9 0.0 copy-start.3
  5.9 0.5 multiply_cosine_fusion
  6.5 0.8 pad_maximum_fusion.1.table_ref
  7.3 1.0 copy.57
  8.2 0.8 pad_maximum_fusion.qkv_ref
  9.1 0.0 copy-done.8
  9.1 1.2 fusion.gb_ref
  10.3 0.0 copy-done.2
  10.3 0.0 copy-done.3
  10.3 1.2 bitcast_bitcast_fusion
  11.5 284.3 %shard_map.221 = (bf16[4,8,64,640]{3,2,1,0:T(8,128)(2,1)}, bf16[8,64,2048]{2,1,0:T(8,128)(2,1)}, bf16[4,8,64,1408]{3,2,1,0:T(8,128)(2,1)}, bf16[4,8,64,1408]{3,2...) custom-call(bf16[256,2048]{1,0:T(8,128)(2,1)} %bitcast.66, ...), custom_call_target="tpu_custom_call" | custom-call | flops 22548578304 | bytes 104857600 | tf_op jit(solution)/shard_map/pallas_call | solution.py:888
  295.8 0.0 copy-start.15
  295.9 0.0 copy-start.16
  295.9 293.3 %shard_map.222 = (bf16[256,2048]{1,0:T(8,128)(2,1)}, bf16[256,2048]{1,0:T(8,128)(2,1)}, f32[176,2048]{1,0:T(8,128)}, f32[64,2048]{1,0:T(8,128)}, bf16[4,64,1408]...) custom-call(bf16[8,176,2048]{2,1,0:T(8,128)(2,1)} %bitcast.68, ...), custom_call_target="tpu_custom_call" | custom-call | flops 35433480192 | bytes 104857600 | tf_op jit(solution)/shard_map/pallas_call | solution.py:1455
  589.2 0.0 copy-start.9
  589.2 0.0 copy-start.17
  589.2 0.0 copy-start.11
  589.2 1.0 convert_bitcast_fusion.3
  590.3 0.1 copy.43
  590.4 0.1 reshape.118
  590.5 0.0 copy-done.15
  590.5 0.1 multiply_reduce_fusion.3
  590.6 0.1 copy.42
  590.7 0.1 reshape.116
  590.9 0.0 copy-done.16
  590.9 0.1 multiply_reduce_fusion.4
  591.0 1.0 convert_bitcast_fusion.2
  592.1 0.0 copy-start.4
  592.1 0.2 multiply_reduce_fusion.2
  592.2 0.0 copy-done.17
  592.2 0.5 convert_divide_fusion.1
  592.8 0.1 convert_bitcast_fusion.1
  592.9 0.0 copy-done.13
  592.9 0.0 copy-done.14
  592.9 0.0 copy-start.10
  592.9 0.1 copy.50
  593.0 0.0 copy-done.4
  593.0 0.0 copy-start
  593.0 0.2 multiply_reduce_fusion.1
  593.3 0.8 copy-done.10
  594.1 0.1 convert_bitcast_fusion
  594.2 0.0 copy-start.18
  594.2 0.0 copy-start.7
  594.3 0.1 copy.51
  594.4 0.0 copy-start.1
  594.4 0.2 multiply_reduce_fusion
  594.6 0.2 copy-done.18
  594.9 0.5 convert_divide_fusion
  595.4 0.5 copy-done.7
  595.9 1.0 copy.62
  596.9 0.0 copy-done.6
  596.9 1.0 copy.63
  597.8 0.8 copy.64
  598.6 0.0 copy-done.5
  598.6 1.1 copy.65
  (13 shorter events, 0.1 us)
Async XLA Ops:
  0.6 8.4 %copy-start.8 = (bf16[1,256,2048]{2,1,0:T(8,128)(2,1)S(1)}, bf16[1,256,2048]{2,1,0:T(8,128)(2,1)}, u32[]{:S(2)}) copy-start(bf16[1,256,2048]{2,1,0:T(8,128)(2,1)} %param.15) | copy-start | bytes 3145732
  5.9 4.4 copy-start.2
  5.9 4.3 copy-start.3
  295.8 294.7 %copy-start.15 = (bf16[64,256]{1,0:T(8,128)(2,1)S(1)}, bf16[64,256]{1,0:T(8,128)(2,1)}, u32[]{:S(2)}) copy-start(bf16[64,256]{1,0:T(8,128)(2,1)} %param.22) | copy-start | bytes 98308
  295.9 295.0 %copy-start.16 = (bf16[64,256]{1,0:T(8,128)(2,1)S(1)}, bf16[64,256]{1,0:T(8,128)(2,1)}, u32[]{:S(2)}) copy-start(bf16[64,256]{1,0:T(8,128)(2,1)} %param.21) | copy-start | bytes 98308
  589.2 2.9 copy-start.9
  589.2 3.0 copy-start.17
  589.2 3.5 copy-start.11
  590.5 2.3 copy-start.13
  590.9 2.0 copy-start.14
  592.1 1.0 copy-start.4
  592.9 1.2 copy-start.10
  593.0 1.2 copy-start
  594.2 0.7 copy-start.18
  594.2 1.6 copy-start.7
  594.4 2.5 copy-start.1
  594.4 2.5 copy-start.6
  595.9 2.0 copy-start.12
  596.9 1.8 copy-start.5
